TPU v7x, 256 devices: a whole 4x4x8 slice. The times are simulated.
256 devices in a mesh: lon: 16 (over x, y_hi, core), lat: 16 (over z, y_lo).
Axes of the slice: x: 4, y: 4 (y_hi: 2, y_lo: 2; y = y_hi * 2 + y_lo), z: 8, core: 2. Of those that a mesh axis runs over, the one named last changes fastest.
Arguments:
- field: bfloat16 [512, 512, 256], P('lat', 'lon'), may hold values from -6 to 6
- first_weight: bfloat16 [2304, 256], replicated, may hold values from -0.125 to 0.125
- second_weight: bfloat16 [2304, 256], replicated, may hold values from -0.125 to 0.125
- cotangent: bfloat16 [512, 512, 256], P('lat', 'lon'), may hold values from -6 to 6
- live_rows: int32 [16, 16], P('lon', 'lat'), may hold values from 8 to 32, as said below
- polar_links: int32 [2, 512], replicated, may hold values from 0 to 511, as said below
Outputs:
- output: bfloat16 [512, 512, 256], P('lat', 'lon')
- field_grad: bfloat16 [512, 512, 256], P('lat', 'lon')
- first_grad: float32 [2304, 256], P('lat')
- second_grad: float32 [2304, 256], P('lat')
Inputs may be any that keep to these rules, and one draw needn't show every extreme that they name: `live_rows`: equals 32 for every tile outside the first and the last row of tiles. `polar_links`: each of the two rows maps column j to (K - j) mod 512 for a whole number K of its own: the loop's columns in reversed order.
All inputs are finite; a program needn't handle non-finite values.
Results may differ from a plain program's by a relative error of at most 0.014.
Values may be sent and summed in bfloat16 or wider, within the bound.
A program may use at most 128 MiB of HBM per device.

v0:
```python
import math

import jax
import jax.numpy as jnp
from jax import lax
from jax.sharding import PartitionSpec as P


def with_halo(block, sides, width):
    for axis, dim in sides:
        count = lax.axis_size(axis)
        forward = [(i, i + 1) for i in range(count - 1)]
        forward.append((count - 1, 0))
        backward = [(target, source) for source, target in forward]
        low = lax.ppermute(
            lax.slice_in_dim(block, block.shape[dim] - width, None, axis=dim), axis, forward
        )
        high = lax.ppermute(lax.slice_in_dim(block, 0, width, axis=dim), axis, backward)
        block = jnp.concatenate([low, block, high], axis=dim)
    return block


def gelu_parts(pre):
    cdf = 0.5 * (1.0 + jax.scipy.special.erf(pre * 0.7071067811865476))
    dens = jnp.exp(-0.5 * pre * pre) * 0.3989422804014327
    return (pre * cdf, cdf + pre * dens)


def surround(field):
    return with_halo(field, (("lon", 1), ("lat", 0)), 1)


def patches(grown, tile_rows, tile_cols):
    pieces = [
        grown[row_off : row_off + tile_rows, col_off : col_off + tile_cols]
        for row_off in range(3)
        for col_off in range(3)
    ]
    return jnp.concatenate(pieces, axis=-1).reshape(tile_rows * tile_cols, -1)


def padded_field(field, edge_links, lat_pos, lat_count):
    grown = surround(field)
    edges = jnp.stack([field[0], field[-1]])
    loop_rows = lax.all_gather(edges, "lon", axis=1, tiled=True)
    north = jnp.take(loop_rows[0], edge_links[0], axis=0)
    south = jnp.take(loop_rows[1], edge_links[1], axis=0)
    top = jnp.where(lat_pos == 0, north, grown[0])
    bottom = jnp.where(lat_pos == lat_count - 1, south, grown[-1])
    return jnp.concatenate([top[None], grown[1:-1], bottom[None]], axis=0)


def spread_back(delta, weight, lat_pos, lat_count):
    tile_rows, tile_cols, channels = delta.shape
    flipped = (
        weight.reshape(9, channels, channels).transpose(0, 2, 1).reshape(9 * channels, channels)
    )
    grown = surround(delta)
    top = jnp.where(lat_pos == 0, jnp.zeros_like(grown[0]), grown[0])
    bottom = jnp.where(lat_pos == lat_count - 1, jnp.zeros_like(grown[-1]), grown[-1])
    grown = jnp.concatenate([top[None], grown[1:-1], bottom[None]], axis=0)
    pieces = [
        grown[2 - row_off : 2 - row_off + tile_rows, 2 - col_off : 2 - col_off + tile_cols]
        for row_off in range(3)
        for col_off in range(3)
    ]
    stacked = jnp.concatenate(pieces, axis=-1).reshape(tile_rows * tile_cols, 9 * channels)
    inner = jnp.dot(stacked, flipped, preferred_element_type=jnp.float32).reshape(
        tile_rows, tile_cols, channels
    )
    north_in = jnp.concatenate(
        [grown[1, 2 - col_off : 2 - col_off + tile_cols] for col_off in range(3)], axis=-1
    )
    south_in = jnp.concatenate(
        [grown[tile_rows, 2 - col_off : 2 - col_off + tile_cols] for col_off in range(3)], axis=-1
    )
    north = jnp.dot(north_in, flipped[: 3 * channels], preferred_element_type=jnp.float32)
    south = jnp.dot(south_in, flipped[6 * channels :], preferred_element_type=jnp.float32)
    north = jnp.where(lat_pos == 0, north, jnp.zeros_like(north))
    south = jnp.where(lat_pos == lat_count - 1, south, jnp.zeros_like(south))
    return (inner, jnp.stack([north, south]))


def route_rim(terms, polar_links, lon_pos):
    tile_cols = terms.shape[1]
    channels = terms.shape[2]
    loop_len = polar_links.shape[1]
    sources = lon_pos * tile_cols + jnp.arange(tile_cols, dtype=jnp.int32)
    targets = jnp.take(polar_links, sources, axis=1)
    spread = jnp.zeros((2, loop_len, channels), jnp.float32)
    spread = spread.at[0, targets[0]].add(terms[0]).at[1, targets[1]].add(terms[1])
    return lax.psum_scatter(
        spread.astype(jnp.bfloat16), "lon", scatter_dimension=1, tiled=True
    ).astype(jnp.float32)


def add_rim(inner, routed):
    return inner.at[0].add(routed[0]).at[-1].add(routed[1])


def weight_term(stacked, delta):
    flat = delta.reshape(-1, delta.shape[2])
    return lax.dot_general(
        stacked, flat, (((0,), (0,)), ((), ())), preferred_element_type=jnp.float32
    )


def local(field, first_weight, second_weight, cotangent, live_rows, polar_links):
    tile_rows, tile_cols, channels = field.shape
    lat_pos = lax.axis_index("lat")
    lon_pos = lax.axis_index("lon")
    lat_count = lax.axis_size("lat")
    loop_len = polar_links.shape[1]
    starts = lon_pos * tile_cols - 1 + jnp.arange(tile_cols + 2, dtype=jnp.int32)
    edge_links = jnp.take(polar_links, starts % loop_len, axis=1)
    keep = (jnp.arange(tile_rows, dtype=jnp.int32) < live_rows[0, 0])[:, None, None]
    keep_f = keep.astype(jnp.float32)
    masked = jnp.where(keep, field, jnp.zeros_like(field))
    grown_in = padded_field(masked, edge_links, lat_pos, lat_count)
    stacked_in = patches(grown_in, tile_rows, tile_cols)
    first_pre = jnp.dot(stacked_in, first_weight, preferred_element_type=jnp.float32).reshape(
        tile_rows, tile_cols, channels
    )
    activated, slope = gelu_parts(first_pre)
    hidden = (activated * keep_f).astype(jnp.bfloat16)
    grown_hidden = padded_field(hidden, edge_links, lat_pos, lat_count)
    stacked_hidden = patches(grown_hidden, tile_rows, tile_cols)
    second_pre = jnp.dot(stacked_hidden, second_weight, preferred_element_type=jnp.float32).reshape(
        tile_rows, tile_cols, channels
    )
    output = (masked.astype(jnp.float32) + second_pre * keep_f).astype(jnp.bfloat16)
    delta_two = jnp.where(keep, cotangent, jnp.zeros_like(cotangent))
    second_local = weight_term(stacked_hidden, delta_two)
    back_hidden, rim_hidden = spread_back(delta_two, second_weight, lat_pos, lat_count)
    back_hidden = add_rim(back_hidden, route_rim(rim_hidden, polar_links, lon_pos))
    delta_one = (back_hidden * keep_f * slope).astype(jnp.bfloat16)
    first_local = weight_term(stacked_in, delta_one)
    back_in, rim_in = spread_back(delta_one, first_weight, lat_pos, lat_count)
    back_in = add_rim(back_in, route_rim(rim_in, polar_links, lon_pos))
    field_grad = ((cotangent.astype(jnp.float32) + back_in) * keep_f).astype(jnp.bfloat16)
    scale = 1.0 / math.sqrt(tile_rows * lat_count * tile_cols * lax.axis_size("lon"))
    share = first_local.shape[0] // lat_count
    total_first, total_second = lax.psum((first_local, second_local), ("lon", "lat"))
    first_sum = lax.dynamic_slice_in_dim(total_first, lat_pos * share, share, 0)
    second_sum = lax.dynamic_slice_in_dim(total_second, lat_pos * share, share, 0)
    return (output, field_grad, first_sum * scale, second_sum * scale)


def solution(mesh):
    in_specs = (P("lat", "lon", None), P(), P(), P("lat", "lon", None), P("lon", "lat"), P())
    out_specs = (P("lat", "lon", None), P("lat", "lon", None), P("lat", None), P("lat", None))
    return jax.shard_map(local, mesh=mesh, in_specs=in_specs, out_specs=out_specs, check_vma=False)
```

profile of v0, /device:TPU:1, one launch (start us, length us, event | category | flops | bytes accessed | tf_op | source)
XLA Modules:
  0.0 571.5 jit_solution(13368240102097199788)
XLA Ops:
  8.0 1.3 broadcast_select_fusion
  10.1 4.3 collective-permute-start
  15.1 3.2 collective-permute-start.8
  18.3 1.0 collective-permute-start.9
  20.0 1.5 copy.22
  21.5 2.1 gather_fusion
  23.7 0.8 select_bitcast_fusion
  26.0 25.7 %all_gather.6 = bf16[2,512,256]{2,1,0:T(8,128)(2,1)S(1)} all-gather(bf16[2,32,256]{2,1,0:T(8,128)(2,1)S(1)} %pad_maximum_fusion.8), channel_id=1, replica_groups=mesh['lon'=16,'lat'=16] {'lon'}, dimensions={1}, use_global_device_ids=true | all-gather | bytes 557056 | tf_op jit(solution)/shard_map/all_gather | solution.py:45
  51.7 0.8 slice_bitcast_fusion.2
  52.6 0.9 fusion.75
  53.5 2.1 gather_fusion.5
  55.6 0.8 select_bitcast_fusion.1
  56.6 0.9 fusion.74
  58.1 1.6 copy.23
  59.7 1.5 copy.27
  61.2 1.2 copy.25
  62.4 1.2 copy.26
  63.6 1.9 copy.29
  65.5 0.9 copy.28
  66.4 1.6 gather_fusion.2
  68.0 1.6 gather_fusion.1
  70.3 4.9 collective-permute-start.3
  75.9 3.6 collective-permute-start.10
  79.9 2.2 scatter_fusion
  82.2 2.2 scatter_fusion.1
  84.5 0.8 convert_element_type.43
  85.6 0.8 fusion.49
  86.4 0.8 fusion.50
  89.4 0.8 broadcast_select_fusion.5
  93.0 2.4 fusion.82
  95.4 57.4 %reduce-scatter.3.cloned.1.call-done = bf16[2,32,256]{2,1,0:T(8,128)(2,1)} async-done(((bf16[2,512,256]{2,1,0:T(8,128)(2,1)}), bf16[2,32,256]{2,1,0:T(8,128)(2,1)}) %reduce-scatter.3.cloned.1.call-update) | async-done | bytes 32784 | tf_op jit(solution)/shard_map/reduce_scatter | solution.py:92
  153.6 1.4 fusion.46
  155.0 1.4 fusion.45
  156.3 4.3 fusion.10
  161.4 5.2 convolution_bitcast_fusion.1
  166.6 25.4 %all_gather.7 = bf16[2,512,256]{2,1,0:T(8,128)(2,1)S(1)} all-gather(bf16[2,32,256]{2,1,0:T(8,128)(2,1)S(1)} %pad_maximum_fusion.9), channel_id=1, replica_groups=mesh['lon'=16,'lat'=16] {'lon'}, dimensions={1}, use_global_device_ids=true | all-gather | bytes 557056 | tf_op jit(solution)/shard_map/all_gather | solution.py:45
  192.8 1.2 gather_fusion.3
  194.7 3.3 collective-permute-start.12
  198.0 1.8 collective-permute-start.13
  199.8 0.9 collective-permute-start.6
  200.7 2.8 collective-permute-start.7
  203.9 2.2 scatter_fusion.2
  206.2 1.2 convolution_select_fusion
  207.3 2.3 scatter_fusion.3
  209.6 0.8 convert_element_type.46
  210.6 2.8 collective-permute-start.14
  217.0 1.1 collective-permute-done.15
  218.6 1.0 slice_dynamic-update-slice_fusion.5
  219.6 1.1 slice_dynamic-update-slice_fusion.4
  220.7 0.9 slice_dynamic-update-slice_fusion.3
  221.6 1.2 fusion.14
  222.8 0.9 constant_dynamic-update-slice_fusion.3
  223.7 2.9 convolution_bitcast_fusion
  226.6 1.1 fusion.12
  227.7 1.1 slice_dynamic-update-slice_fusion.2
  228.8 1.1 slice_dynamic-update-slice_fusion.1
  229.9 0.9 slice_dynamic-update-slice_fusion
  230.9 4.7 fusion.83
  235.6 2.2 fusion.1
  237.8 47.8 %reduce-scatter.5.cloned.1.call-done = bf16[2,32,256]{2,1,0:T(8,128)(2,1)} async-done(((bf16[2,512,256]{2,1,0:T(8,128)(2,1)}), bf16[2,32,256]{2,1,0:T(8,128)(2,1)}) %reduce-scatter.5.cloned.1.call-update) | async-done | bytes 32784 | tf_op jit(solution)/shard_map/reduce_scatter | solution.py:92
  286.4 1.0 multiply_convert_fusion
  287.4 274.4 %all-reduce.5.cloned.1.call-done = (f32[2304,256]{1,0:T(8,128)}, f32[2304,256]{1,0:T(8,128)}) async-done(((f32[2304,256]{1,0:T(8,128)}, f32[2304,256]{1,0:T(8,128)}), (f32[2304,256]{1,0:T(8,128)}, f32[2304,256]{1,0:T(8,128)})) %all-reduce.5.cloned.1.call-update) | async-done | bytes 4718608 | tf_op jit(solution)/shard_map/psum | solution.py:143
  561.8 1.6 dynamic-slice_multiply_fusion
  563.4 1.6 dynamic-slice_multiply_fusion.1
  (141 shorter events, 19.4 us)
Async XLA Ops:
  7.2 45.4 %copy-start.1 = (bf16[2304,256]{1,0:T(8,128)(2,1)S(1)}, bf16[2304,256]{1,0:T(8,128)(2,1)}, u32[]{:S(2)}) copy-start(bf16[2304,256]{1,0:T(8,128)(2,1)} %param.20) | copy-start | bytes 3538948
  7.2 49.4 %copy-start = (bf16[2304,256]{1,0:T(8,128)(2,1)S(1)}, bf16[2304,256]{1,0:T(8,128)(2,1)}, u32[]{:S(2)}) copy-start(bf16[2304,256]{1,0:T(8,128)(2,1)} %param.19) | copy-start | bytes 3538948
  7.2 145.6 %reduce-scatter.3.cloned.1.call-start = ((), (), s32[]{:S(2)}) async-start(), calls=%async_computation.2 | async-start | bytes 557056 | tf_op jit(solution)/shard_map/reduce_scatter | solution.py:92
  10.1 59.6 %collective-permute-start = (bf16[32,1,256]{2,1,0:T(2,128)(2,1)}, bf16[32,1,256]{2,1,0:T(2,128)(2,1)S(1)}, u32[]{:S(2)}, u32[]{:S(2)}) collective-permute-start(bf16[32,1,256]{2,1,0:T(2,128)(2,1)} %get-tuple-element.112), channel_id=1, source_target_pairs={{0,16},{16,32},{32,48},{48,64},{64,80},{80,96},{96,112},{112,128},... | collective-permute-start | bytes 49160 | tf_op jit(solution)/shard_map/ppermute | solution.py:15
  14.4 55.3 %collective-permute-start.1 = (bf16[32,1,256]{2,1,0:T(2,128)(2,1)}, bf16[32,1,256]{2,1,0:T(2,128)(2,1)S(1)}, u32[]{:S(2)}, u32[]{:S(2)}) collective-permute-start(bf16[32,1,256]{2,1,0:T(2,128)(2,1)} %get-tuple-element.113), channel_id=1, source_target_pairs={{16,0},{32,16},{48,32},{64,48},{80,64},{96,80},{112,96},{128,112},... | collective-permute-start | bytes 49160 | tf_op jit(solution)/shard_map/ppermute | solution.py:18
  15.1 60.2 %collective-permute-start.8 = (bf16[32,1,256]{2,1,0:T(2,128)(2,1)}, bf16[32,1,256]{2,1,0:T(2,128)(2,1)S(1)}, u32[]{:S(2)}, u32[]{:S(2)}) collective-permute-start(bf16[32,1,256]{2,1,0:T(2,128)(2,1)} %get-tuple-element.100), channel_id=1, source_target_pairs={{0,16},{16,32},{32,48},{48,64},{64,80},{80,96},{96,112},{112,128},... | collective-permute-start | bytes 49160 | tf_op jit(solution)/shard_map/ppermute | solution.py:15
  18.3 56.9 %collective-permute-start.9 = (bf16[32,1,256]{2,1,0:T(2,128)(2,1)}, bf16[32,1,256]{2,1,0:T(2,128)(2,1)S(1)}, u32[]{:S(2)}, u32[]{:S(2)}) collective-permute-start(bf16[32,1,256]{2,1,0:T(2,128)(2,1)} %get-tuple-element.101), channel_id=1, source_target_pairs={{16,0},{32,16},{48,32},{64,48},{80,64},{96,80},{112,96},{128,112},... | collective-permute-start | bytes 49160 | tf_op jit(solution)/shard_map/ppermute | solution.py:18
  59.7 5.8 %copy-start.5 = (bf16[3,256,256]{1,2,0:T(8,128)(2,1)S(1)}, bf16[3,256,256]{1,2,0:T(8,128)(2,1)}, u32[]{:S(2)}) copy-start(bf16[3,256,256]{1,2,0:T(8,128)(2,1)} %get-tuple-element.61) | copy-start | bytes 1179652
  70.3 15.3 %collective-permute-start.3 = (bf16[1,34,256]{2,1,0:T(8,128)(2,1)}, bf16[1,34,256]{2,1,0:T(8,128)(2,1)}, u32[]{:S(2)}, u32[]{:S(2)}) collective-permute-start(bf16[1,34,256]{2,1,0:T(8,128)(2,1)} %get-tuple-element.80), channel_id=1, source_target_pairs={{1,0},{2,1},{3,2},{4,3},{5,4},{6,5},{7,6},{8,7},{9,8},{10,9},{11,1... | collective-permute-start | bytes 52232 | tf_op jit(solution)/shard_map/ppermute | solution.py:18
  75.2 11.2 %collective-permute-start.2 = (bf16[1,34,256]{2,1,0:T(8,128)(2,1)}, bf16[1,34,256]{2,1,0:T(8,128)(2,1)}, u32[]{:S(2)}, u32[]{:S(2)}) collective-permute-start(bf16[1,34,256]{2,1,0:T(8,128)(2,1)} %get-tuple-element.81), channel_id=1, source_target_pairs={{0,1},{1,2},{2,3},{3,4},{4,5},{5,6},{6,7},{7,8},{8,9},{9,10},{10,1... | collective-permute-start | bytes 52232 | tf_op jit(solution)/shard_map/ppermute | solution.py:15
  75.9 13.4 %collective-permute-start.11 = (bf16[1,34,256]{2,1,0:T(8,128)(2,1)}, bf16[1,34,256]{2,1,0:T(8,128)(2,1)}, u32[]{:S(2)}, u32[]{:S(2)}) collective-permute-start(bf16[1,34,256]{2,1,0:T(8,128)(2,1)} %get-tuple-element.72), channel_id=1, source_target_pairs={{0,1},{1,2},{2,3},{3,4},{4,5},{5,6},{6,7},{7,8},{8,9},{9,10},{10,1... | collective-permute-start | bytes 52232 | tf_op jit(solution)/shard_map/ppermute | solution.py:15
  75.9 13.5 %collective-permute-start.10 = (bf16[1,34,256]{2,1,0:T(8,128)(2,1)}, bf16[1,34,256]{2,1,0:T(8,128)(2,1)}, u32[]{:S(2)}, u32[]{:S(2)}) collective-permute-start(bf16[1,34,256]{2,1,0:T(8,128)(2,1)} %get-tuple-element.73), channel_id=1, source_target_pairs={{1,0},{2,1},{3,2},{4,3},{5,4},{6,5},{7,6},{8,7},{9,8},{10,9},{11,1... | collective-permute-start | bytes 52232 | tf_op jit(solution)/shard_map/ppermute | solution.py:18
  85.3 200.3 %reduce-scatter.5.cloned.1.call-start = ((), (), s32[]{:S(2)}) async-start(), calls=%async_computation.3 | async-start | bytes 557056 | tf_op jit(solution)/shard_map/reduce_scatter | solution.py:92
  89.3 2.1 copy-start.12
  91.4 1.6 copy-start.6
  93.0 63.3 %copy-start.14 = (f32[32]{0:T(128)S(1)}, f32[32]{0:T(128)}, u32[]{:S(2)}) copy-start(f32[32]{0:T(128)} %fusion.73) | copy-start | bytes 388
  161.4 42.3 %copy-start.4 = (bf16[3,256,256]{2,1,0:T(8,128)(2,1)S(1)}, bf16[3,256,256]{2,1,0:T(8,128)(2,1)}, u32[]{:S(2)}) copy-start(bf16[3,256,256]{2,1,0:T(8,128)(2,1)} %copy.28) | copy-start | bytes 1179652
  192.1 7.7 %collective-permute-start.4 = (bf16[32,1,256]{2,1,0:T(2,128)(2,1)}, bf16[32,1,256]{2,1,0:T(2,128)(2,1)S(1)}, u32[]{:S(2)}, u32[]{:S(2)}) collective-permute-start(bf16[32,1,256]{2,1,0:T(2,128)(2,1)} %get-tuple-element.106), channel_id=1, source_target_pairs={{0,16},{16,32},{32,48},{48,64},{64,80},{80,96},{96,112},{112,128},... | collective-permute-start | bytes 49160 | tf_op jit(solution)/shard_map/ppermute | solution.py:15
  192.7 7.0 %collective-permute-start.5 = (bf16[32,1,256]{2,1,0:T(2,128)(2,1)}, bf16[32,1,256]{2,1,0:T(2,128)(2,1)S(1)}, u32[]{:S(2)}, u32[]{:S(2)}) collective-permute-start(bf16[32,1,256]{2,1,0:T(2,128)(2,1)} %get-tuple-element.107), channel_id=1, source_target_pairs={{16,0},{32,16},{48,32},{64,48},{80,64},{96,80},{112,96},{128,112},... | collective-permute-start | bytes 49160 | tf_op jit(solution)/shard_map/ppermute | solution.py:18
  194.0 19.3 %copy-start.11 = (bf16[34,256]{1,0:T(8,128)(2,1)S(1)}, bf16[34,256]{1,0:T(8,128)(2,1)}, u32[]{:S(2)}) copy-start(bf16[34,256]{1,0:T(8,128)(2,1)} %gather_fusion.3) | copy-start | bytes 52228
  194.7 8.9 %collective-permute-start.12 = (bf16[32,1,256]{2,1,0:T(2,128)(2,1)S(1)}, bf16[32,1,256]{2,1,0:T(2,128)(2,1)S(1)}, u32[]{:S(2)}, u32[]{:S(2)}) collective-permute-start(bf16[32,1,256]{2,1,0:T(2,128)(2,1)S(1)} %get-tuple-element.94), channel_id=1, source_target_pairs={{0,16},{16,32},{32,48},{48,64},{64,80},{80,96},{96,112},{112,128},... | collective-permute-start | bytes 49160 | tf_op jit(solution)/shard_map/ppermute | solution.py:15
  198.0 5.6 collective-permute-start.13
  199.8 3.8 copy-start.9
  199.8 3.9 copy-start.7
  199.8 13.5 %collective-permute-start.6 = (bf16[1,34,256]{2,1,0:T(8,128)(2,1)S(1)}, bf16[1,34,256]{2,1,0:T(8,128)(2,1)S(1)}, u32[]{:S(2)}, u32[]{:S(2)}) collective-permute-start(bf16[1,34,256]{2,1,0:T(8,128)(2,1)S(1)} %get-tuple-element.77), channel_id=1, source_target_pairs={{0,1},{1,2},{2,3},{3,4},{4,5},{5,6},{6,7},{7,8},{8,9},{9,10},{10,1... | collective-permute-start | bytes 52232 | tf_op jit(solution)/shard_map/ppermute | solution.py:15
  200.7 13.4 %collective-permute-start.7 = (bf16[1,34,256]{2,1,0:T(8,128)(2,1)S(1)}, bf16[1,34,256]{2,1,0:T(8,128)(2,1)S(1)}, u32[]{:S(2)}, u32[]{:S(2)}) collective-permute-start(bf16[1,34,256]{2,1,0:T(8,128)(2,1)S(1)} %get-tuple-element.76), channel_id=1, source_target_pairs={{1,0},{2,1},{3,2},{4,3},{5,4},{6,5},{7,6},{8,7},{9,8},{10,9},{11,1... | collective-permute-start | bytes 52232 | tf_op jit(solution)/shard_map/ppermute | solution.py:18
  203.8 11.0 %copy-start.8 = (bf16[32,1,256]{2,1,0:T(2,128)(2,1)S(1)}, bf16[32,1,256]{2,1,0:T(2,128)(2,1)}, u32[]{:S(2)}) copy-start(bf16[32,1,256]{2,1,0:T(2,128)(2,1)} %copy-done.7) | copy-start | bytes 49156
  203.8 11.0 %copy-start.10 = (bf16[32,1,256]{2,1,0:T(2,128)(2,1)S(1)}, bf16[32,1,256]{2,1,0:T(2,128)(2,1)}, u32[]{:S(2)}) copy-start(bf16[32,1,256]{2,1,0:T(2,128)(2,1)} %copy-done.9) | copy-start | bytes 49156
  210.5 351.3 %all-reduce.5.cloned.1.call-start = ((), (), s32[]{:S(2)}) async-start(), calls=%async_computation.4 | async-start | bytes 9437184 | tf_op jit(solution)/shard_map/psum | solution.py:143
  210.6 6.4 %collective-permute-start.14 = (bf16[1,34,256]{2,1,0:T(8,128)(2,1)S(1)}, bf16[1,34,256]{2,1,0:T(8,128)(2,1)S(1)}, u32[]{:S(2)}, u32[]{:S(2)}) collective-permute-start(bf16[1,34,256]{2,1,0:T(8,128)(2,1)S(1)} %get-tuple-element.69), channel_id=1, source_target_pairs={{1,0},{2,1},{3,2},{4,3},{5,4},{6,5},{7,6},{8,7},{9,8},{10,9},{11,1... | collective-permute-start | bytes 52232 | tf_op jit(solution)/shard_map/ppermute | solution.py:18
  213.3 4.7 collective-permute-start.15
  216.9 6.8 %copy-start.13 = (bf16[32,32,2304]{2,1,0:T(8,128)(2,1)}, bf16[32,32,2304]{2,1,0:T(8,128)(2,1)S(1)}, u32[]{:S(2)}) copy-start(bf16[32,32,2304]{2,1,0:T(8,128)(2,1)S(1)} %slice_dynamic-update-slice_fusion.12) | copy-start | bytes 14155780
  229.9 5.6 slice-start
  230.9 4.7 copy-start.2
  230.9 4.7 slice-start.1
  230.9 4.7 copy-start.15
  235.6 50.8 %copy-start.3 = (bf16[32,32,256]{2,1,0:T(8,128)(2,1)S(1)}, bf16[32,32,256]{2,1,0:T(8,128)(2,1)}, u32[]{:S(2)}) copy-start(bf16[32,32,256]{2,1,0:T(8,128)(2,1)} %param.21) | copy-start | bytes 1572868
Sparse Core Ops, SparseCore 0:
  85.4 67.3 reduce-scatter.2
  210.6 74.9 reduce-scatter.4
  291.2 270.5 all-reduce.4
where the time goes:
time: 574 us; the launch traced here: 572 us
  waiting for transfers between devices  381 us (66%)
  blocking collectives  51.1 us (9%)
  local copies, waits for them, and re-layouts  36.2 us (6%)
  other arithmetic  35.1 us (6%)
  starting transfers between devices  29.7 us (5%)
  matrix products  23.3 us (4%)
  between operations  15.2 us (3%)
    psum x1, waiting for transfers between devices, local(): lax.psum((first_local, second_local), ('lon', 'lat'))  274 us
    reduce_scatter x2, waiting for transfers between devices, route_rim(): lax.psum_scatter(spread.astype(jnp.bfloat16), 'lon', scatter_dimension=1,...  105 us
    all_gather x2, blocking collectives, padded_field(): loop_rows = lax.all_gather(edges, 'lon', axis=1, tiled=True)  51.1 us
    ppermute x8, starting transfers between devices, with_halo(): lax.ppermute(lax.slice_in_dim(block, 0, width, axis=dim), axis, backward)  16.9 us
    ppermute x8, starting transfers between devices, with_halo(): lax.ppermute(lax.slice_in_dim(block, block.shape[dim] - width, None, axis...  12.5 us
  transfers between devices with their start and end apart: 19, of which 4 were waited for; matrix products, arithmetic and copies ran while one was open for 13% of the time, Pallas kernels for 0%

commit v1 on v0

v1 whole, which is shorter than its diff:
```python
import math

import jax
import jax.numpy as jnp
from jax import lax
from jax.experimental import pallas as pl
from jax.experimental.pallas import tpu as pltpu
from jax.sharding import PartitionSpec as P

MESH = pl.DeviceIdType.MESH
BF = jnp.bfloat16
F32 = jnp.float32
C = 256
T = 32
EXT = T + 4
PX = EXT * T
RING = T + 2
MSG = 5 * T
STRIP = 40
LON = 16
LAT = 16
PLANES = 8
SHARE = 3 * T // 2 * 3
FIRST = (0, 3, 6, 8, 10, 12, 14, 16)


def dot(a, b):
    return jnp.dot(a, b, preferred_element_type=F32)


def gelu_parts(pre):
    cdf = 0.5 * (1.0 + lax.erf(pre * 0.7071067811865476))
    dens = jnp.exp(-0.5 * pre * pre) * 0.3989422804014327
    return (pre * cdf, cdf + pre * dens)


def rows(start, size=T):
    return pl.ds(pl.multiple_of(start * T, T), size)


def kernel(
    field,
    w1,
    w2,
    cot,
    live_ref,
    links,
    out,
    fgrad,
    grad1,
    grad2,
    sx,
    sd,
    sh,
    sg,
    zx,
    zd,
    zh,
    zg,
    zs,
    kz,
    cols,
    corner,
    slope,
    xt,
    dz,
    wt1,
    wt2,
    ext,
    send_ns,
    send_ew,
    send_dg,
    halo_ns,
    halo_ew,
    halo_dg,
    polar,
    gkeep,
    gsend,
    gpair,
    gsum,
    parts2,
    tiles,
    parts3,
    own,
    final,
    hs_sem,
    hr_sem,
    ps_sem,
    pr_sem,
    s1_sem,
    r1_sem,
    s2_sem,
    r2_sem,
    s3_sem,
    r3_sem,
    s4_sem,
    r4_sem,
):
    u, v = lax.axis_index("lon"), lax.axis_index("lat")
    core, x, z = u % 2, u // 4, v // 2
    y = (u // 2) % 2 * 2 + v % 2
    spot = x * 4 + y
    north, south = v == 0, v == LAT - 1
    side = jnp.where(south, 1, 0)
    live = live_ref[0, 0]
    east, west = (u + 1) % LON, (u + LON - 1) % LON

    def in_plane(place):
        px, py = place // 4, place % 4
        return {"lon": px * 4 + py // 2 * 2 + core, "lat": z * 2 + py % 2}

    def in_column(plane):
        return {"lon": u, "lat": plane * 2 + v % 2}

    barrier = pltpu.get_barrier_semaphore()

    def greet(lon, lat):
        pl.semaphore_signal(barrier, inc=1, device_id={"lon": lon, "lat": lat}, device_id_type=MESH)

    greet(east, v)
    greet(west, v)

    @pl.when(v > 0)
    def _():
        for lon in (west, u, east):
            greet(lon, v - 1)

    @pl.when(v < LAT - 1)
    def _():
        for lon in (west, u, east):
            greet(lon, v + 1)

    @pl.when(north | south)
    def _():
        @pl.loop(1, LON)
        def _(d):
            greet((u + d) % LON, v)

    @pl.loop(1, 16)
    def _(d):
        to = in_plane((spot + d) % 16)
        greet(to["lon"], to["lat"])

    @pl.loop(1, PLANES)
    def _(d):
        greet(u, (z + d) % PLANES * 2 + v % 2)

    lane_row = lax.broadcasted_iota(jnp.int32, (T, C), 0)

    @pl.loop(0, T)
    def _(i):
        kept = jnp.full((T, C), i, jnp.int32) < live
        for k, (src, dst) in enumerate(((field, sx), (cot, sd))):
            line = jnp.where(kept, src[i].astype(F32), 0.0)
            dst[1, rows(i + 2), :] = line.astype(BF)
            for n, col in enumerate((0, 1, T - 2, T - 1)):
                cols[k, n, pl.ds(i, 1), :] = line[col : col + 1]

    keep_col = jnp.where(lane_row < live, 1.0, 0.0)
    keep_last = jnp.where(jnp.full((T, C), T - 1, jnp.int32) < live, 1.0, 0.0)
    for s in range(2):
        for k, src in enumerate((sx, sd)):
            first = 2 if s == 0 else T
            send_ns[s, 2 * k * T : (2 * k + 2) * T, :] = src[1, first * T : (first + 2) * T, :]
            for n in range(2):
                send_ew[s, (2 * k + n) * T : (2 * k + n + 1) * T, :] = cols[k, 2 * s + n].astype(BF)
        send_ns[s, 4 * T :, :] = jnp.ones((T, C), BF) if s == 0 else keep_last.astype(BF)
        send_ew[s, 4 * T :, :] = keep_col.astype(BF)
    corner[...] = jnp.zeros_like(corner)
    for s in range(2):
        for t in range(2):
            for k in range(2):
                for r in range(2):
                    for n in range(2):
                        at = 4 * k + 2 * r + n
                        line = (0 if s == 0 else T - 2) + r
                        corner[2 * s + t, at : at + 1, :] = cols[k, 2 * t + n, line : line + 1, :]
            corner[2 * s + t, 8:9, :] = jnp.ones((1, C), F32) if s == 0 else keep_last[0:1]
    send_dg[...] = corner[...].astype(BF)

    here = jnp.where(v > 0, 3, 0) + jnp.where(v < LAT - 1, 3, 0) + jnp.where(north | south, 15, 0)
    pl.semaphore_wait(barrier, here + 2 + 15 + 7)

    def edge(src, dst, n, lon, lat):
        return pltpu.make_async_remote_copy(
            src_ref=src,
            dst_ref=dst,
            send_sem=hs_sem.at[n],
            recv_sem=hr_sem.at[n],
            device_id={"lon": lon, "lat": lat},
            device_id_type=MESH,
        )

    to_west = edge(send_ew.at[0], halo_ew.at[1], 0, west, v)
    to_east = edge(send_ew.at[1], halo_ew.at[0], 1, east, v)
    to_north = [
        edge(send_ns.at[0], halo_ns.at[1], 2, u, v - 1),
        edge(send_dg.at[0], halo_dg.at[3], 3, west, v - 1),
        edge(send_dg.at[1], halo_dg.at[2], 4, east, v - 1),
    ]
    to_south = [
        edge(send_ns.at[1], halo_ns.at[0], 5, u, v + 1),
        edge(send_dg.at[2], halo_dg.at[1], 6, west, v + 1),
        edge(send_dg.at[3], halo_dg.at[0], 7, east, v + 1),
    ]

    def around(lon):
        return pltpu.make_async_remote_copy(
            src_ref=send_ns.at[side],
            dst_ref=polar.at[u],
            send_sem=ps_sem,
            recv_sem=pr_sem,
            device_id={"lon": lon, "lat": v},
            device_id_type=MESH,
        )

    @pl.when(north | south)
    def _():
        @pl.loop(1, LON)
        def _(d):
            around((u + d) % LON).start()

    to_west.start()
    to_east.start()

    @pl.when(v > 0)
    def _():
        for copy in to_north:
            copy.start()

    @pl.when(v < LAT - 1)
    def _():
        for copy in to_south:
            copy.start()

    @pl.loop(0, 9)
    def _(tap):
        at = pl.ds(pl.multiple_of(tap * C, C), C)
        wt1[at, :] = w1[at, :].T
        wt2[at, :] = w2[at, :].T

    for ref in (zx, zd, zh, zg, zs, ext):
        ref[...] = jnp.zeros_like(ref)
    for b in range(3):
        sh[b, 0:T, :] = jnp.zeros((T, C), BF)
        sh[b, PX - T : PX, :] = jnp.zeros((T, C), BF)
    dz[0 : 3 * T, :] = jnp.zeros((3 * T, C), BF)
    dz[35 * T : 38 * T, :] = jnp.zeros((3 * T, C), BF)
    dz[3 * T : 35 * T, :] = sd[1, 2 * T : 34 * T, :]

    to_west.wait_recv()
    to_east.wait_recv()

    @pl.when(v > 0)
    def _():
        for copy in to_south:
            copy.wait_recv()

    @pl.when(v < LAT - 1)
    def _():
        for copy in to_north:
            copy.wait_recv()

    def drain(ref, sem):
        pltpu.make_async_copy(ref, ref, sem).wait()

    @pl.when(north | south)
    def _():
        drain(polar.at[pl.ds(0, LON - 1)], pr_sem)
        drain(polar.at[pl.ds(0, LON - 1)], ps_sem)
        polar[u] = send_ns[side]
        pivot = links[side, 0]
        n = lax.broadcasted_iota(jnp.int32, (2 * T, LON * T), 0)
        at = lax.broadcasted_iota(jnp.int32, (2 * T, LON * T), 1)
        q = n & 15
        in_east = n >= T + 16
        ring_col = jnp.where(in_east, T, -1)
        outer_col = jnp.where(in_east, T, -2) + (q & 1)
        col = jnp.where(n < T, n, jnp.where(q == 8, ring_col, outer_col))
        hit = ((pivot - u * T - col) & (LON * T - 1)) == at
        line = jnp.where(q == 8, 4, jnp.where(q < 8, q // 2, 5))
        corners = jnp.zeros((T, C), F32)
        for part in range(5):
            target = part if part == 4 else part ^ 1
            pick = jnp.where(hit & ((n < T) | (line == target)), 1.0, 0.0).astype(BF)
            lines = polar[:, part * T : (part + 1) * T, :].reshape(LON * T, C)
            found = dot(pick, lines)
            halo_ns[side, target * T : (target + 1) * T, :] = found[:T].astype(BF)
            corners = corners + found[T:]
        halo_dg[2 * side] = corners[:16].astype(BF)
        halo_dg[2 * side + 1] = corners[16:].astype(BF)

    for k, (s, zz) in enumerate(((sx, zx), (sd, zd))):
        s[1, 0 : 2 * T, :] = halo_ns[0, 2 * k * T : (2 * k + 2) * T, :]
        s[1, 34 * T : 36 * T, :] = halo_ns[1, 2 * k * T : (2 * k + 2) * T, :]
        for n in range(2):
            zz[n, 2 : 2 + T, :] = halo_ew[0, (2 * k + n) * T : (2 * k + n + 1) * T, :].astype(F32)
            zz[4 + n, 2 : 2 + T, :] = halo_ew[1, (2 * k + n) * T : (2 * k + n + 1) * T, :].astype(F32)
        for dg in range(4):
            px = halo_dg[dg].astype(F32)
            for r in range(2):
                for n in range(2):
                    e = dg // 2 * 34 + r
                    at = 4 * k + 2 * r + n
                    zz[dg % 2 * 4 + n, e : e + 1, :] = px[at : at + 1]
    kz[...] = jnp.zeros_like(kz)
    for t in range(2):
        kz[t, 2 : 2 + T, :] = halo_ew[t, 4 * T :, :].astype(F32)
        kz[t, 1:2, :] = halo_dg[t].astype(F32)[8:9]
        kz[t, 34:35, :] = halo_dg[2 + t].astype(F32)[8:9]

    def shifted(s, left, right, lo, hi, zz=None):
        @pl.loop(lo, hi)
        def _(e):
            at = rows(e)
            line = s[1, at, :].astype(F32)
            s[0, at, :] = jnp.where(lane_row == 0, left[pl.ds(e, 1), :], pltpu.roll(line, 1, 0)).astype(BF)
            s[2, at, :] = jnp.where(
                lane_row == T - 1, right[pl.ds(e, 1), :], pltpu.roll(line, T - 1, 0)
            ).astype(BF)
            if zz is not None:
                zz[2, pl.ds(e, 1), :] = line[0:1]
                zz[3, pl.ds(e, 1), :] = line[T - 1 : T]

    def transposed(s):
        @pl.loop(0, PX // 128)
        def _(k):
            at = pl.ds(pl.multiple_of(k * 128, 128), 128)
            for b in range(3):
                xt[b * C : (b + 1) * C, at] = s[b, at, :].T

    shifted(sx, zx.at[1], zx.at[4], 0, EXT, zx)
    shifted(sd, zd.at[1], zd.at[4], 0, EXT, zd)

    e_out, e_ring = jnp.where(south, 35, 0), jnp.where(south, 34, 1)
    e_edge, e_in = jnp.where(south, 33, 2), jnp.where(south, 32, 3)
    far = jnp.where(south, 2, 0)

    def extend(n, s, left, right, e):
        ext[n, 2 : 2 + T, :] = s[1, rows(e), :].astype(F32)
        for k, ref in enumerate(left):
            at = 2 - len(left) + k
            ext[n, at : at + 1, :] = ref[pl.ds(e, 1), :]
        for k, ref in enumerate(right):
            ext[n, 34 + k : 35 + k, :] = ref[pl.ds(e, 1), :]

    def straight(n):
        return jnp.concatenate([ext[n, 2 - b : 42 - b, :] for b in range(3)], axis=1).astype(BF)

    def turned(n):
        return jnp.concatenate([ext[n, b : b + 40, :] for b in range(3)], axis=1).astype(BF)

    def taps(w, row):
        return w[pl.ds(pl.multiple_of(row * 3 * C, 3 * C), 3 * C), :]

    def strips(zz, w, back):
        order = (2, 1, 0) if back else (0, 1, 2)
        both = jnp.concatenate(
            [jnp.concatenate([zz[3 * t + b] for b in order], axis=1) for t in range(2)], axis=0
        ).astype(BF)
        up, mid, down = (dot(both, w[a * 3 * C : (a + 1) * 3 * C, :]) for a in range(3))
        if back:
            up, down = down, up
        return pltpu.roll(up, 1, 0) + mid + pltpu.roll(down, 2 * STRIP - 1, 0)

    step = 272

    @pl.loop(0, RING * T // step)
    def _(c):
        m = pl.multiple_of(c * step, 16)
        stacked = jnp.concatenate(
            [sx[b, pl.ds(pl.multiple_of(m + a * T, 16), step), :] for a in range(3) for b in range(3)],
            axis=1,
        )
        act, slp = gelu_parts(dot(stacked, w1[...]))
        row = (lax.broadcasted_iota(jnp.int32, (step, C), 0) + m) // T
        kept = (row - 1 < live) | (row == RING - 1)
        sh[1, pl.ds(pl.multiple_of(m + T, 16), step), :] = jnp.where(kept, act, 0.0).astype(BF)
        slope[pl.ds(m, step), :] = jnp.where(kept, slp, 0.0)

    act, slp = gelu_parts(strips(zx, w1, False))
    for t in range(2):
        zh[t] = act[t * STRIP : (t + 1) * STRIP] * kz[t]
        zs[t] = slp[t * STRIP : (t + 1) * STRIP] * kz[t]

    @pl.when(north | south)
    def _():
        for n, e in enumerate((e_out, e_ring, e_edge)):
            extend(n, sx, (zx.at[0], zx.at[1]), (zx.at[4], zx.at[5]), e)
        pre = dot(straight(2), taps(w1, far)) + dot(straight(1), taps(w1, 1)) + dot(straight(0), taps(w1, 2 - far))
        act, slp = gelu_parts(pre)
        sh[1, rows(e_ring), :] = act[1 : 1 + T].astype(BF)
        slope[rows(e_ring - 1), :] = slp[1 : 1 + T]
        for t in range(2):
            at = t * (T + 1)
            mask = kz[t, pl.ds(e_ring, 1), :]
            zh[t, pl.ds(e_ring, 1), :] = act[at : at + 1] * mask
            zs[t, pl.ds(e_ring, 1), :] = slp[at : at + 1] * mask

    for s in range(2):
        mask = halo_ns[s, 4 * T :, :].astype(F32)
        e = 1 if s == 0 else 34
        sh[1, e * T : (e + 1) * T, :] = (sh[1, e * T : (e + 1) * T, :].astype(F32) * mask).astype(BF)
        slope[(e - 1) * T : e * T, :] = slope[(e - 1) * T : e * T, :] * mask

    shifted(sh, zh.at[0], zh.at[1], 1, 35)
    transposed(sh)

    sibling = {"lon": u + 1 - 2 * core, "lat": v}

    def pair(g, a):
        return pltpu.make_async_remote_copy(
            src_ref=gsend.at[g, a],
            dst_ref=gpair.at[g, a],
            send_sem=s1_sem.at[g, a],
            recv_sem=r1_sem.at[g, a],
            device_id=sibling,
            device_id_type=MESH,
        )

    def scatter(g, a):
        pair(g, a).wait()
        gsum[g, a] = (gkeep[g, a] + gpair[g, a].astype(F32)).astype(BF)

        @pl.loop(1, 16)
        def _(d):
            to = (spot + d) % 16
            pltpu.make_async_remote_copy(
                src_ref=gsum.at[g, a, :, pl.ds(pl.multiple_of(to * 16, 16), 16), :],
                dst_ref=parts2.at[g, a, spot],
                send_sem=s2_sem.at[g, a],
                recv_sem=r2_sem.at[g, a],
                device_id=in_plane(to),
                device_id_type=MESH,
            ).start()

    def weight_grad(g):
        @pl.loop(0, 3)
        def _(a):
            res = dot(xt[...], dz[rows(2 - a, PX), :])
            lo, hi = res[:, : C // 2], res[:, C // 2 :]
            gkeep[g, a] = jnp.where(core == 0, lo, hi).reshape(3, C, C // 2)
            gsend[g, a] = jnp.where(core == 0, hi, lo).astype(BF).reshape(3, C, C // 2)
            pair(g, a).start()

            @pl.when(a > 0)
            def _():
                scatter(g, a - 1)

    weight_grad(0)

    @pl.loop(0, RING * T // step)
    def _(c):
        m = pl.multiple_of(c * step, 16)
        stacked = jnp.concatenate(
            [
                sd[2 - b, pl.ds(pl.multiple_of(m + (2 - a) * T, 16), step), :]
                for a in range(3)
                for b in range(3)
            ],
            axis=1,
        )
        back = dot(stacked, wt2[...])
        sg[1, pl.ds(pl.multiple_of(m + T, 16), step), :] = (back * slope[pl.ds(m, step), :]).astype(BF)

    scatter(0, 2)
    back = strips(zd, wt2, True)
    for t in range(2):
        zg[t] = back[t * STRIP : (t + 1) * STRIP] * zs[t]

    @pl.when(north | south)
    def _():
        for n, e in enumerate((e_out, e_ring, e_edge, e_in)):
            extend(n, sd, (zd.at[0], zd.at[1]), (zd.at[4], zd.at[5]), e)
        w_far, w_mid = taps(wt2, far), taps(wt2, 1)
        ring = dot(turned(0), w_far) + dot(straight(2), w_far) + dot(turned(1), w_mid)
        rim = dot(turned(1), w_far) + dot(straight(3), w_far) + dot(straight(2), w_mid)
        for e, res in ((e_ring, ring), (e_edge, rim)):
            sg[1, rows(e), :] = (res[1 : 1 + T] * slope[rows(e - 1), :]).astype(BF)
            for t in range(2):
                at = t * (T + 1)
                zg[t, pl.ds(e, 1), :] = res[at : at + 1] * zs[t, pl.ds(e, 1), :]

    shifted(sg, zg.at[0], zg.at[1], 1, 35)
    dz[3 * T : 35 * T, :] = sg[1, 2 * T : 34 * T, :]
    transposed(sx)
    weight_grad(1)

    size = 8 * T

    @pl.loop(0, T * T // size)
    def _(c):
        m = pl.multiple_of(c * size, size)
        stacked = jnp.concatenate(
            [
                sh[b, pl.ds(pl.multiple_of(m + (1 + a) * T, T), size), :]
                for a in range(3)
                for b in range(3)
            ],
            axis=1,
        )
        pre = dot(stacked, w2[...])
        row = (lax.broadcasted_iota(jnp.int32, (size, C), 0) + m) // T
        masked = sx[1, pl.ds(pl.multiple_of(m + 2 * T, T), size), :].astype(F32)
        res = (masked + jnp.where(row < live, pre, 0.0)).astype(BF)
        out[pl.ds(c * 8, 8)] = res.reshape(8, T, C)

    scatter(1, 2)

    @pl.loop(0, T * T // size)
    def _(c):
        m = pl.multiple_of(c * size, size)
        stacked = jnp.concatenate(
            [
                sg[2 - b, pl.ds(pl.multiple_of(m + (3 - a) * T, T), size), :]
                for a in range(3)
                for b in range(3)
            ],
            axis=1,
        )
        back = dot(stacked, wt1[...])
        row = (lax.broadcasted_iota(jnp.int32, (size, C), 0) + m) // T
        total = cot[pl.ds(c * 8, 8)].reshape(size, C).astype(F32) + back
        fgrad[pl.ds(c * 8, 8)] = jnp.where(row < live, total, 0.0).astype(BF).reshape(8, T, C)

    @pl.when(north | south)
    def _():
        for n, e in ((1, e_ring), (2, e_edge), (3, e_in)):
            extend(n, sg, (zg.at[0],), (zg.at[1],), e)
        w_far, w_mid = taps(wt1, far), taps(wt1, 1)
        rim = dot(turned(1), w_far) + dot(straight(3), w_far) + dot(straight(2), w_mid)
        i = e_edge - 2
        total = cot[i].astype(F32) + rim[1 : 1 + T]
        kept = jnp.full((T, C), i, jnp.int32) < live
        fgrad[i] = jnp.where(kept, total, 0.0).astype(BF)

    tiles[18] = jnp.zeros((16, C // 2), BF)
    for g in range(2):
        for a in range(3):
            drain(parts2.at[g, a, pl.ds(0, 15)], r2_sem.at[g, a])
            parts2[g, a, spot] = gsum[g, a, :, pl.ds(pl.multiple_of(spot * 16, 16), 16), :]
            total = parts2[g, a, 0].astype(F32)
            for k in range(1, 16):
                total = total + parts2[g, a, k].astype(F32)
            tiles[9 * g + 3 * a : 9 * g + 3 * a + 3] = total.astype(BF)

    def window(plane):
        start = plane * 3
        for k, first in enumerate(FIRST):
            if first != 3 * k:
                start = jnp.where(plane == k, first, start)
        return start

    @pl.loop(1, PLANES)
    def _(d):
        to = (z + d) % PLANES
        pltpu.make_async_remote_copy(
            src_ref=tiles.at[pl.ds(window(to), 3)],
            dst_ref=parts3.at[z],
            send_sem=s3_sem,
            recv_sem=r3_sem,
            device_id=in_column(to),
            device_id_type=MESH,
        ).start()

    mine = window(z)
    drain(parts3.at[pl.ds(0, PLANES - 1)], r3_sem)
    parts3[z] = tiles[pl.ds(mine, 3)]
    total = parts3[0].astype(F32)
    for k in range(1, PLANES):
        total = total + parts3[k].astype(F32)
    own[...] = total.astype(BF)

    def deliver(slot, act):
        tile = mine + slot
        g = tile // 9
        place = tile % 9 * 16 + spot
        lat, at = place // 9, place % 9

        @pl.loop(0, LON)
        def _(d):
            to = (u + d) % LON
            src, dst = own.at[slot], final.at[g, at, core]

            @pl.when((d == 0) & (lat == v))
            def _():
                if act:
                    pltpu.make_async_copy(src, dst, r4_sem).start()

            @pl.when((d > 0) | (lat != v))
            def _():
                copy = pltpu.make_async_remote_copy(
                    src_ref=src,
                    dst_ref=dst,
                    send_sem=s4_sem.at[slot, d],
                    recv_sem=r4_sem,
                    device_id={"lon": to, "lat": lat},
                    device_id_type=MESH,
                )
                if act:
                    copy.start()
                else:
                    copy.wait_send()

    for act in (True, False):
        deliver(0, act)
        deliver(1, act)

        @pl.when(z < 2)
        def _(act=act):
            deliver(2, act)

        if act:
            drain(final, r4_sem)

    scale = 1.0 / math.sqrt(LON * T * LAT * T)
    for g, ref in enumerate((grad2, grad1)):
        for k in range(9):
            for h in range(2):
                ref[k * 16 : (k + 1) * 16, h * 128 : (h + 1) * 128] = final[g, k, h].astype(F32) * scale

    to_west.wait_send()
    to_east.wait_send()

    @pl.when(v > 0)
    def _():
        for copy in to_north:
            copy.wait_send()

    @pl.when(v < LAT - 1)
    def _():
        for copy in to_south:
            copy.wait_send()

    for g in range(2):
        for a in range(3):
            drain(parts2.at[g, a, pl.ds(0, 15)], s2_sem.at[g, a])
    drain(parts3.at[pl.ds(0, PLANES - 1)], s3_sem)


def local(field, first_weight, second_weight, cotangent, live_rows, polar_links):
    vmem = pl.BlockSpec(memory_space=pltpu.VMEM)
    smem = pl.BlockSpec(memory_space=pltpu.SMEM)
    tile = jax.ShapeDtypeStruct((T, T, C), BF)
    share = jax.ShapeDtypeStruct((SHARE, C), F32)
    flat = pltpu.VMEM((3, PX, C), BF)
    columns = pltpu.VMEM((6, STRIP, C), F32)
    two = pltpu.VMEM((2, STRIP, C), F32)
    half = C // 2
    output, field_grad, grad1, grad2 = pl.pallas_call(
        kernel,
        out_shape=(tile, tile, share, share),
        in_specs=[vmem, vmem, vmem, vmem, smem, smem],
        out_specs=(vmem, vmem, vmem, vmem),
        scratch_shapes=[
            flat,
            flat,
            flat,
            flat,
            columns,
            columns,
            two,
            two,
            two,
            two,
            pltpu.VMEM((2, 4, T, C), F32),
            pltpu.VMEM((4, 16, C), F32),
            pltpu.VMEM((RING * T, C), F32),
            pltpu.VMEM((3 * C, PX), BF),
            pltpu.VMEM((38 * T, C), BF),
            pltpu.VMEM((9 * C, C), BF),
            pltpu.VMEM((9 * C, C), BF),
            pltpu.VMEM((4, 48, C), F32),
            pltpu.VMEM((2, MSG, C), BF),
            pltpu.VMEM((2, MSG, C), BF),
            pltpu.VMEM((4, 16, C), BF),
            pltpu.VMEM((2, MSG, C), BF),
            pltpu.VMEM((2, MSG, C), BF),
            pltpu.VMEM((4, 16, C), BF),
            pltpu.VMEM((LON, MSG, C), BF),
            pltpu.VMEM((2, 3, 3, C, half), F32),
            pltpu.VMEM((2, 3, 3, C, half), BF),
            pltpu.VMEM((2, 3, 3, C, half), BF),
            pltpu.VMEM((2, 3, 3, C, half), BF),
            pltpu.VMEM((2, 3, 16, 3, 16, half), BF),
            pltpu.VMEM((19, 16, half), BF),
            pltpu.VMEM((PLANES, 3, 16, half), BF),
            pltpu.VMEM((3, 16, half), BF),
            pltpu.VMEM((2, 9, 2, 16, half), BF),
            pltpu.SemaphoreType.DMA((8,)),
            pltpu.SemaphoreType.DMA((8,)),
            pltpu.SemaphoreType.DMA,
            pltpu.SemaphoreType.DMA,
            pltpu.SemaphoreType.DMA((2, 3)),
            pltpu.SemaphoreType.DMA((2, 3)),
            pltpu.SemaphoreType.DMA((2, 3)),
            pltpu.SemaphoreType.DMA((2, 3)),
            pltpu.SemaphoreType.DMA,
            pltpu.SemaphoreType.DMA,
            pltpu.SemaphoreType.DMA((3, LON)),
            pltpu.SemaphoreType.DMA,
        ],
        compiler_params=pltpu.CompilerParams(
            collective_id=0, has_side_effects=True, vmem_limit_bytes=56 * 1024 * 1024
        ),
        cost_estimate=pl.CostEstimate(
            flops=12 * T * T * 9 * C * C, bytes_accessed=6_000_000, transcendentals=2 * T * T * C
        ),
    )(field, first_weight, second_weight, cotangent, live_rows, polar_links)
    return (output, field_grad, grad1, grad2)


def solution(mesh):
    in_specs = (P("lat", "lon", None), P(), P(), P("lat", "lon", None), P("lon", "lat"), P())
    out_specs = (P("lat", "lon", None), P("lat", "lon", None), P("lat", None), P("lat", None))
    return jax.shard_map(local, mesh=mesh, in_specs=in_specs, out_specs=out_specs, check_vma=False)
```

time: 574 us -> 85.8 us (0.15)
  waiting for transfers between devices: 381 us -> 0 us
  Pallas kernels: 0 us -> 80.3 us
  blocking collectives: 51.1 us -> 0 us
  other arithmetic: 35.1 us -> 0 us
  local copies, waits for them, and re-layouts: 36.2 us -> 4.07 us
  starting transfers between devices: 29.7 us -> 0 us
  matrix products: 23.3 us -> 0 us
  between operations: 15.2 us -> 1.31 us
    psum x1 -> x0, waiting for transfers between devices: 274 us -> none  [local(): lax.psum((first_local, second_local), ('lon', 'lat'))]
    reduce_scatter x2 -> x0, waiting for transfers between devices: 105 us -> none  [route_rim(): lax.psum_scatter(spread.astype(jnp.bfloat16), 'lon', scatter_dimension=1,...]
    pallas_call x0 -> x1, Pallas kernels: none -> 80.3 us  [local(): pl.pallas_call(kernel, out_shape=(tile, tile, share, share), in_specs=[vm...]
    all_gather x2 -> x0, blocking collectives: 51.1 us -> none  [padded_field(): loop_rows = lax.all_gather(edges, 'lon', axis=1, tiled=True)]
    ppermute x16 -> x0, starting transfers between devices: 29.4 us -> none  [the longest x8 16.9 us: with_halo(): lax.ppermute(lax.slice_in_dim(block, 0, width, axis=dim), axis, backward)]
    dot_general x10 -> x0, matrix products: 23.3 us -> none  [the longest x2 8.06 us: weight_term(): lax.dot_general(stacked, flat, (((0,), (0,)), ((), ())), preferred_elemen...]
    scatter-add x8 -> x0, other arithmetic: 11.8 us -> none  [the longest x4 9.02 us: route_rim(): spread.at[0, targets[0]].add(terms[0]).at[1, targets[1]].add(terms[1])]
    slice x14 -> x0, local copies, waits for them, and re-layouts: 10.1 us -> none  [the longest x4 4.96 us: spread_back(): flipped[6 * channels:]]
  transfers between devices with their start and end apart: 19 -> 0, of which waited for: 4 -> 0; matrix products, arithmetic and copies ran while one was open for 13% -> 0% of each run, Pallas kernels for 0% -> 0%
where the time goes in v1:
time: 85.8 us; the launch traced here: 85.7 us
  Pallas kernels  80.3 us (94%)
  local copies, waits for them, and re-layouts  4.07 us (5%)
  between operations  1.31 us (2%)
    pallas_call x1, Pallas kernels, local(): pl.pallas_call(kernel, out_shape=(tile, tile, share, share), in_specs=[vm...  80.3 us
    unnamed x10, local copies, waits for them, and re-layouts  4.07 us

profile of v1, /device:TPU:1, one launch (start us, length us, event | category | flops | bytes accessed | tf_op | source)
XLA Modules:
  0.0 85.7 jit_solution(8843890043425665592)
XLA Ops:
  1.3 80.3 %shard_map.93 = (bf16[32,32,256]{2,1,0:T(8,128)(2,1)}, bf16[32,32,256]{2,1,0:T(8,128)(2,1)}, f32[144,256]{1,0:T(8,128)}, f32[144,256]{1,0:T(8,128)}) custom-call(bf16[32,32,256]{2,1,0:T(8,128)(2,1)} %field.1, bf16[2304,256]{1,0:T(8,128)(2,1)} %w1.1, bf16[2304,256]{1,0:T(8,128)(2,1)} %w2.1, bf16[32,32,256]{2,1,0:T(8,128)(2,1)} %cot.1, ...), custom_call_target="tpu_custom_call" | custom-call | flops 7247757312 | bytes 6000000 | tf_op jit(solution)/shard_map/pallas_call | solution.py:650
  81.6 0.0 copy-start
  81.6 0.0 copy-start.2
  81.6 0.0 copy-start.1
  81.6 1.9 %copy.15 = bf16[32,32,256]{2,1,0:T(8,128)(2,1)} copy(bf16[32,32,256]{2,1,0:T(8,128)(2,1)} %get-tuple-element.8) | data formatting | bytes 1048576
  83.5 0.0 copy-done
  83.6 0.8 copy.16
  84.3 0.0 copy-done.2
  84.3 0.7 copy.17
  85.0 0.0 copy-done.1
  85.0 0.7 copy.18
Async XLA Ops:
  81.6 2.0 %copy-start = (bf16[32,32,256]{2,1,0:T(8,128)(2,1)S(1)}, bf16[32,32,256]{2,1,0:T(8,128)(2,1)}, u32[]{:S(2)}) copy-start(bf16[32,32,256]{2,1,0:T(8,128)(2,1)} %get-tuple-element.9) | copy-start | bytes 1572868
  81.6 2.8 %copy-start.2 = (f32[144,256]{1,0:T(8,128)S(1)}, f32[144,256]{1,0:T(8,128)}, u32[]{:S(2)}) copy-start(f32[144,256]{1,0:T(8,128)} %get-tuple-element.10) | copy-start | bytes 442372
  81.6 3.4 %copy-start.1 = (f32[144,256]{1,0:T(8,128)S(1)}, f32[144,256]{1,0:T(8,128)}, u32[]{:S(2)}) copy-start(f32[144,256]{1,0:T(8,128)} %get-tuple-element.11) | copy-start | bytes 442372

commit v2 on v1

v2 whole, which is shorter than its diff:
```python
import math

import jax
import jax.numpy as jnp
from jax import lax
from jax.experimental import pallas as pl
from jax.experimental.pallas import tpu as pltpu
from jax.sharding import PartitionSpec as P

MESH = pl.DeviceIdType.MESH
BF = jnp.bfloat16
F32 = jnp.float32
C = 256
T = 32
EXT = T + 4
PX = EXT * T
RING = T + 2
MSG = 5 * T
STRIP = 40
LON = 16
LAT = 16
PLANES = 8
SHARE = 3 * T // 2 * 3
PICK = MSG + T


def dot(a, b):
    return jnp.dot(a, b, preferred_element_type=F32)


def gelu_parts(pre):
    cdf = 0.5 * (1.0 + lax.erf(pre * 0.7071067811865476))
    dens = jnp.exp(-0.5 * pre * pre) * 0.3989422804014327
    return (pre * cdf, cdf + pre * dens)


def rows(start, size=T):
    return pl.ds(pl.multiple_of(start * T, T), size)


def finish(made, back, sums, out, fgrad, grad1, grad2):
    out[...] = made[...]
    fgrad[...] = back[...]
    scale = 1.0 / math.sqrt(LON * T * LAT * T)
    for g, ref in enumerate((grad2, grad1)):
        for k in range(9):
            for h in range(2):
                ref[k * 16 : (k + 1) * 16, h * 128 : (h + 1) * 128] = sums[k, h, g].astype(F32) * scale


def kernel(
    field,
    w1_hbm,
    w2_hbm,
    cot,
    live_ref,
    links,
    out,
    fgrad,
    sums,
    sx,
    sd,
    sh,
    sg,
    zx,
    zd,
    zh,
    zg,
    zs,
    kz,
    fix,
    cols,
    corner,
    pre1,
    back2,
    slope,
    xt,
    dz,
    w1,
    w2,
    wt1,
    wt2,
    ext,
    send_ns,
    send_ew,
    send_dg,
    halo_ns,
    halo_ew,
    halo_dg,
    near,
    picked,
    arrived,
    gkeep,
    gsend,
    gpair,
    gsum,
    parts2,
    tiles,
    parts3,
    own,
    final,
    w_sem,
    hs_sem,
    hr_sem,
    pas_sem,
    par_sem,
    pbs_sem,
    pbr_sem,
    s1_sem,
    r1_sem,
    s2_sem,
    r2_sem,
    s3_sem,
    r3_sem,
    s4_sem,
    r4_sem,
):
    u, v = lax.axis_index("lon"), lax.axis_index("lat")
    core, x, z = u % 2, u // 4, v // 2
    y = (u // 2) % 2 * 2 + v % 2
    spot = x * 4 + y
    north, south = v == 0, v == LAT - 1
    rim_tile = north | south
    side = jnp.where(south, 1, 0)
    live = live_ref[0, 0]
    east, west = (u + 1) % LON, (u + LON - 1) % LON

    def in_plane(place):
        px, py = place // 4, place % 4
        return {"lon": px * 4 + py // 2 * 2 + core, "lat": z * 2 + py % 2}

    def quarter(d):
        return u // 4 * 4 + (u % 4 + d) % 4

    w1_copy = pltpu.make_async_copy(w1_hbm, w1, w_sem.at[0])
    w2_copy = pltpu.make_async_copy(w2_hbm, w2, w_sem.at[1])
    w1_copy.start()
    w2_copy.start()

    barrier = pltpu.get_barrier_semaphore()

    def greet(lon, lat):
        pl.semaphore_signal(barrier, inc=1, device_id={"lon": lon, "lat": lat}, device_id_type=MESH)

    greet(east, v)
    greet(west, v)

    @pl.when(v > 0)
    def _():
        for lon in (west, u, east):
            greet(lon, v - 1)

    @pl.when(v < LAT - 1)
    def _():
        for lon in (west, u, east):
            greet(lon, v + 1)

    @pl.when(rim_tile)
    def _():
        for d in range(1, 4):
            greet(quarter(d), v)
            greet((u + 4 * d) % LON, v)

    @pl.loop(1, 16)
    def _(d):
        to = in_plane((spot + d) % 16)
        greet(to["lon"], to["lat"])

    @pl.loop(1, PLANES)
    def _(d):
        greet(u, (z + d) % PLANES * 2 + v % 2)

    lane_row = lax.broadcasted_iota(jnp.int32, (T, C), 0)

    @pl.loop(0, T)
    def _(i):
        kept = jnp.full((T, C), i, jnp.int32) < live
        for k, (src, dst) in enumerate(((field, sx), (cot, sd))):
            line = jnp.where(kept, src[i].astype(F32), 0.0)
            dst[1, rows(i + 2), :] = line.astype(BF)
            for n, col in enumerate((0, 1, T - 2, T - 1)):
                cols[k, n, pl.ds(i, 1), :] = line[col : col + 1]

    keep_col = jnp.where(lane_row < live, 1.0, 0.0)
    keep_last = jnp.where(jnp.full((T, C), T - 1, jnp.int32) < live, 1.0, 0.0)
    for s in range(2):
        for k, src in enumerate((sx, sd)):
            first = 2 if s == 0 else T
            send_ns[s, 2 * k * T : (2 * k + 2) * T, :] = src[1, first * T : (first + 2) * T, :]
            for n in range(2):
                send_ew[s, (2 * k + n) * T : (2 * k + n + 1) * T, :] = cols[k, 2 * s + n].astype(BF)
        send_ns[s, 4 * T :, :] = jnp.ones((T, C), BF) if s == 0 else keep_last.astype(BF)
        send_ew[s, 4 * T :, :] = keep_col.astype(BF)
    corner[...] = jnp.zeros_like(corner)
    for s in range(2):
        for t in range(2):
            for k in range(2):
                for r in range(2):
                    for n in range(2):
                        at = 4 * k + 2 * r + n
                        line = (0 if s == 0 else T - 2) + r
                        corner[2 * s + t, at : at + 1, :] = cols[k, 2 * t + n, line : line + 1, :]
            corner[2 * s + t, 8:9, :] = jnp.ones((1, C), F32) if s == 0 else keep_last[0:1]
    send_dg[...] = corner[...].astype(BF)

    here = jnp.where(v > 0, 3, 0) + jnp.where(v < LAT - 1, 3, 0) + jnp.where(rim_tile, 6, 0)
    pl.semaphore_wait(barrier, here + 2 + 15 + 7)

    def remote(src, dst, send, recv, to):
        return pltpu.make_async_remote_copy(
            src_ref=src, dst_ref=dst, send_sem=send, recv_sem=recv, device_id=to, device_id_type=MESH
        )

    def drain(ref, sem):
        pltpu.make_async_copy(ref, ref, sem).wait()

    def edge(src, dst, n, lon, lat):
        return remote(src, dst, hs_sem.at[n], hr_sem.at[n], {"lon": lon, "lat": lat})

    @pl.when(rim_tile)
    def _():
        for d in range(1, 4):
            remote(send_ns.at[side], near.at[u % 4], pas_sem, par_sem, {"lon": quarter(d), "lat": v}).start()

    to_west = edge(send_ew.at[0], halo_ew.at[1], 0, west, v)
    to_east = edge(send_ew.at[1], halo_ew.at[0], 1, east, v)
    to_north = [
        edge(send_ns.at[0], halo_ns.at[1], 2, u, v - 1),
        edge(send_dg.at[0], halo_dg.at[3], 3, west, v - 1),
        edge(send_dg.at[1], halo_dg.at[2], 4, east, v - 1),
    ]
    to_south = [
        edge(send_ns.at[1], halo_ns.at[0], 5, u, v + 1),
        edge(send_dg.at[2], halo_dg.at[1], 6, west, v + 1),
        edge(send_dg.at[3], halo_dg.at[0], 7, east, v + 1),
    ]

    to_west.start()
    to_east.start()

    @pl.when(v > 0)
    def _():
        for copy in to_north:
            copy.start()

    @pl.when(v < LAT - 1)
    def _():
        for copy in to_south:
            copy.start()

    @pl.loop(2, 34)
    def _(e):
        at = rows(e)
        for s in (sx, sd):
            line = s[1, at, :].astype(F32)
            s[0, at, :] = jnp.where(lane_row == 0, 0.0, pltpu.roll(line, 1, 0)).astype(BF)
            s[2, at, :] = jnp.where(lane_row == T - 1, 0.0, pltpu.roll(line, T - 1, 0)).astype(BF)

    for ref in (zx, zd, zh, zg, zs, ext, kz):
        ref[...] = jnp.zeros_like(ref)
    for b in range(3):
        sh[b, 0:T, :] = jnp.zeros((T, C), BF)
        sh[b, PX - T : PX, :] = jnp.zeros((T, C), BF)
    dz[0 : 3 * T, :] = jnp.zeros((3 * T, C), BF)
    dz[35 * T : 38 * T, :] = jnp.zeros((3 * T, C), BF)
    dz[3 * T : 35 * T, :] = sd[1, 2 * T : 34 * T, :]
    tiles[:, 9] = jnp.zeros((2, 16, C // 2), BF)

    def window(s, back, first, size):
        pieces = []
        for a in range(3):
            for b in range(3):
                start = (first + (2 - a if back else a)) * T
                pieces.append(s[2 - b if back else b, start : start + size * T, :])
        return jnp.concatenate(pieces, axis=1)

    w1_copy.wait()
    pre1[2 * T : 32 * T, :] = dot(window(sx, False, 2, 30), w1[...])

    @pl.when(rim_tile)
    def _():
        drain(near.at[pl.ds(0, 3)], par_sem)
        drain(near.at[pl.ds(0, 3)], pas_sem)
        near[u % 4] = send_ns[side]
        pivot = links[side, 0]
        n = lax.broadcasted_iota(jnp.int32, (8 * T, 4 * T), 0)
        at = lax.broadcasted_iota(jnp.int32, (8 * T, 4 * T), 1) + x * (4 * T)
        to = (n // (2 * T)) * 4 + u % 4
        n = n & (2 * T - 1)
        q = n & 15
        in_east = n >= T + 16
        ring_col = jnp.where(in_east, T, -1)
        outer_col = jnp.where(in_east, T, -2) + (q & 1)
        col = jnp.where(n < T, n, jnp.where(q == 8, ring_col, outer_col))
        hit = ((pivot - to * T - col) & (LON * T - 1)) == at
        line = jnp.where(q == 8, 4, jnp.where(q < 8, q // 2, 5))
        corners = jnp.zeros((4, T, C), F32)
        for part in range(5):
            target = part if part == 4 else part ^ 1
            pick = jnp.where(hit & ((n < T) | (line == target)), 1.0, 0.0).astype(BF)
            lines = near[:, part * T : (part + 1) * T, :].reshape(4 * T, C)
            found = dot(pick, lines).reshape(4, 2 * T, C)
            picked[:, target * T : (target + 1) * T, :] = found[:, :T].astype(BF)
            corners = corners + found[:, T:]
        picked[:, MSG:, :] = corners.astype(BF)
        for d in range(1, 4):
            to = (x + d) % 4
            remote(picked.at[to], arrived.at[x], pbs_sem, pbr_sem, {"lon": (u + 4 * d) % LON, "lat": v}).start()

    w2_copy.wait()

    @pl.loop(0, 9)
    def _(tap):
        at = pl.ds(pl.multiple_of(tap * C, C), C)
        wt2[at, :] = w2[at, :].T

    back2[2 * T : 32 * T, :] = dot(window(sd, True, 2, 30), wt2[...])

    to_west.wait_recv()
    to_east.wait_recv()

    @pl.when(v > 0)
    def _():
        for copy in to_south:
            copy.wait_recv()

    @pl.when(v < LAT - 1)
    def _():
        for copy in to_north:
            copy.wait_recv()

    @pl.when(rim_tile)
    def _():
        drain(arrived.at[pl.ds(0, 3)], pbr_sem)
        drain(arrived.at[pl.ds(0, 3)], pbs_sem)
        arrived[x] = picked[x]
        total = arrived[0].astype(F32)
        for k in range(1, 4):
            total = total + arrived[k].astype(F32)
        halo_ns[side] = total[:MSG].astype(BF)
        halo_dg[2 * side] = total[MSG : MSG + 16].astype(BF)
        halo_dg[2 * side + 1] = total[MSG + 16 :].astype(BF)

    head = lax.broadcasted_iota(jnp.int32, (16, C), 0)
    for k, (s, zz) in enumerate(((sx, zx), (sd, zd))):
        for n in range(2):
            zz[n, 2 : 2 + T, :] = halo_ew[0, (2 * k + n) * T : (2 * k + n + 1) * T, :].astype(F32)
            zz[4 + n, 2 : 2 + T, :] = halo_ew[1, (2 * k + n) * T : (2 * k + n + 1) * T, :].astype(F32)
            zz[2 + n, 2 : 2 + T, :] = cols[k, 3 * n]
        for dg in range(4):
            px = halo_dg[dg].astype(F32)
            for r in range(2):
                for n in range(2):
                    e = dg // 2 * 34 + r
                    at = 4 * k + 2 * r + n
                    zz[dg % 2 * 4 + n, e : e + 1, :] = px[at : at + 1]
        for e in (0, 1, 34, 35):
            h, r = e // 34, e % 34
            line = halo_ns[h, (2 * k + r) * T : (2 * k + r + 1) * T, :].astype(F32)
            s[1, e * T : (e + 1) * T, :] = line.astype(BF)
            s[0, e * T : (e + 1) * T, :] = jnp.where(
                lane_row == 0, zz[1, e : e + 1, :], pltpu.roll(line, 1, 0)
            ).astype(BF)
            s[2, e * T : (e + 1) * T, :] = jnp.where(
                lane_row == T - 1, zz[4, e : e + 1, :], pltpu.roll(line, T - 1, 0)
            ).astype(BF)
            zz[2, e : e + 1, :] = line[0:1]
            zz[3, e : e + 1, :] = line[T - 1 : T]

    def insert(s, zz, e):
        at = pl.ds(pl.multiple_of(e * T, T), 16)
        s[0, at, :] = jnp.where(head == 0, zz[1, pl.ds(e, 1), :], s[0, at, :].astype(F32)).astype(BF)
        at = pl.ds(pl.multiple_of(e * T + 16, 16), 16)
        s[2, at, :] = jnp.where(head == 15, zz[4, pl.ds(e, 1), :], s[2, at, :].astype(F32)).astype(BF)

    for e in (2, 3, 32, 33):
        insert(sd, zd, e)

    @pl.loop(2, 34)
    def _(e):
        insert(sx, zx, e)

    for t in range(2):
        kz[t, 2 : 2 + T, :] = halo_ew[t, 4 * T :, :].astype(F32)
        kz[t, 1:2, :] = halo_dg[t].astype(F32)[8:9]
        kz[t, 34:35, :] = halo_dg[2 + t].astype(F32)[8:9]

    def transposed(s):
        @pl.loop(0, PX // 128)
        def _(k):
            at = pl.ds(pl.multiple_of(k * 128, 128), 128)
            for b in range(3):
                xt[b * C : (b + 1) * C, at] = s[b, at, :].T

    e_out, e_ring = jnp.where(south, 35, 0), jnp.where(south, 34, 1)
    e_edge, e_in = jnp.where(south, 33, 2), jnp.where(south, 32, 3)
    far = jnp.where(south, 2, 0)

    def extend(n, s, left, right, e):
        ext[n, 2 : 2 + T, :] = s[1, rows(e), :].astype(F32)
        for k, ref in enumerate(left):
            at = 2 - len(left) + k
            ext[n, at : at + 1, :] = ref[pl.ds(e, 1), :]
        for k, ref in enumerate(right):
            ext[n, 34 + k : 35 + k, :] = ref[pl.ds(e, 1), :]

    def straight(n):
        return jnp.concatenate([ext[n, 2 - b : 42 - b, :] for b in range(3)], axis=1).astype(BF)

    def turned(n):
        return jnp.concatenate([ext[n, b : b + 40, :] for b in range(3)], axis=1).astype(BF)

    def taps(w, row):
        return w[pl.ds(pl.multiple_of(row * 3 * C, 3 * C), 3 * C), :]

    def combine(up, mid, down, back):
        if back:
            up, down = down, up
        return pltpu.roll(up, 1, 0) + mid + pltpu.roll(down, mid.shape[0] - 1, 0)

    def strips(zz, w, back):
        order = (2, 1, 0) if back else (0, 1, 2)
        both = jnp.concatenate(
            [jnp.concatenate([zz[3 * t + b] for b in order], axis=1) for t in range(2)], axis=0
        ).astype(BF)
        ring = combine(*(dot(both, w[a * 3 * C : (a + 1) * 3 * C, :]) for a in range(3)), back)
        row = lax.broadcasted_iota(jnp.int32, (STRIP, C), 0)
        for t in range(2):
            b = 2 - 2 * t if back else 2 * t
            line = zz[1 + 3 * t].astype(BF)
            res = combine(*(dot(line, w[(3 * a + b) * C : (3 * a + b + 1) * C, :]) for a in range(3)), back)
            fix[t] = jnp.where((row > 2) & (row < 33), res, 0.0)
        return ring

    def with_fix(line, e):
        line = line + jnp.where(lane_row == 0, fix[0, pl.ds(e, 1), :], 0.0)
        return line + jnp.where(lane_row == T - 1, fix[1, pl.ds(e, 1), :], 0.0)

    def spread(s, zz, e, line):
        at = rows(e)
        s[1, at, :] = line.astype(BF)
        s[0, at, :] = jnp.where(lane_row == 0, zz[0, pl.ds(e, 1), :], pltpu.roll(line, 1, 0)).astype(BF)
        s[2, at, :] = jnp.where(lane_row == T - 1, zz[1, pl.ds(e, 1), :], pltpu.roll(line, T - 1, 0)).astype(BF)

    def outer(s, back):
        return jnp.concatenate([window(s, back, 0, 2), window(s, back, 32, 2)], axis=0)

    res = dot(outer(sx, False), w1[...])
    pre1[0 : 2 * T, :] = res[: 2 * T]
    pre1[32 * T : 34 * T, :] = res[2 * T :]
    ring = strips(zx, w1, False)
    for t in range(2):
        zh[t] = ring[t * STRIP : (t + 1) * STRIP]

    @pl.when(rim_tile)
    def _():
        for n, e in enumerate((e_out, e_ring, e_edge)):
            extend(n, sx, (zx.at[0], zx.at[1]), (zx.at[4], zx.at[5]), e)
        pre = dot(straight(2), taps(w1, far)) + dot(straight(1), taps(w1, 1)) + dot(straight(0), taps(w1, 2 - far))
        pre1[rows(e_ring - 1), :] = pre[1 : 1 + T]
        for t in range(2):
            at = t * (T + 1)
            zh[t, pl.ds(e_ring, 1), :] = pre[at : at + 1]

    for t in range(2):
        act, slp = gelu_parts(zh[t])
        zh[t] = act * kz[t]
        zs[t] = slp * kz[t]

    def activate(e, mask):
        act, slp = gelu_parts(with_fix(pre1[rows(e - 1), :], e))
        slope[rows(e - 1), :] = slp * mask
        spread(sh, zh, e, act * mask)

    for s in range(2):
        activate(1 + 33 * s, halo_ns[s, 4 * T :, :].astype(F32))

    @pl.loop(2, 34)
    def _(e):
        activate(e, jnp.where(jnp.full((T, C), e - 2, jnp.int32) < live, 1.0, 0.0))

    transposed(sh)

    sibling = {"lon": u + 1 - 2 * core, "lat": v}

    def pair(g, a):
        return remote(gsend.at[g, a], gpair.at[g, a], s1_sem.at[g, a], r1_sem.at[g, a], sibling)

    def scatter(g, a):
        pair(g, a).wait()
        gsum[g, a] = (gkeep[g, a] + gpair[g, a].astype(F32)).astype(BF)

        @pl.loop(1, 16)
        def _(d):
            to = (spot + d) % 16
            remote(
                gsum.at[g, a, :, pl.ds(pl.multiple_of(to * 16, 16), 16), :],
                parts2.at[g, a, spot],
                s2_sem.at[g, a],
                r2_sem.at[g, a],
                in_plane(to),
            ).start()

    def weight_grad(g):
        @pl.loop(0, 3)
        def _(a):
            res = dot(xt[...], dz[rows(2 - a, PX), :])
            lo, hi = res[:, : C // 2], res[:, C // 2 :]
            gkeep[g, a] = jnp.where(core == 0, lo, hi).reshape(3, C, C // 2)
            gsend[g, a] = jnp.where(core == 0, hi, lo).astype(BF).reshape(3, C, C // 2)
            pair(g, a).start()

            @pl.when(a > 0)
            def _():
                scatter(g, a - 1)

    weight_grad(0)

    res = dot(outer(sd, True), wt2[...])
    back2[0 : 2 * T, :] = res[: 2 * T]
    back2[32 * T : 34 * T, :] = res[2 * T :]
    ring = strips(zd, wt2, True)
    for t in range(2):
        zg[t] = ring[t * STRIP : (t + 1) * STRIP]

    @pl.when(rim_tile)
    def _():
        for n, e in enumerate((e_out, e_ring, e_edge, e_in)):
            extend(n, sd, (zd.at[0], zd.at[1]), (zd.at[4], zd.at[5]), e)
        w_far, w_mid = taps(wt2, far), taps(wt2, 1)
        ring = dot(turned(0), w_far) + dot(straight(2), w_far) + dot(turned(1), w_mid)
        rim = dot(turned(1), w_far) + dot(straight(3), w_far) + dot(straight(2), w_mid)
        for e, res in ((e_ring, ring), (e_edge, rim)):
            back2[rows(e - 1), :] = res[1 : 1 + T]
            for t in range(2):
                at = t * (T + 1)
                zg[t, pl.ds(e, 1), :] = res[at : at + 1]

    for t in range(2):
        zg[t] = zg[t] * zs[t]
    scatter(0, 2)

    @pl.loop(1, 35)
    def _(e):
        spread(sg, zg, e, with_fix(back2[rows(e - 1), :], e) * slope[rows(e - 1), :])

    dz[3 * T : 35 * T, :] = sg[1, 2 * T : 34 * T, :]
    transposed(sx)
    weight_grad(1)

    row = lax.broadcasted_iota(jnp.int32, (T * T, C), 0) // T
    pre = dot(window(sh, False, 1, T), w2[...])
    masked = sx[1, 2 * T : 34 * T, :].astype(F32)
    out[...] = (masked + jnp.where(row < live, pre, 0.0)).astype(BF).reshape(T, T, C)

    @pl.loop(0, 9)
    def _(tap):
        at = pl.ds(pl.multiple_of(tap * C, C), C)
        wt1[at, :] = w1[at, :].T

    scatter(1, 2)

    back = dot(window(sg, True, 1, T), wt1[...])
    total = cot[...].reshape(T * T, C).astype(F32) + back
    fgrad[...] = jnp.where(row < live, total, 0.0).astype(BF).reshape(T, T, C)

    @pl.when(rim_tile)
    def _():
        for n, e in ((1, e_ring), (2, e_edge), (3, e_in)):
            extend(n, sg, (zg.at[0],), (zg.at[1],), e)
        w_far, w_mid = taps(wt1, far), taps(wt1, 1)
        rim = dot(turned(1), w_far) + dot(straight(3), w_far) + dot(straight(2), w_mid)
        i = e_edge - 2
        total = cot[i].astype(F32) + rim[1 : 1 + T]
        kept = jnp.full((T, C), i, jnp.int32) < live
        fgrad[i] = jnp.where(kept, total, 0.0).astype(BF)

    for g in range(2):
        for a in range(3):
            drain(parts2.at[g, a, pl.ds(0, 15)], r2_sem.at[g, a])
            parts2[g, a, spot] = gsum[g, a, :, pl.ds(pl.multiple_of(spot * 16, 16), 16), :]
            total = parts2[g, a, 0].astype(F32)
            for k in range(1, 16):
                total = total + parts2[g, a, k].astype(F32)
            tiles[g, 3 * a : 3 * a + 3] = total.astype(BF)

    def first_tile(plane):
        return (18 * plane + 15 - spot) // 16

    @pl.loop(1, PLANES)
    def _(d):
        to = (z + d) % PLANES
        remote(
            tiles.at[:, pl.ds(first_tile(to), 2)],
            parts3.at[z],
            s3_sem,
            r3_sem,
            {"lon": u, "lat": to * 2 + v % 2},
        ).start()

    mine = first_tile(z)
    drain(parts3.at[pl.ds(0, PLANES - 1)], r3_sem)
    parts3[z] = tiles[:, pl.ds(mine, 2)]
    total = parts3[0].astype(F32)
    for k in range(1, PLANES):
        total = total + parts3[k].astype(F32)
    for slot in range(2):
        own[slot] = total[:, slot].astype(BF)

    def deliver(slot):
        group = (mine + slot) * 16 + spot
        lat, at = group // 9, group % 9
        src, dst = own.at[slot], final.at[at, core]

        def to(d):
            return remote(src, dst, s4_sem.at[slot, d], r4_sem, {"lon": (u + d) % LON, "lat": lat})

        @pl.loop(1, LON)
        def _(d):
            to(d).start()

        @pl.when(lat == v)
        def _():
            pltpu.make_async_copy(src, dst, r4_sem).start()

        @pl.when(lat != v)
        def _():
            to(0).start()

        def left():
            @pl.loop(1, LON)
            def _(d):
                to(d).wait_send()

            @pl.when(lat != v)
            def _():
                to(0).wait_send()

        return left

    has_two = first_tile(z + 1) - mine == 2
    left0 = deliver(0)

    @pl.when(has_two)
    def _():
        deliver(1)

    drain(final, r4_sem)
    sums[...] = final[...]

    left0()

    @pl.when(has_two)
    def _():
        group = (mine + 1) * 16 + spot
        lat = group // 9
        dst = final.at[group % 9, core]

        def to(d):
            return remote(own.at[1], dst, s4_sem.at[1, d], r4_sem, {"lon": (u + d) % LON, "lat": lat})

        @pl.loop(1, LON)
        def _(d):
            to(d).wait_send()

        @pl.when(lat != v)
        def _():
            to(0).wait_send()

    to_west.wait_send()
    to_east.wait_send()

    @pl.when(v > 0)
    def _():
        for copy in to_north:
            copy.wait_send()

    @pl.when(v < LAT - 1)
    def _():
        for copy in to_south:
            copy.wait_send()

    for g in range(2):
        for a in range(3):
            drain(parts2.at[g, a, pl.ds(0, 15)], s2_sem.at[g, a])
    drain(parts3.at[pl.ds(0, PLANES - 1)], s3_sem)


def local(field, first_weight, second_weight, cotangent, live_rows, polar_links):
    vmem = pl.BlockSpec(memory_space=pltpu.VMEM)
    smem = pl.BlockSpec(memory_space=pltpu.SMEM)
    anywhere = pl.BlockSpec(memory_space=pl.ANY)
    half = C // 2
    tile = jax.ShapeDtypeStruct((T, T, C), BF)
    share = jax.ShapeDtypeStruct((SHARE, C), F32)
    flat = pltpu.VMEM((3, PX, C), BF)
    columns = pltpu.VMEM((6, STRIP, C), F32)
    two = pltpu.VMEM((2, STRIP, C), F32)
    ringed = pltpu.VMEM((RING * T, C), F32)
    weights = pltpu.VMEM((9 * C, C), BF)
    message = pltpu.VMEM((2, MSG, C), BF)
    corners = pltpu.VMEM((4, 16, C), BF)
    grads = pltpu.VMEM((2, 3, 3, C, half), BF)
    dma = pltpu.SemaphoreType.DMA
    made, back, sums = pl.pallas_call(
        kernel,
        out_shape=(tile, tile, jax.ShapeDtypeStruct((9, 2, 2, 16, half), BF)),
        in_specs=[vmem, anywhere, anywhere, vmem, smem, smem],
        out_specs=(vmem, vmem, vmem),
        scratch_shapes=[
            *([flat] * 4),
            *([columns] * 2),
            *([two] * 5),
            pltpu.VMEM((2, 4, T, C), F32),
            pltpu.VMEM((4, 16, C), F32),
            *([ringed] * 3),
            pltpu.VMEM((3 * C, PX), BF),
            pltpu.VMEM((38 * T, C), BF),
            *([weights] * 4),
            pltpu.VMEM((4, 48, C), F32),
            message,
            message,
            corners,
            message,
            message,
            corners,
            pltpu.VMEM((4, MSG, C), BF),
            pltpu.VMEM((4, PICK, C), BF),
            pltpu.VMEM((4, PICK, C), BF),
            pltpu.VMEM((2, 3, 3, C, half), F32),
            grads,
            grads,
            grads,
            pltpu.VMEM((2, 3, 16, 3, 16, half), BF),
            pltpu.VMEM((2, 10, 16, half), BF),
            pltpu.VMEM((PLANES, 2, 2, 16, half), BF),
            pltpu.VMEM((2, 2, 16, half), BF),
            pltpu.VMEM((9, 2, 2, 16, half), BF),
            dma((2,)),
            dma((8,)),
            dma((8,)),
            dma,
            dma,
            dma,
            dma,
            dma((2, 3)),
            dma((2, 3)),
            dma((2, 3)),
            dma((2, 3)),
            dma,
            dma,
            dma((2, LON)),
            dma,
        ],
        compiler_params=pltpu.CompilerParams(
            collective_id=0, has_side_effects=True, vmem_limit_bytes=56 * 1024 * 1024
        ),
        cost_estimate=pl.CostEstimate(
            flops=12 * T * T * 9 * C * C, bytes_accessed=6_000_000, transcendentals=2 * T * T * C
        ),
    )(field, first_weight, second_weight, cotangent, live_rows, polar_links)
    return pl.pallas_call(
        finish,
        out_shape=(tile, tile, share, share),
        in_specs=[vmem] * 3,
        out_specs=(vmem,) * 4,
        cost_estimate=pl.CostEstimate(flops=2 * SHARE * C, bytes_accessed=3_000_000, transcendentals=0),
    )(made, back, sums)


def solution(mesh):
    in_specs = (P("lat", "lon", None), P(), P(), P("lat", "lon", None), P("lon", "lat"), P())
    out_specs = (P("lat", "lon", None), P("lat", "lon", None), P("lat", None), P("lat", None))
    return jax.shard_map(local, mesh=mesh, in_specs=in_specs, out_specs=out_specs, check_vma=False)
```

time: 85.8 us -> 63.7 us (0.74)
  Pallas kernels: 80.3 us -> 62.2 us
  local copies, waits for them, and re-layouts: 4.07 us -> 0 us
    pallas_call x1 -> x2, Pallas kernels: 80.3 us -> 62.2 us  [the longest x1 59.9 us: local(): pl.pallas_call(kernel, out_shape=(tile, tile, jax.ShapeDtypeStruct((9, 2,...]
    unnamed x10 -> x0, local copies, waits for them, and re-layouts: 4.07 us -> none
where the time goes in v2:
time: 63.7 us; the launch traced here: 63.5 us
  Pallas kernels  62.2 us (98%)
  between operations  1.29 us (2%)
    pallas_call x1, Pallas kernels, local(): pl.pallas_call(kernel, out_shape=(tile, tile, jax.ShapeDtypeStruct((9, 2,...  59.9 us
    pallas_call x1, Pallas kernels, local(): pl.pallas_call(finish, out_shape=(tile, tile, share, share), in_specs=[vm...  2.32 us

profile of v2, /device:TPU:1, one launch (start us, length us, event | category | flops | bytes accessed | tf_op | source)
XLA Modules:
  0.0 63.5 jit_solution(9577664637146780116)
XLA Ops:
  1.3 59.9 %shard_map.93 = (bf16[32,32,256]{2,1,0:T(8,128)(2,1)}, bf16[32,32,256]{2,1,0:T(8,128)(2,1)}, bf16[9,2,2,16,128]{4,3,2,1,0:T(8,128)(2,1)}) custom-call(bf16[32,32,256]{2,1,0:T(8,128)(2,1)} %field.1, bf16[2304,256]{1,0:T(8,128)(2,1)} %w1_hbm.1, bf16[2304,256]{1,0:T(8,128)(2,1)} %w2_hbm.1, bf16[32,32,256]{2,1,0:T(8,128)(2,1)} %cot.1, ...), custom_call_target="tpu_custom_call" | custom-call | flops 7247757312 | bytes 6000000 | tf_op jit(solution)/shard_map/pallas_call | solution.py:705
  61.2 2.3 %shard_map.94 = (bf16[32,32,256]{2,1,0:T(8,128)(2,1)}, bf16[32,32,256]{2,1,0:T(8,128)(2,1)}, f32[144,256]{1,0:T(8,128)}, f32[144,256]{1,0:T(8,128)}) custom-call(bf16[32,32,256]{2,1,0:T(8,128)(2,1)} %get-tuple-element.7.made, bf16[32,32,256]{2,1,0:T(8,128)(2,1)} %get-tuple-element.8.back, bf16[9,2,2,16,128]{4,3,2,1,0:T(8,128)(2,1)} %get-tuple-element.9.sums), custom_call_target="tpu_custom_call" | custom-call | flops 73728 | bytes 3000000 | tf_op jit(solution)/shard_map/pallas_call | solution.py:762

commit v3 on v2

--- a/solution.py
+++ b/solution.py
@@ -38,21 +38,26 @@
     return pl.ds(pl.multiple_of(start * T, T), size)
 
 
-def finish(made, back, sums, out, fgrad, grad1, grad2):
-    out[...] = made[...]
-    fgrad[...] = back[...]
+def finish(made, back, sums, out, fgrad, grad1, grad2, share1, share2, sem):
+    copies = [pltpu.make_async_copy(made, out, sem.at[0]), pltpu.make_async_copy(back, fgrad, sem.at[1])]
+    for copy in copies:
+        copy.start()
     scale = 1.0 / math.sqrt(LON * T * LAT * T)
-    for g, ref in enumerate((grad2, grad1)):
+    for g, (ref, dst) in enumerate(((share2, grad2), (share1, grad1))):
         for k in range(9):
             for h in range(2):
                 ref[k * 16 : (k + 1) * 16, h * 128 : (h + 1) * 128] = sums[k, h, g].astype(F32) * scale
+        copies.append(pltpu.make_async_copy(ref, dst, sem.at[2 + g]))
+        copies[-1].start()
+    for copy in copies:
+        copy.wait()
 
 
 def kernel(
-    field,
+    field_hbm,
     w1_hbm,
     w2_hbm,
-    cot,
+    cot_hbm,
     live_ref,
     links,
     out,
@@ -68,7 +73,8 @@
     zg,
     zs,
     kz,
-    fix,
+    field,
+    cot,
     cols,
     corner,
     pre1,
@@ -132,10 +138,12 @@
     def quarter(d):
         return u // 4 * 4 + (u % 4 + d) % 4
 
-    w1_copy = pltpu.make_async_copy(w1_hbm, w1, w_sem.at[0])
-    w2_copy = pltpu.make_async_copy(w2_hbm, w2, w_sem.at[1])
-    w1_copy.start()
-    w2_copy.start()
+    fetched = [
+        pltpu.make_async_copy(src, dst, w_sem.at[n])
+        for n, (src, dst) in enumerate(((field_hbm, field), (cot_hbm, cot), (w1_hbm, w1), (w2_hbm, w2)))
+    ]
+    for copy in fetched:
+        copy.start()
 
     barrier = pltpu.get_barrier_semaphore()
 
@@ -171,6 +179,8 @@
         greet(u, (z + d) % PLANES * 2 + v % 2)
 
     lane_row = lax.broadcasted_iota(jnp.int32, (T, C), 0)
+    fetched[0].wait()
+    fetched[1].wait()
 
     @pl.loop(0, T)
     def _(i):
@@ -274,8 +284,28 @@
                 pieces.append(s[2 - b if back else b, start : start + size * T, :])
         return jnp.concatenate(pieces, axis=1)
 
-    w1_copy.wait()
+    def spread(s, left, right, e, line):
+        at = rows(e)
+        s[1, at, :] = line.astype(BF)
+        s[0, at, :] = jnp.where(lane_row == 0, left, pltpu.roll(line, 1, 0)).astype(BF)
+        s[2, at, :] = jnp.where(lane_row == T - 1, right, pltpu.roll(line, T - 1, 0)).astype(BF)
+
+    fetched[2].wait()
     pre1[2 * T : 32 * T, :] = dot(window(sx, False, 2, 30), w1[...])
+
+    @pl.loop(3, 33)
+    def _(e):
+        act, slp = gelu_parts(pre1[rows(e - 1), :])
+        mask = jnp.where(jnp.full((T, C), e - 2, jnp.int32) < live, 1.0, 0.0)
+        slope[rows(e - 1), :] = slp * mask
+        spread(sh, 0.0, 0.0, e, act * mask)
+
+    fetched[3].wait()
+
+    @pl.loop(0, 9)
+    def _(tap):
+        at = pl.ds(pl.multiple_of(tap * C, C), C)
+        wt2[at, :] = w2[at, :].T
 
     @pl.when(rim_tile)
     def _():
@@ -307,14 +337,16 @@
             to = (x + d) % 4
             remote(picked.at[to], arrived.at[x], pbs_sem, pbr_sem, {"lon": (u + 4 * d) % LON, "lat": v}).start()
 
-    w2_copy.wait()
+    back2[2 * T : 32 * T, :] = dot(window(sd, True, 2, 30), wt2[...])
+
+    @pl.loop(3, 33)
+    def _(e):
+        spread(sg, 0.0, 0.0, e, back2[rows(e - 1), :] * slope[rows(e - 1), :])
 
     @pl.loop(0, 9)
     def _(tap):
         at = pl.ds(pl.multiple_of(tap * C, C), C)
-        wt2[at, :] = w2[at, :].T
-
-    back2[2 * T : 32 * T, :] = dot(window(sd, True, 2, 30), wt2[...])
+        wt1[at, :] = w1[at, :].T
 
     to_west.wait_recv()
     to_east.wait_recv()
@@ -345,33 +377,28 @@
     for k, (s, zz) in enumerate(((sx, zx), (sd, zd))):
         for n in range(2):
             zz[n, 2 : 2 + T, :] = halo_ew[0, (2 * k + n) * T : (2 * k + n + 1) * T, :].astype(F32)
-            zz[4 + n, 2 : 2 + T, :] = halo_ew[1, (2 * k + n) * T : (2 * k + n + 1) * T, :].astype(F32)
-            zz[2 + n, 2 : 2 + T, :] = cols[k, 3 * n]
+            zz[6 + n, 2 : 2 + T, :] = halo_ew[1, (2 * k + n) * T : (2 * k + n + 1) * T, :].astype(F32)
+            zz[2 + n, 2 : 2 + T, :] = cols[k, n]
+            zz[4 + n, 2 : 2 + T, :] = cols[k, 2 + n]
         for dg in range(4):
             px = halo_dg[dg].astype(F32)
             for r in range(2):
                 for n in range(2):
                     e = dg // 2 * 34 + r
                     at = 4 * k + 2 * r + n
-                    zz[dg % 2 * 4 + n, e : e + 1, :] = px[at : at + 1]
+                    zz[dg % 2 * 6 + n, e : e + 1, :] = px[at : at + 1]
         for e in (0, 1, 34, 35):
             h, r = e // 34, e % 34
             line = halo_ns[h, (2 * k + r) * T : (2 * k + r + 1) * T, :].astype(F32)
-            s[1, e * T : (e + 1) * T, :] = line.astype(BF)
-            s[0, e * T : (e + 1) * T, :] = jnp.where(
-                lane_row == 0, zz[1, e : e + 1, :], pltpu.roll(line, 1, 0)
-            ).astype(BF)
-            s[2, e * T : (e + 1) * T, :] = jnp.where(
-                lane_row == T - 1, zz[4, e : e + 1, :], pltpu.roll(line, T - 1, 0)
-            ).astype(BF)
-            zz[2, e : e + 1, :] = line[0:1]
-            zz[3, e : e + 1, :] = line[T - 1 : T]
+            spread(s, zz[1, e : e + 1, :], zz[6, e : e + 1, :], e, line)
+            for n, col in enumerate((0, 1, T - 2, T - 1)):
+                zz[2 + n, e : e + 1, :] = line[col : col + 1]
 
     def insert(s, zz, e):
         at = pl.ds(pl.multiple_of(e * T, T), 16)
         s[0, at, :] = jnp.where(head == 0, zz[1, pl.ds(e, 1), :], s[0, at, :].astype(F32)).astype(BF)
         at = pl.ds(pl.multiple_of(e * T + 16, 16), 16)
-        s[2, at, :] = jnp.where(head == 15, zz[4, pl.ds(e, 1), :], s[2, at, :].astype(F32)).astype(BF)
+        s[2, at, :] = jnp.where(head == 15, zz[6, pl.ds(e, 1), :], s[2, at, :].astype(F32)).astype(BF)
 
     for e in (2, 3, 32, 33):
         insert(sd, zd, e)
@@ -381,9 +408,14 @@
         insert(sx, zx, e)
 
     for t in range(2):
-        kz[t, 2 : 2 + T, :] = halo_ew[t, 4 * T :, :].astype(F32)
-        kz[t, 1:2, :] = halo_dg[t].astype(F32)[8:9]
-        kz[t, 34:35, :] = halo_dg[2 + t].astype(F32)[8:9]
+        kz[3 * t, 2 : 2 + T, :] = halo_ew[t, 4 * T :, :].astype(F32)
+        kz[3 * t, 1:2, :] = halo_dg[t].astype(F32)[8:9]
+        kz[3 * t, 34:35, :] = halo_dg[2 + t].astype(F32)[8:9]
+        kz[1 + t, 2 : 2 + T, :] = keep_col
+    for h in range(2):
+        mask = halo_ns[h, 4 * T :, :].astype(F32)
+        kz[1, 1 + 33 * h : 2 + 33 * h, :] = mask[0:1]
+        kz[2, 1 + 33 * h : 2 + 33 * h, :] = mask[T - 1 : T]
 
     def transposed(s):
         @pl.loop(0, PX // 128)
@@ -418,29 +450,31 @@
             up, down = down, up
         return pltpu.roll(up, 1, 0) + mid + pltpu.roll(down, mid.shape[0] - 1, 0)
 
-    def strips(zz, w, back):
+    def strips(zz, w, back, ref):
         order = (2, 1, 0) if back else (0, 1, 2)
-        both = jnp.concatenate(
-            [jnp.concatenate([zz[3 * t + b] for b in order], axis=1) for t in range(2)], axis=0
+        lines = jnp.concatenate(
+            [jnp.concatenate([zz[first + b] for b in order], axis=1) for first in (0, 1, 4, 5)], axis=0
         ).astype(BF)
-        ring = combine(*(dot(both, w[a * 3 * C : (a + 1) * 3 * C, :]) for a in range(3)), back)
-        row = lax.broadcasted_iota(jnp.int32, (STRIP, C), 0)
-        for t in range(2):
-            b = 2 - 2 * t if back else 2 * t
-            line = zz[1 + 3 * t].astype(BF)
-            res = combine(*(dot(line, w[(3 * a + b) * C : (3 * a + b + 1) * C, :]) for a in range(3)), back)
-            fix[t] = jnp.where((row > 2) & (row < 33), res, 0.0)
-        return ring
-
-    def with_fix(line, e):
-        line = line + jnp.where(lane_row == 0, fix[0, pl.ds(e, 1), :], 0.0)
-        return line + jnp.where(lane_row == T - 1, fix[1, pl.ds(e, 1), :], 0.0)
-
-    def spread(s, zz, e, line):
-        at = rows(e)
-        s[1, at, :] = line.astype(BF)
-        s[0, at, :] = jnp.where(lane_row == 0, zz[0, pl.ds(e, 1), :], pltpu.roll(line, 1, 0)).astype(BF)
-        s[2, at, :] = jnp.where(lane_row == T - 1, zz[1, pl.ds(e, 1), :], pltpu.roll(line, T - 1, 0)).astype(BF)
+        res = combine(*(dot(lines, w[a * 3 * C : (a + 1) * 3 * C, :]) for a in range(3)), back)
+        for t in range(4):
+            ref[t] = res[t * STRIP : (t + 1) * STRIP]
+
+    def put_columns(s, zz):
+        @pl.loop(3, 33)
+        def _(e):
+            c = [zz[t, pl.ds(e, 1), :] for t in range(4)]
+            at = pl.ds(pl.multiple_of(e * T, T), 16)
+            s[1, at, :] = jnp.where(head == 0, c[1], s[1, at, :].astype(F32)).astype(BF)
+            line = jnp.where(head == 1, c[1], s[0, at, :].astype(F32))
+            s[0, at, :] = jnp.where(head == 0, c[0], line).astype(BF)
+            at = pl.ds(pl.multiple_of(e * T + 16, 16), 16)
+            s[1, at, :] = jnp.where(head == 15, c[2], s[1, at, :].astype(F32)).astype(BF)
+            line = jnp.where(head == 14, c[2], s[2, at, :].astype(F32))
+            s[2, at, :] = jnp.where(head == 15, c[3], line).astype(BF)
+
+    def of_row(res, t):
+        at = (0, 1, T, T + 1)[t]
+        return res[at : at + 1]
 
     def outer(s, back):
         return jnp.concatenate([window(s, back, 0, 2), window(s, back, 32, 2)], axis=0)
@@ -448,37 +482,32 @@
     res = dot(outer(sx, False), w1[...])
     pre1[0 : 2 * T, :] = res[: 2 * T]
     pre1[32 * T : 34 * T, :] = res[2 * T :]
-    ring = strips(zx, w1, False)
-    for t in range(2):
-        zh[t] = ring[t * STRIP : (t + 1) * STRIP]
+    strips(zx, w1, False, zh)
 
     @pl.when(rim_tile)
     def _():
         for n, e in enumerate((e_out, e_ring, e_edge)):
-            extend(n, sx, (zx.at[0], zx.at[1]), (zx.at[4], zx.at[5]), e)
+            extend(n, sx, (zx.at[0], zx.at[1]), (zx.at[6], zx.at[7]), e)
         pre = dot(straight(2), taps(w1, far)) + dot(straight(1), taps(w1, 1)) + dot(straight(0), taps(w1, 2 - far))
         pre1[rows(e_ring - 1), :] = pre[1 : 1 + T]
-        for t in range(2):
-            at = t * (T + 1)
-            zh[t, pl.ds(e_ring, 1), :] = pre[at : at + 1]
-
-    for t in range(2):
+        for t in range(4):
+            zh[t, pl.ds(e_ring, 1), :] = of_row(pre, t)
+
+    for t in range(4):
         act, slp = gelu_parts(zh[t])
         zh[t] = act * kz[t]
         zs[t] = slp * kz[t]
 
     def activate(e, mask):
-        act, slp = gelu_parts(with_fix(pre1[rows(e - 1), :], e))
+        act, slp = gelu_parts(pre1[rows(e - 1), :])
         slope[rows(e - 1), :] = slp * mask
-        spread(sh, zh, e, act * mask)
-
-    for s in range(2):
-        activate(1 + 33 * s, halo_ns[s, 4 * T :, :].astype(F32))
-
-    @pl.loop(2, 34)
-    def _(e):
-        activate(e, jnp.where(jnp.full((T, C), e - 2, jnp.int32) < live, 1.0, 0.0))
-
+        spread(sh, zh[0, e : e + 1, :], zh[3, e : e + 1, :], e, act * mask)
+
+    activate(1, halo_ns[0, 4 * T :, :].astype(F32))
+    activate(2, jnp.where(jnp.zeros((T, C), jnp.int32) < live, 1.0, 0.0))
+    activate(33, keep_last)
+    activate(34, halo_ns[1, 4 * T :, :].astype(F32))
+    put_columns(sh, zh)
     transposed(sh)
 
     sibling = {"lon": u + 1 - 2 * core, "lat": v}
@@ -519,47 +548,44 @@
     res = dot(outer(sd, True), wt2[...])
     back2[0 : 2 * T, :] = res[: 2 * T]
     back2[32 * T : 34 * T, :] = res[2 * T :]
-    ring = strips(zd, wt2, True)
-    for t in range(2):
-        zg[t] = ring[t * STRIP : (t + 1) * STRIP]
+    strips(zd, wt2, True, zg)
 
     @pl.when(rim_tile)
     def _():
         for n, e in enumerate((e_out, e_ring, e_edge, e_in)):
-            extend(n, sd, (zd.at[0], zd.at[1]), (zd.at[4], zd.at[5]), e)
+            extend(n, sd, (zd.at[0], zd.at[1]), (zd.at[6], zd.at[7]), e)
         w_far, w_mid = taps(wt2, far), taps(wt2, 1)
         ring = dot(turned(0), w_far) + dot(straight(2), w_far) + dot(turned(1), w_mid)
         rim = dot(turned(1), w_far) + dot(straight(3), w_far) + dot(straight(2), w_mid)
         for e, res in ((e_ring, ring), (e_edge, rim)):
             back2[rows(e - 1), :] = res[1 : 1 + T]
-            for t in range(2):
-                at = t * (T + 1)
-                zg[t, pl.ds(e, 1), :] = res[at : at + 1]
-
-    for t in range(2):
+            for t in range(4):
+                zg[t, pl.ds(e, 1), :] = of_row(res, t)
+
+    for t in range(4):
         zg[t] = zg[t] * zs[t]
     scatter(0, 2)
-
-    @pl.loop(1, 35)
-    def _(e):
-        spread(sg, zg, e, with_fix(back2[rows(e - 1), :], e) * slope[rows(e - 1), :])
-
+    for e in (1, 2, 33, 34):
+        line = back2[rows(e - 1), :] * slope[rows(e - 1), :]
+        spread(sg, zg[0, e : e + 1, :], zg[3, e : e + 1, :], e, line)
+    put_columns(sg, zg)
     dz[3 * T : 35 * T, :] = sg[1, 2 * T : 34 * T, :]
     transposed(sx)
     weight_grad(1)
 
+    size = T // 2
+
+    def forward(first):
+        row = lax.broadcasted_iota(jnp.int32, (size * T, C), 0) // T + first
+        pre = dot(window(sh, False, 1 + first, size), w2[...])
+        masked = sx[1, (2 + first) * T : (2 + first + size) * T, :].astype(F32)
+        out[first : first + size] = (masked + jnp.where(row < live, pre, 0.0)).astype(BF).reshape(size, T, C)
+
+    forward(0)
+    scatter(1, 2)
+    forward(size)
+
     row = lax.broadcasted_iota(jnp.int32, (T * T, C), 0) // T
-    pre = dot(window(sh, False, 1, T), w2[...])
-    masked = sx[1, 2 * T : 34 * T, :].astype(F32)
-    out[...] = (masked + jnp.where(row < live, pre, 0.0)).astype(BF).reshape(T, T, C)
-
-    @pl.loop(0, 9)
-    def _(tap):
-        at = pl.ds(pl.multiple_of(tap * C, C), C)
-        wt1[at, :] = w1[at, :].T
-
-    scatter(1, 2)
-
     back = dot(window(sg, True, 1, T), wt1[...])
     total = cot[...].reshape(T * T, C).astype(F32) + back
     fgrad[...] = jnp.where(row < live, total, 0.0).astype(BF).reshape(T, T, C)
@@ -567,7 +593,7 @@
     @pl.when(rim_tile)
     def _():
         for n, e in ((1, e_ring), (2, e_edge), (3, e_in)):
-            extend(n, sg, (zg.at[0],), (zg.at[1],), e)
+            extend(n, sg, (zg.at[0],), (zg.at[3],), e)
         w_far, w_mid = taps(wt1, far), taps(wt1, 1)
         rim = dot(turned(1), w_far) + dot(straight(3), w_far) + dot(straight(2), w_mid)
         i = e_edge - 2
@@ -694,8 +720,8 @@
     tile = jax.ShapeDtypeStruct((T, T, C), BF)
     share = jax.ShapeDtypeStruct((SHARE, C), F32)
     flat = pltpu.VMEM((3, PX, C), BF)
-    columns = pltpu.VMEM((6, STRIP, C), F32)
-    two = pltpu.VMEM((2, STRIP, C), F32)
+    columns = pltpu.VMEM((8, STRIP, C), F32)
+    four = pltpu.VMEM((4, STRIP, C), F32)
     ringed = pltpu.VMEM((RING * T, C), F32)
     weights = pltpu.VMEM((9 * C, C), BF)
     message = pltpu.VMEM((2, MSG, C), BF)
@@ -704,13 +730,15 @@
     dma = pltpu.SemaphoreType.DMA
     made, back, sums = pl.pallas_call(
         kernel,
-        out_shape=(tile, tile, jax.ShapeDtypeStruct((9, 2, 2, 16, half), BF)),
-        in_specs=[vmem, anywhere, anywhere, vmem, smem, smem],
+        out_shape=(pltpu.VMEM((T, T, C), BF), pltpu.VMEM((T, T, C), BF), pltpu.VMEM((9, 2, 2, 16, half), BF)),
+        in_specs=[anywhere, anywhere, anywhere, anywhere, smem, smem],
         out_specs=(vmem, vmem, vmem),
         scratch_shapes=[
             *([flat] * 4),
             *([columns] * 2),
-            *([two] * 5),
+            *([four] * 4),
+            pltpu.VMEM((T, T, C), BF),
+            pltpu.VMEM((T, T, C), BF),
             pltpu.VMEM((2, 4, T, C), F32),
             pltpu.VMEM((4, 16, C), F32),
             *([ringed] * 3),
@@ -736,7 +764,7 @@
             pltpu.VMEM((PLANES, 2, 2, 16, half), BF),
             pltpu.VMEM((2, 2, 16, half), BF),
             pltpu.VMEM((9, 2, 2, 16, half), BF),
-            dma((2,)),
+            dma((4,)),
             dma((8,)),
             dma((8,)),
             dma,
@@ -763,7 +791,8 @@
         finish,
         out_shape=(tile, tile, share, share),
         in_specs=[vmem] * 3,
-        out_specs=(vmem,) * 4,
+        out_specs=(anywhere,) * 4,
+        scratch_shapes=[pltpu.VMEM((SHARE, C), F32), pltpu.VMEM((SHARE, C), F32), dma((4,))],
         cost_estimate=pl.CostEstimate(flops=2 * SHARE * C, bytes_accessed=3_000_000, transcendentals=0),
     )(made, back, sums)
 

time: 63.7 us -> 62.8 us (0.986)
  Pallas kernels: 62.2 us -> 59.1 us
  local copies, waits for them, and re-layouts: 0 us -> 2.23 us
    pallas_call x1, Pallas kernels: 59.9 us -> 56.8 us  [local(): pl.pallas_call(kernel, out_shape=(pltpu.VMEM((T, T, C), BF), pltpu.VMEM((...]
    unnamed x0 -> x6, local copies, waits for them, and re-layouts: none -> 2.23 us
where the time goes in v3:
time: 62.8 us; the launch traced here: 62.7 us
  Pallas kernels  59.1 us (94%)
  local copies, waits for them, and re-layouts  2.23 us (4%)
  between operations  1.3 us (2%)
    pallas_call x1, Pallas kernels, local(): pl.pallas_call(kernel, out_shape=(pltpu.VMEM((T, T, C), BF), pltpu.VMEM((...  56.8 us
    pallas_call x1, Pallas kernels, local(): pl.pallas_call(finish, out_shape=(tile, tile, share, share), in_specs=[vm...  2.31 us
    unnamed x6, local copies, waits for them, and re-layouts  2.23 us

profile of v3, /device:TPU:1, one launch (start us, length us, event | category | flops | bytes accessed | tf_op | source)
XLA Modules:
  0.0 62.7 jit_solution(3601817655161569436)
XLA Ops:
  1.3 56.8 %shard_map.93 = (bf16[32,32,256]{2,1,0:T(8,128)(2,1)S(1)}, bf16[32,32,256]{2,1,0:T(8,128)(2,1)S(1)}, bf16[9,2,2,16,128]{4,3,2,1,0:T(8,128)(2,1)S(1)}) custom-call(bf16[32,32,256]{2,1,0:T(8,128)(2,1)} %field_hbm.1, bf16[2304,256]{1,0:T(8,128)(2,1)} %w1_hbm.1, bf16[2304,256]{1,0:T(8,128)(2,1)} %w2_hbm.1, bf16[32,32,256]{2,1,0:T(8,128)(2,1)} %cot_hbm.1, ...), custom_call_target="tpu_custom_call" | custom-call | flops 7247757312 | bytes 6000000 | tf_op jit(solution)/shard_map/pallas_call | solution.py:731
  58.1 0.0 copy-start
  58.1 0.8 %copy-done = bf16[32,32,256]{2,1,0:T(8,128)(2,1)} copy-done((bf16[32,32,256]{2,1,0:T(8,128)(2,1)}, bf16[32,32,256]{2,1,0:T(8,128)(2,1)S(1)}, u32[]{:S(2)}) %copy-start) | copy-done | bytes 524312
  58.9 0.0 copy-start.1
  58.9 0.8 %copy-done.1 = bf16[32,32,256]{2,1,0:T(8,128)(2,1)} copy-done((bf16[32,32,256]{2,1,0:T(8,128)(2,1)}, bf16[32,32,256]{2,1,0:T(8,128)(2,1)S(1)}, u32[]{:S(2)}) %copy-start.1) | copy-done | bytes 524312
  59.7 0.0 copy-start.2
  59.7 0.7 %copy-done.2 = bf16[9,2,2,16,128]{4,3,2,1,0:T(8,128)(2,1)} copy-done((bf16[9,2,2,16,128]{4,3,2,1,0:T(8,128)(2,1)}, bf16[9,2,2,16,128]{4,3,2,1,0:T(8,128)(2,1)S(1)}, u32[]{:S(2)}) %copy-start.2) | copy-done | bytes 147480
  60.4 2.3 %shard_map.94 = (bf16[32,32,256]{2,1,0:T(8,128)(2,1)}, bf16[32,32,256]{2,1,0:T(8,128)(2,1)}, f32[144,256]{1,0:T(8,128)}, f32[144,256]{1,0:T(8,128)}) custom-call(bf16[32,32,256]{2,1,0:T(8,128)(2,1)} %copy-done, bf16[32,32,256]{2,1,0:T(8,128)(2,1)} %copy-done.1, bf16[9,2,2,16,128]{4,3,2,1,0:T(8,128)(2,1)} %copy-done.2), custom_call_target="tpu_custom_call" | custom-call | flops 73728 | bytes 3000000 | tf_op jit(solution)/shard_map/pallas_call | solution.py:790
Async XLA Ops:
  58.1 0.8 %copy-start = (bf16[32,32,256]{2,1,0:T(8,128)(2,1)}, bf16[32,32,256]{2,1,0:T(8,128)(2,1)S(1)}, u32[]{:S(2)}) copy-start(bf16[32,32,256]{2,1,0:T(8,128)(2,1)S(1)} %get-tuple-element.7.made) | copy-start | bytes 1572868
  58.9 0.8 %copy-start.1 = (bf16[32,32,256]{2,1,0:T(8,128)(2,1)}, bf16[32,32,256]{2,1,0:T(8,128)(2,1)S(1)}, u32[]{:S(2)}) copy-start(bf16[32,32,256]{2,1,0:T(8,128)(2,1)S(1)} %get-tuple-element.8.back) | copy-start | bytes 1572868
  59.7 0.7 %copy-start.2 = (bf16[9,2,2,16,128]{4,3,2,1,0:T(8,128)(2,1)}, bf16[9,2,2,16,128]{4,3,2,1,0:T(8,128)(2,1)S(1)}, u32[]{:S(2)}) copy-start(bf16[9,2,2,16,128]{4,3,2,1,0:T(8,128)(2,1)S(1)} %get-tuple-element.9.sums) | copy-start | bytes 442372

commit v4 on v3

--- a/solution.py
+++ b/solution.py
@@ -46,7 +46,7 @@
     for g, (ref, dst) in enumerate(((share2, grad2), (share1, grad1))):
         for k in range(9):
             for h in range(2):
-                ref[k * 16 : (k + 1) * 16, h * 128 : (h + 1) * 128] = sums[k, h, g].astype(F32) * scale
+                ref[k * 16 : (k + 1) * 16, h * 128 : (h + 1) * 128] = sums[h, k, g].astype(F32) * scale
         copies.append(pltpu.make_async_copy(ref, dst, sem.at[2 + g]))
         copies[-1].start()
     for copy in copies:
@@ -72,6 +72,8 @@
     zh,
     zg,
     zs,
+    zp,
+    zq,
     kz,
     field,
     cot,
@@ -81,7 +83,9 @@
     back2,
     slope,
     xt,
+    xth,
     dz,
+    dzg,
     w1,
     w2,
     wt1,
@@ -100,7 +104,12 @@
     gsend,
     gpair,
     gsum,
-    parts2,
+    px1,
+    py1,
+    sx1,
+    sy1,
+    py2,
+    px2,
     tiles,
     parts3,
     own,
@@ -120,23 +129,33 @@
     r3_sem,
     s4_sem,
     r4_sem,
+    s5_sem,
+    r5_sem,
 ):
     u, v = lax.axis_index("lon"), lax.axis_index("lat")
-    core, x, z = u % 2, u // 4, v // 2
-    y = (u // 2) % 2 * 2 + v % 2
+    core, x, z = lax.rem(u, 2), lax.div(u, 4), lax.div(v, 2)
+    low = lax.rem(u, 4)
+    y_lo = lax.rem(v, 2)
+    y = lax.div(low, 2) * 2 + y_lo
     spot = x * 4 + y
     north, south = v == 0, v == LAT - 1
     rim_tile = north | south
     side = jnp.where(south, 1, 0)
     live = live_ref[0, 0]
-    east, west = (u + 1) % LON, (u + LON - 1) % LON
+    east, west = lax.rem(u + 1, LON), lax.rem(u + LON - 1, LON)
 
     def in_plane(place):
-        px, py = place // 4, place % 4
-        return {"lon": px * 4 + py // 2 * 2 + core, "lat": z * 2 + py % 2}
+        px, py = lax.div(place, 4), lax.rem(place, 4)
+        return {"lon": px * 4 + lax.div(py, 2) * 2 + core, "lat": z * 2 + lax.rem(py, 2)}
+
+    def along_x(d):
+        return in_plane(lax.rem(x + d, 4) * 4 + y)
+
+    def along_y(d):
+        return in_plane(x * 4 + lax.rem(y + d, 4))
 
     def quarter(d):
-        return u // 4 * 4 + (u % 4 + d) % 4
+        return x * 4 + lax.rem(low + d, 4)
 
     fetched = [
         pltpu.make_async_copy(src, dst, w_sem.at[n])
@@ -167,16 +186,15 @@
     def _():
         for d in range(1, 4):
             greet(quarter(d), v)
-            greet((u + 4 * d) % LON, v)
-
-    @pl.loop(1, 16)
-    def _(d):
-        to = in_plane((spot + d) % 16)
-        greet(to["lon"], to["lat"])
+            greet(lax.rem(u + 4 * d, LON), v)
+
+    for d in range(1, 4):
+        for to in (along_x(d), along_y(d)):
+            greet(to["lon"], to["lat"])
 
     @pl.loop(1, PLANES)
     def _(d):
-        greet(u, (z + d) % PLANES * 2 + v % 2)
+        greet(u, lax.rem(z + d, PLANES) * 2 + y_lo)
 
     lane_row = lax.broadcasted_iota(jnp.int32, (T, C), 0)
     fetched[0].wait()
@@ -214,7 +232,7 @@
     send_dg[...] = corner[...].astype(BF)
 
     here = jnp.where(v > 0, 3, 0) + jnp.where(v < LAT - 1, 3, 0) + jnp.where(rim_tile, 6, 0)
-    pl.semaphore_wait(barrier, here + 2 + 15 + 7)
+    pl.semaphore_wait(barrier, here + 2 + 6 + 7)
 
     def remote(src, dst, send, recv, to):
         return pltpu.make_async_remote_copy(
@@ -230,7 +248,7 @@
     @pl.when(rim_tile)
     def _():
         for d in range(1, 4):
-            remote(send_ns.at[side], near.at[u % 4], pas_sem, par_sem, {"lon": quarter(d), "lat": v}).start()
+            remote(send_ns.at[side], near.at[low], pas_sem, par_sem, {"lon": quarter(d), "lat": v}).start()
 
     to_west = edge(send_ew.at[0], halo_ew.at[1], 0, west, v)
     to_east = edge(send_ew.at[1], halo_ew.at[0], 1, east, v)
@@ -266,13 +284,14 @@
             s[0, at, :] = jnp.where(lane_row == 0, 0.0, pltpu.roll(line, 1, 0)).astype(BF)
             s[2, at, :] = jnp.where(lane_row == T - 1, 0.0, pltpu.roll(line, T - 1, 0)).astype(BF)
 
-    for ref in (zx, zd, zh, zg, zs, ext, kz):
+    for ref in (zx, zd, zh, zg, zs, zp, zq, ext, kz):
         ref[...] = jnp.zeros_like(ref)
     for b in range(3):
         sh[b, 0:T, :] = jnp.zeros((T, C), BF)
         sh[b, PX - T : PX, :] = jnp.zeros((T, C), BF)
-    dz[0 : 3 * T, :] = jnp.zeros((3 * T, C), BF)
-    dz[35 * T : 38 * T, :] = jnp.zeros((3 * T, C), BF)
+    for ref in (dz, dzg):
+        ref[0 : 3 * T, :] = jnp.zeros((3 * T, C), BF)
+        ref[35 * T : 38 * T, :] = jnp.zeros((3 * T, C), BF)
     dz[3 * T : 35 * T, :] = sd[1, 2 * T : 34 * T, :]
     tiles[:, 9] = jnp.zeros((2, 16, C // 2), BF)
 
@@ -307,15 +326,17 @@
         at = pl.ds(pl.multiple_of(tap * C, C), C)
         wt2[at, :] = w2[at, :].T
 
+    back2[2 * T : 32 * T, :] = dot(window(sd, True, 2, 30), wt2[...])
+
     @pl.when(rim_tile)
     def _():
         drain(near.at[pl.ds(0, 3)], par_sem)
         drain(near.at[pl.ds(0, 3)], pas_sem)
-        near[u % 4] = send_ns[side]
+        near[low] = send_ns[side]
         pivot = links[side, 0]
         n = lax.broadcasted_iota(jnp.int32, (8 * T, 4 * T), 0)
         at = lax.broadcasted_iota(jnp.int32, (8 * T, 4 * T), 1) + x * (4 * T)
-        to = (n // (2 * T)) * 4 + u % 4
+        to = (n // (2 * T)) * 4 + low
         n = n & (2 * T - 1)
         q = n & 15
         in_east = n >= T + 16
@@ -334,10 +355,8 @@
             corners = corners + found[:, T:]
         picked[:, MSG:, :] = corners.astype(BF)
         for d in range(1, 4):
-            to = (x + d) % 4
-            remote(picked.at[to], arrived.at[x], pbs_sem, pbr_sem, {"lon": (u + 4 * d) % LON, "lat": v}).start()
-
-    back2[2 * T : 32 * T, :] = dot(window(sd, True, 2, 30), wt2[...])
+            to = lax.rem(x + d, 4)
+            remote(picked.at[to], arrived.at[x], pbs_sem, pbr_sem, {"lon": lax.rem(u + 4 * d, LON), "lat": v}).start()
 
     @pl.loop(3, 33)
     def _(e):
@@ -361,38 +380,39 @@
         for copy in to_north:
             copy.wait_recv()
 
-    @pl.when(rim_tile)
-    def _():
-        drain(arrived.at[pl.ds(0, 3)], pbr_sem)
-        drain(arrived.at[pl.ds(0, 3)], pbs_sem)
-        arrived[x] = picked[x]
-        total = arrived[0].astype(F32)
-        for k in range(1, 4):
-            total = total + arrived[k].astype(F32)
-        halo_ns[side] = total[:MSG].astype(BF)
-        halo_dg[2 * side] = total[MSG : MSG + 16].astype(BF)
-        halo_dg[2 * side + 1] = total[MSG + 16 :].astype(BF)
-
     head = lax.broadcasted_iota(jnp.int32, (16, C), 0)
-    for k, (s, zz) in enumerate(((sx, zx), (sd, zd))):
+
+    def place(h):
+        for k, (s, zz) in enumerate(((sx, zx), (sd, zd))):
+            for t in range(2):
+                px = halo_dg[2 * h + t].astype(F32)
+                for r in range(2):
+                    for n in range(2):
+                        at = 4 * k + 2 * r + n
+                        zz[t * 6 + n, pl.ds(34 * h + r, 1), :] = px[at : at + 1]
+            for r in range(2):
+                e = 34 * h + r
+                line = halo_ns[h, (2 * k + r) * T : (2 * k + r + 1) * T, :].astype(F32)
+                spread(s, zz[1, pl.ds(e, 1), :], zz[6, pl.ds(e, 1), :], e, line)
+                for n, col in enumerate((0, 1, T - 2, T - 1)):
+                    zz[2 + n, pl.ds(e, 1), :] = line[col : col + 1]
+        mask = halo_ns[h, 4 * T :, :].astype(F32)
+        e = 33 * h + 1
+        for t in range(2):
+            kz[3 * t, pl.ds(e, 1), :] = halo_dg[2 * h + t].astype(F32)[8:9]
+            kz[1 + t, pl.ds(e, 1), :] = mask[t * (T - 1) : t * (T - 1) + 1]
+
+    for k, zz in enumerate((zx, zd)):
         for n in range(2):
             zz[n, 2 : 2 + T, :] = halo_ew[0, (2 * k + n) * T : (2 * k + n + 1) * T, :].astype(F32)
             zz[6 + n, 2 : 2 + T, :] = halo_ew[1, (2 * k + n) * T : (2 * k + n + 1) * T, :].astype(F32)
             zz[2 + n, 2 : 2 + T, :] = cols[k, n]
             zz[4 + n, 2 : 2 + T, :] = cols[k, 2 + n]
-        for dg in range(4):
-            px = halo_dg[dg].astype(F32)
-            for r in range(2):
-                for n in range(2):
-                    e = dg // 2 * 34 + r
-                    at = 4 * k + 2 * r + n
-                    zz[dg % 2 * 6 + n, e : e + 1, :] = px[at : at + 1]
-        for e in (0, 1, 34, 35):
-            h, r = e // 34, e % 34
-            line = halo_ns[h, (2 * k + r) * T : (2 * k + r + 1) * T, :].astype(F32)
-            spread(s, zz[1, e : e + 1, :], zz[6, e : e + 1, :], e, line)
-            for n, col in enumerate((0, 1, T - 2, T - 1)):
-                zz[2 + n, e : e + 1, :] = line[col : col + 1]
+    for t in range(2):
+        kz[3 * t, 2 : 2 + T, :] = halo_ew[t, 4 * T :, :].astype(F32)
+        kz[1 + t, 2 : 2 + T, :] = keep_col
+    place(0)
+    place(1)
 
     def insert(s, zz, e):
         at = pl.ds(pl.multiple_of(e * T, T), 16)
@@ -407,22 +427,15 @@
     def _(e):
         insert(sx, zx, e)
 
-    for t in range(2):
-        kz[3 * t, 2 : 2 + T, :] = halo_ew[t, 4 * T :, :].astype(F32)
-        kz[3 * t, 1:2, :] = halo_dg[t].astype(F32)[8:9]
-        kz[3 * t, 34:35, :] = halo_dg[2 + t].astype(F32)[8:9]
-        kz[1 + t, 2 : 2 + T, :] = keep_col
-    for h in range(2):
-        mask = halo_ns[h, 4 * T :, :].astype(F32)
-        kz[1, 1 + 33 * h : 2 + 33 * h, :] = mask[0:1]
-        kz[2, 1 + 33 * h : 2 + 33 * h, :] = mask[T - 1 : T]
-
-    def transposed(s):
+    def transpose(s, ref, k):
+        at = pl.ds(pl.multiple_of(k * 128, 128), 128)
+        for b in range(3):
+            ref[b * C : (b + 1) * C, at] = s[b, at, :].T
+
+    def transposed(s, ref):
         @pl.loop(0, PX // 128)
         def _(k):
-            at = pl.ds(pl.multiple_of(k * 128, 128), 128)
-            for b in range(3):
-                xt[b * C : (b + 1) * C, at] = s[b, at, :].T
+            transpose(s, ref, k)
 
     e_out, e_ring = jnp.where(south, 35, 0), jnp.where(south, 34, 1)
     e_edge, e_in = jnp.where(south, 33, 2), jnp.where(south, 32, 3)
@@ -482,96 +495,151 @@
     res = dot(outer(sx, False), w1[...])
     pre1[0 : 2 * T, :] = res[: 2 * T]
     pre1[32 * T : 34 * T, :] = res[2 * T :]
-    strips(zx, w1, False, zh)
-
-    @pl.when(rim_tile)
-    def _():
-        for n, e in enumerate((e_out, e_ring, e_edge)):
-            extend(n, sx, (zx.at[0], zx.at[1]), (zx.at[6], zx.at[7]), e)
-        pre = dot(straight(2), taps(w1, far)) + dot(straight(1), taps(w1, 1)) + dot(straight(0), taps(w1, 2 - far))
-        pre1[rows(e_ring - 1), :] = pre[1 : 1 + T]
+    strips(zx, w1, False, zp)
+
+    def activate_strips():
         for t in range(4):
-            zh[t, pl.ds(e_ring, 1), :] = of_row(pre, t)
-
-    for t in range(4):
-        act, slp = gelu_parts(zh[t])
-        zh[t] = act * kz[t]
-        zs[t] = slp * kz[t]
+            act, slp = gelu_parts(zp[t])
+            zh[t] = act * kz[t]
+            zs[t] = slp * kz[t]
 
     def activate(e, mask):
         act, slp = gelu_parts(pre1[rows(e - 1), :])
         slope[rows(e - 1), :] = slp * mask
-        spread(sh, zh[0, e : e + 1, :], zh[3, e : e + 1, :], e, act * mask)
-
+        spread(sh, zh[0, pl.ds(e, 1), :], zh[3, pl.ds(e, 1), :], e, act * mask)
+
+    activate_strips()
     activate(1, halo_ns[0, 4 * T :, :].astype(F32))
     activate(2, jnp.where(jnp.zeros((T, C), jnp.int32) < live, 1.0, 0.0))
     activate(33, keep_last)
     activate(34, halo_ns[1, 4 * T :, :].astype(F32))
     put_columns(sh, zh)
-    transposed(sh)
+    transposed(sh, xth)
+
+    res = dot(outer(sd, True), wt2[...])
+    back2[0 : 2 * T, :] = res[: 2 * T]
+    back2[32 * T : 34 * T, :] = res[2 * T :]
+    strips(zd, wt2, True, zq)
+
+    def scale_strips():
+        for t in range(4):
+            zg[t] = zq[t] * zs[t]
+
+    def scale(e):
+        line = back2[rows(e - 1), :] * slope[rows(e - 1), :]
+        spread(sg, zg[0, pl.ds(e, 1), :], zg[3, pl.ds(e, 1), :], e, line)
+
+    scale_strips()
+    for e in (1, 2, 33, 34):
+        scale(e)
+    put_columns(sg, zg)
+    dzg[3 * T : 35 * T, :] = sg[1, 2 * T : 34 * T, :]
+    transposed(sx, xt)
+
+    @pl.when(rim_tile)
+    def _():
+        drain(arrived.at[pl.ds(0, 3)], pbr_sem)
+        drain(arrived.at[pl.ds(0, 3)], pbs_sem)
+        arrived[x] = picked[x]
+        total = arrived[0].astype(F32)
+        for k in range(1, 4):
+            total = total + arrived[k].astype(F32)
+        halo_ns[side] = total[:MSG].astype(BF)
+        halo_dg[2 * side] = total[MSG : MSG + 16].astype(BF)
+        halo_dg[2 * side + 1] = total[MSG + 16 :].astype(BF)
+        place(side)
+        for n, e in enumerate((e_out, e_ring, e_edge, e_in)):
+            extend(n, sx, (zx.at[0], zx.at[1]), (zx.at[6], zx.at[7]), e)
+        pre = jnp.zeros((2 * STRIP, C), F32)
+        for pair_of, row in (((straight(2), turned(1)), far), ((straight(1), turned(2)), 1), ((straight(0), turned(3)), 2 - far)):
+            pre = pre + dot(jnp.concatenate(pair_of, axis=0), taps(w1, row))
+        for k, e in enumerate((e_ring, e_edge)):
+            pre1[rows(e - 1), :] = pre[k * STRIP + 1 : k * STRIP + 1 + T]
+            for t in range(4):
+                zp[t, pl.ds(e, 1), :] = of_row(pre[k * STRIP : (k + 1) * STRIP], t)
+        activate_strips()
+        activate(e_ring, halo_ns[side, 4 * T :, :].astype(F32))
+        activate(e_edge, jnp.where(jnp.full((T, C), e_edge - 2, jnp.int32) < live, 1.0, 0.0))
+
+        for n, e in enumerate((e_out, e_ring, e_edge, e_in)):
+            extend(n, sd, (zd.at[0], zd.at[1]), (zd.at[6], zd.at[7]), e)
+        back = dot(jnp.concatenate([turned(0), turned(1)], axis=0), taps(wt2, far))
+        back = back + dot(jnp.concatenate([straight(2), straight(3)], axis=0), taps(wt2, far))
+        back = back + dot(jnp.concatenate([turned(1), straight(2)], axis=0), taps(wt2, 1))
+        for k, e in enumerate((e_ring, e_edge)):
+            back2[rows(e - 1), :] = back[k * STRIP + 1 : k * STRIP + 1 + T]
+            for t in range(4):
+                zq[t, pl.ds(e, 1), :] = of_row(back[k * STRIP : (k + 1) * STRIP], t)
+        scale_strips()
+        scale(e_ring)
+        scale(e_edge)
+        dzg[rows(e_edge + 1), :] = sg[1, rows(e_edge), :]
+        transpose(sx, xt, 8 * side)
+        transpose(sh, xth, 8 * side)
 
     sibling = {"lon": u + 1 - 2 * core, "lat": v}
 
     def pair(g, a):
         return remote(gsend.at[g, a], gpair.at[g, a], s1_sem.at[g, a], r1_sem.at[g, a], sibling)
 
-    def scatter(g, a):
+    def add_pair(g, a):
         pair(g, a).wait()
-        gsum[g, a] = (gkeep[g, a] + gpair[g, a].astype(F32)).astype(BF)
-
-        @pl.loop(1, 16)
-        def _(d):
-            to = (spot + d) % 16
-            remote(
-                gsum.at[g, a, :, pl.ds(pl.multiple_of(to * 16, 16), 16), :],
-                parts2.at[g, a, spot],
-                s2_sem.at[g, a],
-                r2_sem.at[g, a],
-                in_plane(to),
-            ).start()
-
-    def weight_grad(g):
-        @pl.loop(0, 3)
-        def _(a):
-            res = dot(xt[...], dz[rows(2 - a, PX), :])
+        total = gkeep[g, a] + gpair[g, a].astype(F32)
+        gsum[g, 3 * a : 3 * a + 3] = total.astype(BF).reshape(3, 4, 4, 16, C // 2)
+
+    def first_axis(g):
+        for d in range(1, 4):
+            to = lax.rem(x + d, 4)
+            remote(gsum.at[g, pl.ds(0, 5), to], px1.at[g, x], s2_sem.at[g, 0], r2_sem.at[g, 0], along_x(d)).start()
+            to = lax.rem(y + d, 4)
+            remote(gsum.at[g, pl.ds(5, 4), :, to], py1.at[g, y], s2_sem.at[g, 1], r2_sem.at[g, 1], along_y(d)).start()
+
+    def total_of(ref, g):
+        total = ref[g, 0].astype(F32)
+        for k in range(1, 4):
+            total = total + ref[g, k].astype(F32)
+        return total.astype(BF)
+
+    def second_axis(g):
+        drain(px1.at[g, pl.ds(0, 3)], r2_sem.at[g, 0])
+        px1[g, x] = gsum[g, 0:5, x]
+        sx1[g] = total_of(px1, g)
+        for d in range(1, 4):
+            to = lax.rem(y + d, 4)
+            remote(sx1.at[g, :, to], py2.at[g, y], s2_sem.at[g, 2], r2_sem.at[g, 2], along_y(d)).start()
+        drain(py1.at[g, pl.ds(0, 3)], r2_sem.at[g, 1])
+        py1[g, y] = gsum[g, 5:9, :, y]
+        sy1[g] = total_of(py1, g)
+        for d in range(1, 4):
+            to = lax.rem(x + d, 4)
+            remote(sy1.at[g, :, to], px2.at[g, x], s2_sem.at[g, 3], r2_sem.at[g, 3], along_x(d)).start()
+
+    def plane_total(g):
+        drain(py2.at[g, pl.ds(0, 3)], r2_sem.at[g, 2])
+        py2[g, y] = sx1[g, :, y]
+        tiles[g, 0:5] = total_of(py2, g)
+        drain(px2.at[g, pl.ds(0, 3)], r2_sem.at[g, 3])
+        px2[g, x] = sy1[g, :, x]
+        tiles[g, 5:9] = total_of(px2, g)
+
+    def weight_grad(g, left, right, between=None):
+        for a in range(3):
+            res = dot(left[...], right[(2 - a) * T : (2 - a) * T + PX, :])
             lo, hi = res[:, : C // 2], res[:, C // 2 :]
             gkeep[g, a] = jnp.where(core == 0, lo, hi).reshape(3, C, C // 2)
             gsend[g, a] = jnp.where(core == 0, hi, lo).astype(BF).reshape(3, C, C // 2)
             pair(g, a).start()
-
-            @pl.when(a > 0)
-            def _():
-                scatter(g, a - 1)
-
-    weight_grad(0)
-
-    res = dot(outer(sd, True), wt2[...])
-    back2[0 : 2 * T, :] = res[: 2 * T]
-    back2[32 * T : 34 * T, :] = res[2 * T :]
-    strips(zd, wt2, True, zg)
-
-    @pl.when(rim_tile)
-    def _():
-        for n, e in enumerate((e_out, e_ring, e_edge, e_in)):
-            extend(n, sd, (zd.at[0], zd.at[1]), (zd.at[6], zd.at[7]), e)
-        w_far, w_mid = taps(wt2, far), taps(wt2, 1)
-        ring = dot(turned(0), w_far) + dot(straight(2), w_far) + dot(turned(1), w_mid)
-        rim = dot(turned(1), w_far) + dot(straight(3), w_far) + dot(straight(2), w_mid)
-        for e, res in ((e_ring, ring), (e_edge, rim)):
-            back2[rows(e - 1), :] = res[1 : 1 + T]
-            for t in range(4):
-                zg[t, pl.ds(e, 1), :] = of_row(res, t)
-
-    for t in range(4):
-        zg[t] = zg[t] * zs[t]
-    scatter(0, 2)
-    for e in (1, 2, 33, 34):
-        line = back2[rows(e - 1), :] * slope[rows(e - 1), :]
-        spread(sg, zg[0, e : e + 1, :], zg[3, e : e + 1, :], e, line)
-    put_columns(sg, zg)
-    dz[3 * T : 35 * T, :] = sg[1, 2 * T : 34 * T, :]
-    transposed(sx)
-    weight_grad(1)
+            if a:
+                add_pair(g, a - 1)
+            elif between is not None:
+                between()
+
+    def first_done():
+        add_pair(0, 2)
+        first_axis(0)
+
+    weight_grad(0, xth, dz)
+    weight_grad(1, xt, dzg, first_done)
 
     size = T // 2
 
@@ -582,8 +650,10 @@
         out[first : first + size] = (masked + jnp.where(row < live, pre, 0.0)).astype(BF).reshape(size, T, C)
 
     forward(0)
-    scatter(1, 2)
+    add_pair(1, 2)
+    first_axis(1)
     forward(size)
+    second_axis(0)
 
     row = lax.broadcasted_iota(jnp.int32, (T * T, C), 0) // T
     back = dot(window(sg, True, 1, T), wt1[...])
@@ -601,27 +671,21 @@
         kept = jnp.full((T, C), i, jnp.int32) < live
         fgrad[i] = jnp.where(kept, total, 0.0).astype(BF)
 
-    for g in range(2):
-        for a in range(3):
-            drain(parts2.at[g, a, pl.ds(0, 15)], r2_sem.at[g, a])
-            parts2[g, a, spot] = gsum[g, a, :, pl.ds(pl.multiple_of(spot * 16, 16), 16), :]
-            total = parts2[g, a, 0].astype(F32)
-            for k in range(1, 16):
-                total = total + parts2[g, a, k].astype(F32)
-            tiles[g, 3 * a : 3 * a + 3] = total.astype(BF)
+    second_axis(1)
+    plane_total(0)
+    plane_total(1)
 
     def first_tile(plane):
-        return (18 * plane + 15 - spot) // 16
-
-    @pl.loop(1, PLANES)
-    def _(d):
-        to = (z + d) % PLANES
+        return lax.div(18 * plane + 15 - spot, 16)
+
+    for d in range(1, PLANES):
+        to = lax.rem(z + d, PLANES)
         remote(
             tiles.at[:, pl.ds(first_tile(to), 2)],
             parts3.at[z],
             s3_sem,
             r3_sem,
-            {"lon": u, "lat": to * 2 + v % 2},
+            {"lon": u, "lat": to * 2 + y_lo},
         ).start()
 
     mine = first_tile(z)
@@ -635,14 +699,14 @@
 
     def deliver(slot):
         group = (mine + slot) * 16 + spot
-        lat, at = group // 9, group % 9
-        src, dst = own.at[slot], final.at[at, core]
+        lat, at = lax.div(group, 9), lax.rem(group, 9)
+        src, dst = own.at[slot], final.at[core, at]
 
         def to(d):
-            return remote(src, dst, s4_sem.at[slot, d], r4_sem, {"lon": (u + d) % LON, "lat": lat})
-
-        @pl.loop(1, LON)
-        def _(d):
+            lon = 2 * lax.rem(lax.div(u, 2) + d, 8) + core
+            return remote(src, dst, s4_sem.at[2 * slot + (d == 0)], r4_sem, {"lon": lon, "lat": lat})
+
+        for d in range(1, 8):
             to(d).start()
 
         @pl.when(lat == v)
@@ -653,45 +717,39 @@
         def _():
             to(0).start()
 
-        def left():
-            @pl.loop(1, LON)
-            def _(d):
-                to(d).wait_send()
-
-            @pl.when(lat != v)
-            def _():
-                to(0).wait_send()
-
-        return left
-
-    has_two = first_tile(z + 1) - mine == 2
-    left0 = deliver(0)
-
-    @pl.when(has_two)
-    def _():
-        deliver(1)
-
-    drain(final, r4_sem)
-    sums[...] = final[...]
-
-    left0()
-
-    @pl.when(has_two)
-    def _():
-        group = (mine + 1) * 16 + spot
-        lat = group // 9
-        dst = final.at[group % 9, core]
-
-        def to(d):
-            return remote(own.at[1], dst, s4_sem.at[1, d], r4_sem, {"lon": (u + d) % LON, "lat": lat})
-
-        @pl.loop(1, LON)
-        def _(d):
-            to(d).wait_send()
+    def delivered(slot):
+        lat = lax.div((mine + slot) * 16 + spot, 9)
+        drain(final.at[0, pl.ds(0, 7)], s4_sem.at[2 * slot])
 
         @pl.when(lat != v)
         def _():
-            to(0).wait_send()
+            drain(final.at[0, 0], s4_sem.at[2 * slot + 1])
+
+    has_two = first_tile(z + 1) - mine == 2
+    deliver(0)
+
+    @pl.when(has_two)
+    def _():
+        deliver(1)
+
+    drain(final.at[core], r4_sem)
+    last = remote(final.at[core], final.at[core], s5_sem, r5_sem, sibling)
+    last.start()
+    for h in range(2):
+        @pl.when(core == h)
+        def _(h=h):
+            sums[h] = final[h]
+    delivered(0)
+
+    @pl.when(has_two)
+    def _():
+        delivered(1)
+
+    last.wait()
+    for h in range(2):
+        @pl.when(core != h)
+        def _(h=h):
+            sums[h] = final[h]
 
     to_west.wait_send()
     to_east.wait_send()
@@ -707,8 +765,8 @@
             copy.wait_send()
 
     for g in range(2):
-        for a in range(3):
-            drain(parts2.at[g, a, pl.ds(0, 15)], s2_sem.at[g, a])
+        for k, ref in enumerate((px1, py1, py2, px2)):
+            drain(ref.at[g, pl.ds(0, 3)], s2_sem.at[g, k])
     drain(parts3.at[pl.ds(0, PLANES - 1)], s3_sem)
 
 
@@ -730,20 +788,20 @@
     dma = pltpu.SemaphoreType.DMA
     made, back, sums = pl.pallas_call(
         kernel,
-        out_shape=(pltpu.VMEM((T, T, C), BF), pltpu.VMEM((T, T, C), BF), pltpu.VMEM((9, 2, 2, 16, half), BF)),
+        out_shape=(pltpu.VMEM((T, T, C), BF), pltpu.VMEM((T, T, C), BF), pltpu.VMEM((2, 9, 2, 16, half), BF)),
         in_specs=[anywhere, anywhere, anywhere, anywhere, smem, smem],
         out_specs=(vmem, vmem, vmem),
         scratch_shapes=[
             *([flat] * 4),
             *([columns] * 2),
-            *([four] * 4),
+            *([four] * 6),
             pltpu.VMEM((T, T, C), BF),
             pltpu.VMEM((T, T, C), BF),
             pltpu.VMEM((2, 4, T, C), F32),
             pltpu.VMEM((4, 16, C), F32),
             *([ringed] * 3),
-            pltpu.VMEM((3 * C, PX), BF),
-            pltpu.VMEM((38 * T, C), BF),
+            *([pltpu.VMEM((3 * C, PX), BF)] * 2),
+            *([pltpu.VMEM((38 * T, C), BF)] * 2),
             *([weights] * 4),
             pltpu.VMEM((4, 48, C), F32),
             message,
@@ -758,12 +816,17 @@
             pltpu.VMEM((2, 3, 3, C, half), F32),
             grads,
             grads,
-            grads,
-            pltpu.VMEM((2, 3, 16, 3, 16, half), BF),
+            pltpu.VMEM((2, 9, 4, 4, 16, half), BF),
+            pltpu.VMEM((2, 4, 5, 4, 16, half), BF),
+            pltpu.VMEM((2, 4, 4, 4, 16, half), BF),
+            pltpu.VMEM((2, 5, 4, 16, half), BF),
+            pltpu.VMEM((2, 4, 4, 16, half), BF),
+            pltpu.VMEM((2, 4, 5, 16, half), BF),
+            pltpu.VMEM((2, 4, 4, 16, half), BF),
             pltpu.VMEM((2, 10, 16, half), BF),
             pltpu.VMEM((PLANES, 2, 2, 16, half), BF),
             pltpu.VMEM((2, 2, 16, half), BF),
-            pltpu.VMEM((9, 2, 2, 16, half), BF),
+            pltpu.VMEM((2, 9, 2, 16, half), BF),
             dma((4,)),
             dma((8,)),
             dma((8,)),
@@ -773,11 +836,13 @@
             dma,
             dma((2, 3)),
             dma((2, 3)),
-            dma((2, 3)),
-            dma((2, 3)),
+            dma((2, 4)),
+            dma((2, 4)),
             dma,
             dma,
-            dma((2, LON)),
+            dma((4,)),
+            dma,
+            dma,
             dma,
         ],
         compiler_params=pltpu.CompilerParams(
@@ -787,12 +852,14 @@
             flops=12 * T * T * 9 * C * C, bytes_accessed=6_000_000, transcendentals=2 * T * T * C
         ),
     )(field, first_weight, second_weight, cotangent, live_rows, polar_links)
+    made, back, sums = (pltpu.with_memory_space_constraint(r, pltpu.VMEM) for r in (made, back, sums))
     return pl.pallas_call(
         finish,
         out_shape=(tile, tile, share, share),
         in_specs=[vmem] * 3,
         out_specs=(anywhere,) * 4,
         scratch_shapes=[pltpu.VMEM((SHARE, C), F32), pltpu.VMEM((SHARE, C), F32), dma((4,))],
+        compiler_params=pltpu.CompilerParams(vmem_limit_bytes=4 * 1024 * 1024),
         cost_estimate=pl.CostEstimate(flops=2 * SHARE * C, bytes_accessed=3_000_000, transcendentals=0),
     )(made, back, sums)
 

time: 62.8 us -> 57.2 us (0.911)
  Pallas kernels: 59.1 us -> 55.4 us
  local copies, waits for them, and re-layouts: 2.23 us -> 0 us
    pallas_call x1, Pallas kernels: 56.8 us -> 54.3 us  [local(): pl.pallas_call(kernel, out_shape=(pltpu.VMEM((T, T, C), BF), pltpu.VMEM((...]
    unnamed x6 -> x0, local copies, waits for them, and re-layouts: 2.23 us -> none
    pallas_call x1, Pallas kernels: 2.31 us -> 1.09 us  [local(): pl.pallas_call(finish, out_shape=(tile, tile, share, share), in_specs=[vm...]
where the time goes in v4:
time: 57.2 us; the launch traced here: 56.7 us
  Pallas kernels  55.4 us (97%)
  between operations  1.29 us (2%)
    pallas_call x1, Pallas kernels, local(): pl.pallas_call(kernel, out_shape=(pltpu.VMEM((T, T, C), BF), pltpu.VMEM((...  54.3 us

profile of v4, /device:TPU:1, one launch (start us, length us, event | category | flops | bytes accessed | tf_op | source)
XLA Modules:
  0.0 56.7 jit_solution(12919814151418065524)
XLA Ops:
  1.3 54.3 %shard_map.93 = (bf16[32,32,256]{2,1,0:T(8,128)(2,1)S(1)}, bf16[32,32,256]{2,1,0:T(8,128)(2,1)S(1)}, bf16[2,9,2,16,128]{4,3,2,1,0:T(8,128)(2,1)S(1)}) custom-call(bf16[32,32,256]{2,1,0:T(8,128)(2,1)} %field_hbm.1, bf16[2304,256]{1,0:T(8,128)(2,1)} %w1_hbm.1, bf16[2304,256]{1,0:T(8,128)(2,1)} %w2_hbm.1, bf16[32,32,256]{2,1,0:T(8,128)(2,1)} %cot_hbm.1, ...), custom_call_target="tpu_custom_call" | custom-call | flops 7247757312 | bytes 6000000 | tf_op jit(solution)/shard_map/pallas_call | solution.py:789
  55.6 1.1 %shard_map.94 = (bf16[32,32,256]{2,1,0:T(8,128)(2,1)}, bf16[32,32,256]{2,1,0:T(8,128)(2,1)}, f32[144,256]{1,0:T(8,128)}, f32[144,256]{1,0:T(8,128)}) custom-call(bf16[32,32,256]{2,1,0:T(8,128)(2,1)S(1)} %get-tuple-element.7.made, bf16[32,32,256]{2,1,0:T(8,128)(2,1)S(1)} %get-tuple-element.8.back, bf16[2,9,2,16,128]{4,3,2,1,0:T(8,128)(2,1)S(1)} %get-tuple-element.9.sums), custom_call_target="tpu_custom_call" | custom-call | flops 73728 | bytes 3000000 | tf_op jit(solution)/shard_map/pallas_call | solution.py:856

commit v5 on v4

--- a/solution.py
+++ b/solution.py
@@ -200,7 +200,7 @@
     fetched[0].wait()
     fetched[1].wait()
 
-    @pl.loop(0, T)
+    @pl.loop(0, T, unroll=4)
     def _(i):
         kept = jnp.full((T, C), i, jnp.int32) < live
         for k, (src, dst) in enumerate(((field, sx), (cot, sd))):
@@ -276,7 +276,7 @@
         for copy in to_south:
             copy.start()
 
-    @pl.loop(2, 34)
+    @pl.loop(2, 34, unroll=4)
     def _(e):
         at = rows(e)
         for s in (sx, sd):
@@ -310,23 +310,16 @@
         s[2, at, :] = jnp.where(lane_row == T - 1, right, pltpu.roll(line, T - 1, 0)).astype(BF)
 
     fetched[2].wait()
+    fetched[3].wait()
     pre1[2 * T : 32 * T, :] = dot(window(sx, False, 2, 30), w1[...])
-
-    @pl.loop(3, 33)
-    def _(e):
+    for tap in range(9):
+        wt2[tap * C : (tap + 1) * C, :] = w2[tap * C : (tap + 1) * C, :].T
+    back2[2 * T : 32 * T, :] = dot(window(sd, True, 2, 30), wt2[...])
+    for e in range(3, 33):
         act, slp = gelu_parts(pre1[rows(e - 1), :])
         mask = jnp.where(jnp.full((T, C), e - 2, jnp.int32) < live, 1.0, 0.0)
         slope[rows(e - 1), :] = slp * mask
         spread(sh, 0.0, 0.0, e, act * mask)
-
-    fetched[3].wait()
-
-    @pl.loop(0, 9)
-    def _(tap):
-        at = pl.ds(pl.multiple_of(tap * C, C), C)
-        wt2[at, :] = w2[at, :].T
-
-    back2[2 * T : 32 * T, :] = dot(window(sd, True, 2, 30), wt2[...])
 
     @pl.when(rim_tile)
     def _():
@@ -358,14 +351,9 @@
             to = lax.rem(x + d, 4)
             remote(picked.at[to], arrived.at[x], pbs_sem, pbr_sem, {"lon": lax.rem(u + 4 * d, LON), "lat": v}).start()
 
-    @pl.loop(3, 33)
+    @pl.loop(3, 33, unroll=3)
     def _(e):
         spread(sg, 0.0, 0.0, e, back2[rows(e - 1), :] * slope[rows(e - 1), :])
-
-    @pl.loop(0, 9)
-    def _(tap):
-        at = pl.ds(pl.multiple_of(tap * C, C), C)
-        wt1[at, :] = w1[at, :].T
 
     to_west.wait_recv()
     to_east.wait_recv()
@@ -423,7 +411,7 @@
     for e in (2, 3, 32, 33):
         insert(sd, zd, e)
 
-    @pl.loop(2, 34)
+    @pl.loop(2, 34, unroll=4)
     def _(e):
         insert(sx, zx, e)
 
@@ -433,8 +421,7 @@
             ref[b * C : (b + 1) * C, at] = s[b, at, :].T
 
     def transposed(s, ref):
-        @pl.loop(0, PX // 128)
-        def _(k):
+        for k in range(PX // 128):
             transpose(s, ref, k)
 
     e_out, e_ring = jnp.where(south, 35, 0), jnp.where(south, 34, 1)
@@ -473,7 +460,7 @@
             ref[t] = res[t * STRIP : (t + 1) * STRIP]
 
     def put_columns(s, zz):
-        @pl.loop(3, 33)
+        @pl.loop(3, 33, unroll=3)
         def _(e):
             c = [zz[t, pl.ds(e, 1), :] for t in range(4)]
             at = pl.ds(pl.multiple_of(e * T, T), 16)
@@ -492,6 +479,7 @@
     def outer(s, back):
         return jnp.concatenate([window(s, back, 0, 2), window(s, back, 32, 2)], axis=0)
 
+    transposed(sx, xt)
     res = dot(outer(sx, False), w1[...])
     pre1[0 : 2 * T, :] = res[: 2 * T]
     pre1[32 * T : 34 * T, :] = res[2 * T :]
@@ -534,7 +522,6 @@
         scale(e)
     put_columns(sg, zg)
     dzg[3 * T : 35 * T, :] = sg[1, 2 * T : 34 * T, :]
-    transposed(sx, xt)
 
     @pl.when(rim_tile)
     def _():
@@ -649,6 +636,8 @@
         masked = sx[1, (2 + first) * T : (2 + first + size) * T, :].astype(F32)
         out[first : first + size] = (masked + jnp.where(row < live, pre, 0.0)).astype(BF).reshape(size, T, C)
 
+    for tap in range(9):
+        wt1[tap * C : (tap + 1) * C, :] = w1[tap * C : (tap + 1) * C, :].T
     forward(0)
     add_pair(1, 2)
     first_axis(1)

time: 57.2 us -> 56.8 us (level)
  no operation moved by 1% of the time
where the time goes in v5:
time: 56.8 us; the launch traced here: 56.6 us
  Pallas kernels  55.3 us (97%)
  between operations  1.29 us (2%)
    pallas_call x1, Pallas kernels, local(): pl.pallas_call(kernel, out_shape=(pltpu.VMEM((T, T, C), BF), pltpu.VMEM((...  54.2 us

profile of v5, /device:TPU:1, one launch (start us, length us, event | category | flops | bytes accessed | tf_op | source)
XLA Modules:
  0.0 56.6 jit_solution(11008988857312831007)
XLA Ops:
  1.3 54.2 %shard_map.93 = (bf16[32,32,256]{2,1,0:T(8,128)(2,1)S(1)}, bf16[32,32,256]{2,1,0:T(8,128)(2,1)S(1)}, bf16[2,9,2,16,128]{4,3,2,1,0:T(8,128)(2,1)S(1)}) custom-call(bf16[32,32,256]{2,1,0:T(8,128)(2,1)} %field_hbm.1, bf16[2304,256]{1,0:T(8,128)(2,1)} %w1_hbm.1, bf16[2304,256]{1,0:T(8,128)(2,1)} %w2_hbm.1, bf16[32,32,256]{2,1,0:T(8,128)(2,1)} %cot_hbm.1, ...), custom_call_target="tpu_custom_call" | custom-call | flops 7247757312 | bytes 6000000 | tf_op jit(solution)/shard_map/pallas_call | solution.py:778
  55.5 1.1 %shard_map.94 = (bf16[32,32,256]{2,1,0:T(8,128)(2,1)}, bf16[32,32,256]{2,1,0:T(8,128)(2,1)}, f32[144,256]{1,0:T(8,128)}, f32[144,256]{1,0:T(8,128)}) custom-call(bf16[32,32,256]{2,1,0:T(8,128)(2,1)S(1)} %get-tuple-element.7.made, bf16[32,32,256]{2,1,0:T(8,128)(2,1)S(1)} %get-tuple-element.8.back, bf16[2,9,2,16,128]{4,3,2,1,0:T(8,128)(2,1)S(1)} %get-tuple-element.9.sums), custom_call_target="tpu_custom_call" | custom-call | flops 73728 | bytes 3000000 | tf_op jit(solution)/shard_map/pallas_call | solution.py:845

commit v6 on v5

--- a/solution.py
+++ b/solution.py
@@ -86,6 +86,7 @@
     xth,
     dz,
     dzg,
+    gm,
     w1,
     w2,
     wt1,
@@ -287,11 +288,20 @@
     for ref in (zx, zd, zh, zg, zs, zp, zq, ext, kz):
         ref[...] = jnp.zeros_like(ref)
     for b in range(3):
-        sh[b, 0:T, :] = jnp.zeros((T, C), BF)
-        sh[b, PX - T : PX, :] = jnp.zeros((T, C), BF)
+        for first, last in ((0, 3), (33, EXT)):
+            sh[b, first * T : last * T, :] = jnp.zeros(((last - first) * T, C), BF)
+        for first, last in ((0, 2), (34, EXT)):
+            sx[b, first * T : last * T, :] = jnp.zeros(((last - first) * T, C), BF)
     for ref in (dz, dzg):
-        ref[0 : 3 * T, :] = jnp.zeros((3 * T, C), BF)
-        ref[35 * T : 38 * T, :] = jnp.zeros((3 * T, C), BF)
+        ref[0 : 4 * T, :] = jnp.zeros((4 * T, C), BF)
+        ref[34 * T : 38 * T, :] = jnp.zeros((4 * T, C), BF)
+
+    @pl.when(rim_tile)
+    def _():
+        halo_ns[side] = jnp.zeros((MSG, C), BF)
+        for t in range(2):
+            halo_dg[2 * side + t] = jnp.zeros((16, C), BF)
+
     dz[3 * T : 35 * T, :] = sd[1, 2 * T : 34 * T, :]
     tiles[:, 9] = jnp.zeros((2, 16, C // 2), BF)
 
@@ -309,15 +319,23 @@
         s[0, at, :] = jnp.where(lane_row == 0, left, pltpu.roll(line, 1, 0)).astype(BF)
         s[2, at, :] = jnp.where(lane_row == T - 1, right, pltpu.roll(line, T - 1, 0)).astype(BF)
 
+    def transposed(s, ref):
+        for k in range(PX // 128):
+            for b in range(3):
+                ref[b * C : (b + 1) * C, k * 128 : (k + 1) * 128] = s[b, k * 128 : (k + 1) * 128, :].T
+
+    inner = (lane_row > 0) & (lane_row < T - 1)
+
     fetched[2].wait()
     fetched[3].wait()
     pre1[2 * T : 32 * T, :] = dot(window(sx, False, 2, 30), w1[...])
     for tap in range(9):
         wt2[tap * C : (tap + 1) * C, :] = w2[tap * C : (tap + 1) * C, :].T
+    transposed(sx, xt)
     back2[2 * T : 32 * T, :] = dot(window(sd, True, 2, 30), wt2[...])
     for e in range(3, 33):
         act, slp = gelu_parts(pre1[rows(e - 1), :])
-        mask = jnp.where(jnp.full((T, C), e - 2, jnp.int32) < live, 1.0, 0.0)
+        mask = jnp.where((jnp.full((T, C), e - 2, jnp.int32) < live) & inner, 1.0, 0.0)
         slope[rows(e - 1), :] = slp * mask
         spread(sh, 0.0, 0.0, e, act * mask)
 
@@ -355,6 +373,12 @@
     def _(e):
         spread(sg, 0.0, 0.0, e, back2[rows(e - 1), :] * slope[rows(e - 1), :])
 
+    dzg[4 * T : 34 * T, :] = sg[1, 3 * T : 33 * T, :]
+    transposed(sh, xth)
+    for g, left, right in ((1, xt, dzg), (0, xth, dz)):
+        for a in range(3):
+            gm[g, a] = dot(left[...], right[(2 - a) * T : (2 - a) * T + PX, :])
+
     to_west.wait_recv()
     to_east.wait_recv()
 
@@ -409,20 +433,8 @@
         s[2, at, :] = jnp.where(head == 15, zz[6, pl.ds(e, 1), :], s[2, at, :].astype(F32)).astype(BF)
 
     for e in (2, 3, 32, 33):
+        insert(sx, zx, e)
         insert(sd, zd, e)
-
-    @pl.loop(2, 34, unroll=4)
-    def _(e):
-        insert(sx, zx, e)
-
-    def transpose(s, ref, k):
-        at = pl.ds(pl.multiple_of(k * 128, 128), 128)
-        for b in range(3):
-            ref[b * C : (b + 1) * C, at] = s[b, at, :].T
-
-    def transposed(s, ref):
-        for k in range(PX // 128):
-            transpose(s, ref, k)
 
     e_out, e_ring = jnp.where(south, 35, 0), jnp.where(south, 34, 1)
     e_edge, e_in = jnp.where(south, 33, 2), jnp.where(south, 32, 3)
@@ -479,7 +491,6 @@
     def outer(s, back):
         return jnp.concatenate([window(s, back, 0, 2), window(s, back, 32, 2)], axis=0)
 
-    transposed(sx, xt)
     res = dot(outer(sx, False), w1[...])
     pre1[0 : 2 * T, :] = res[: 2 * T]
     pre1[32 * T : 34 * T, :] = res[2 * T :]
@@ -501,8 +512,6 @@
     activate(2, jnp.where(jnp.zeros((T, C), jnp.int32) < live, 1.0, 0.0))
     activate(33, keep_last)
     activate(34, halo_ns[1, 4 * T :, :].astype(F32))
-    put_columns(sh, zh)
-    transposed(sh, xth)
 
     res = dot(outer(sd, True), wt2[...])
     back2[0 : 2 * T, :] = res[: 2 * T]
@@ -520,8 +529,6 @@
     scale_strips()
     for e in (1, 2, 33, 34):
         scale(e)
-    put_columns(sg, zg)
-    dzg[3 * T : 35 * T, :] = sg[1, 2 * T : 34 * T, :]
 
     @pl.when(rim_tile)
     def _():
@@ -560,9 +567,6 @@
         scale_strips()
         scale(e_ring)
         scale(e_edge)
-        dzg[rows(e_edge + 1), :] = sg[1, rows(e_edge), :]
-        transpose(sx, xt, 8 * side)
-        transpose(sh, xth, 8 * side)
 
     sibling = {"lon": u + 1 - 2 * core, "lat": v}
 
@@ -609,24 +613,52 @@
         px2[g, x] = sy1[g, :, x]
         tiles[g, 5:9] = total_of(px2, g)
 
-    def weight_grad(g, left, right, between=None):
-        for a in range(3):
-            res = dot(left[...], right[(2 - a) * T : (2 - a) * T + PX, :])
+    def column(ref, t, first, mask):
+        return jnp.where(mask, ref[t, first : first + T, :], 0.0).astype(BF)
+
+    def left_side(pieces):
+        return jnp.concatenate([jnp.concatenate(p, axis=0).T for p in pieces], axis=0)
+
+    def finish_grad(g, left, rights):
+        for a, right in enumerate(rights):
+            res = gm[g, a] + dot(left, jnp.concatenate(right, axis=0))
             lo, hi = res[:, : C // 2], res[:, C // 2 :]
             gkeep[g, a] = jnp.where(core == 0, lo, hi).reshape(3, C, C // 2)
             gsend[g, a] = jnp.where(core == 0, hi, lo).astype(BF).reshape(3, C, C // 2)
             pair(g, a).start()
-            if a:
-                add_pair(g, a - 1)
-            elif between is not None:
-                between()
-
-    def first_done():
-        add_pair(0, 2)
-        first_axis(0)
-
-    weight_grad(0, xth, dz)
-    weight_grad(1, xt, dzg, first_done)
+
+    blank = jnp.zeros((T, C), BF)
+    places = ((0, 1, None, None), (1, None, None, 2), (None, None, 2, 3))
+    left = left_side(
+        [
+            [sh[b, T : 3 * T, :], sh[b, 33 * T : 35 * T, :]]
+            + [blank if t is None else column(zh, t, 2, inner) for t in places[b]]
+            for b in range(3)
+        ]
+    )
+    rights = [
+        [dz[(3 - a) * T : (5 - a) * T, :], dz[(35 - a) * T : (37 - a) * T, :]]
+        + [zd[2 + q, 3 - a : 35 - a, :].astype(BF) for q in range(4)]
+        for a in range(3)
+    ]
+    finish_grad(0, left, rights)
+    left = left_side(
+        [
+            [sx[b, T : 4 * T, :], sx[b, 32 * T : 35 * T, :]]
+            + [zx[t + b, 2 : 2 + T, :].astype(BF) for t in (1, 4)]
+            for b in range(3)
+        ]
+    )
+    rights = [
+        [sg[1, e * T : (e + 1) * T, :] if k == a else blank for e in (2, 33) for k in range(3)]
+        + [column(zg, t, 3 - a, (lane_row >= a) & (lane_row < T - 2 + a)) for t in (1, 2)]
+        for a in range(3)
+    ]
+    finish_grad(1, left, rights)
+    for g in range(2):
+        for a in range(3):
+            add_pair(g, a)
+        first_axis(g)
 
     size = T // 2
 
@@ -636,13 +668,13 @@
         masked = sx[1, (2 + first) * T : (2 + first + size) * T, :].astype(F32)
         out[first : first + size] = (masked + jnp.where(row < live, pre, 0.0)).astype(BF).reshape(size, T, C)
 
+    put_columns(sh, zh)
     for tap in range(9):
         wt1[tap * C : (tap + 1) * C, :] = w1[tap * C : (tap + 1) * C, :].T
     forward(0)
-    add_pair(1, 2)
-    first_axis(1)
     forward(size)
     second_axis(0)
+    put_columns(sg, zg)
 
     row = lax.broadcasted_iota(jnp.int32, (T * T, C), 0) // T
     back = dot(window(sg, True, 1, T), wt1[...])
@@ -791,6 +823,7 @@
             *([ringed] * 3),
             *([pltpu.VMEM((3 * C, PX), BF)] * 2),
             *([pltpu.VMEM((38 * T, C), BF)] * 2),
+            pltpu.VMEM((2, 3, 3 * C, C), F32),
             *([weights] * 4),
             pltpu.VMEM((4, 48, C), F32),
             message,

time: 56.8 us -> 53.6 us (0.944)
  Pallas kernels: 55.3 us -> 52.1 us
    pallas_call x1, Pallas kernels: 54.2 us -> 51 us  [local(): pl.pallas_call(kernel, out_shape=(pltpu.VMEM((T, T, C), BF), pltpu.VMEM((...]
where the time goes in v6:
time: 53.6 us; the launch traced here: 53.4 us
  Pallas kernels  52.1 us (97%)
  between operations  1.29 us (2%)
    pallas_call x1, Pallas kernels, local(): pl.pallas_call(kernel, out_shape=(pltpu.VMEM((T, T, C), BF), pltpu.VMEM((...  51 us
    pallas_call x1, Pallas kernels, local(): pl.pallas_call(finish, out_shape=(tile, tile, share, share), in_specs=[vm...  1.09 us

profile of v6, /device:TPU:1, one launch (start us, length us, event | category | flops | bytes accessed | tf_op | source)
XLA Modules:
  0.0 53.4 jit_solution(10475140646610202504)
XLA Ops:
  1.3 51.0 %shard_map.93 = (bf16[32,32,256]{2,1,0:T(8,128)(2,1)S(1)}, bf16[32,32,256]{2,1,0:T(8,128)(2,1)S(1)}, bf16[2,9,2,16,128]{4,3,2,1,0:T(8,128)(2,1)S(1)}) custom-call(bf16[32,32,256]{2,1,0:T(8,128)(2,1)} %field_hbm.1, bf16[2304,256]{1,0:T(8,128)(2,1)} %w1_hbm.1, bf16[2304,256]{1,0:T(8,128)(2,1)} %w2_hbm.1, bf16[32,32,256]{2,1,0:T(8,128)(2,1)} %cot_hbm.1, ...), custom_call_target="tpu_custom_call" | custom-call | flops 7247757312 | bytes 6000000 | tf_op jit(solution)/shard_map/pallas_call | solution.py:810
  52.3 1.1 %shard_map.94 = (bf16[32,32,256]{2,1,0:T(8,128)(2,1)}, bf16[32,32,256]{2,1,0:T(8,128)(2,1)}, f32[144,256]{1,0:T(8,128)}, f32[144,256]{1,0:T(8,128)}) custom-call(bf16[32,32,256]{2,1,0:T(8,128)(2,1)S(1)} %get-tuple-element.7.made, bf16[32,32,256]{2,1,0:T(8,128)(2,1)S(1)} %get-tuple-element.8.back, bf16[2,9,2,16,128]{4,3,2,1,0:T(8,128)(2,1)S(1)} %get-tuple-element.9.sums), custom_call_target="tpu_custom_call" | custom-call | flops 73728 | bytes 3000000 | tf_op jit(solution)/shard_map/pallas_call | solution.py:878

commit v7 on v6

--- a/solution.py
+++ b/solution.py
@@ -21,6 +21,7 @@
 LAT = 16
 PLANES = 8
 SHARE = 3 * T // 2 * 3
+XT = 3
 PICK = MSG + T
 
 
@@ -170,24 +171,24 @@
     def greet(lon, lat):
         pl.semaphore_signal(barrier, inc=1, device_id={"lon": lon, "lat": lat}, device_id_type=MESH)
 
-    greet(east, v)
-    greet(west, v)
-
-    @pl.when(v > 0)
-    def _():
-        for lon in (west, u, east):
-            greet(lon, v - 1)
-
-    @pl.when(v < LAT - 1)
-    def _():
-        for lon in (west, u, east):
-            greet(lon, v + 1)
-
     @pl.when(rim_tile)
     def _():
         for d in range(1, 4):
             greet(quarter(d), v)
             greet(lax.rem(u + 4 * d, LON), v)
+
+    greet(east, v)
+    greet(west, v)
+
+    @pl.when(v > 0)
+    def _():
+        for lon in (west, u, east):
+            greet(lon, v - 1)
+
+    @pl.when(v < LAT - 1)
+    def _():
+        for lon in (west, u, east):
+            greet(lon, v + 1)
 
     for d in range(1, 4):
         for to in (along_x(d), along_y(d)):
@@ -581,9 +582,9 @@
     def first_axis(g):
         for d in range(1, 4):
             to = lax.rem(x + d, 4)
-            remote(gsum.at[g, pl.ds(0, 5), to], px1.at[g, x], s2_sem.at[g, 0], r2_sem.at[g, 0], along_x(d)).start()
+            remote(gsum.at[g, pl.ds(0, XT), to], px1.at[g, x], s2_sem.at[g, 0], r2_sem.at[g, 0], along_x(d)).start()
             to = lax.rem(y + d, 4)
-            remote(gsum.at[g, pl.ds(5, 4), :, to], py1.at[g, y], s2_sem.at[g, 1], r2_sem.at[g, 1], along_y(d)).start()
+            remote(gsum.at[g, pl.ds(XT, 9 - XT), :, to], py1.at[g, y], s2_sem.at[g, 1], r2_sem.at[g, 1], along_y(d)).start()
 
     def total_of(ref, g):
         total = ref[g, 0].astype(F32)
@@ -593,13 +594,13 @@
 
     def second_axis(g):
         drain(px1.at[g, pl.ds(0, 3)], r2_sem.at[g, 0])
-        px1[g, x] = gsum[g, 0:5, x]
+        px1[g, x] = gsum[g, 0:XT, x]
         sx1[g] = total_of(px1, g)
         for d in range(1, 4):
             to = lax.rem(y + d, 4)
             remote(sx1.at[g, :, to], py2.at[g, y], s2_sem.at[g, 2], r2_sem.at[g, 2], along_y(d)).start()
         drain(py1.at[g, pl.ds(0, 3)], r2_sem.at[g, 1])
-        py1[g, y] = gsum[g, 5:9, :, y]
+        py1[g, y] = gsum[g, XT:9, :, y]
         sy1[g] = total_of(py1, g)
         for d in range(1, 4):
             to = lax.rem(x + d, 4)
@@ -608,10 +609,10 @@
     def plane_total(g):
         drain(py2.at[g, pl.ds(0, 3)], r2_sem.at[g, 2])
         py2[g, y] = sx1[g, :, y]
-        tiles[g, 0:5] = total_of(py2, g)
+        tiles[g, 0:XT] = total_of(py2, g)
         drain(px2.at[g, pl.ds(0, 3)], r2_sem.at[g, 3])
         px2[g, x] = sy1[g, :, x]
-        tiles[g, 5:9] = total_of(px2, g)
+        tiles[g, XT:9] = total_of(px2, g)
 
     def column(ref, t, first, mask):
         return jnp.where(mask, ref[t, first : first + T, :], 0.0).astype(BF)
@@ -673,7 +674,6 @@
         wt1[tap * C : (tap + 1) * C, :] = w1[tap * C : (tap + 1) * C, :].T
     forward(0)
     forward(size)
-    second_axis(0)
     put_columns(sg, zg)
 
     row = lax.broadcasted_iota(jnp.int32, (T * T, C), 0) // T
@@ -692,6 +692,7 @@
         kept = jnp.full((T, C), i, jnp.int32) < live
         fgrad[i] = jnp.where(kept, total, 0.0).astype(BF)
 
+    second_axis(0)
     second_axis(1)
     plane_total(0)
     plane_total(1)
@@ -839,12 +840,12 @@
             grads,
             grads,
             pltpu.VMEM((2, 9, 4, 4, 16, half), BF),
-            pltpu.VMEM((2, 4, 5, 4, 16, half), BF),
-            pltpu.VMEM((2, 4, 4, 4, 16, half), BF),
-            pltpu.VMEM((2, 5, 4, 16, half), BF),
-            pltpu.VMEM((2, 4, 4, 16, half), BF),
-            pltpu.VMEM((2, 4, 5, 16, half), BF),
-            pltpu.VMEM((2, 4, 4, 16, half), BF),
+            pltpu.VMEM((2, 4, XT, 4, 16, half), BF),
+            pltpu.VMEM((2, 4, 9 - XT, 4, 16, half), BF),
+            pltpu.VMEM((2, XT, 4, 16, half), BF),
+            pltpu.VMEM((2, 9 - XT, 4, 16, half), BF),
+            pltpu.VMEM((2, 4, XT, 16, half), BF),
+            pltpu.VMEM((2, 4, 9 - XT, 16, half), BF),
             pltpu.VMEM((2, 10, 16, half), BF),
             pltpu.VMEM((PLANES, 2, 2, 16, half), BF),
             pltpu.VMEM((2, 2, 16, half), BF),

time: 53.6 us -> 55.2 us (1.030)
  Pallas kernels: 52.1 us -> 53.2 us
    pallas_call x1, Pallas kernels: 51 us -> 52.1 us  [local(): pl.pallas_call(kernel, out_shape=(pltpu.VMEM((T, T, C), BF), pltpu.VMEM((...]
where the time goes in v7:
time: 55.2 us; the launch traced here: 54.4 us
  Pallas kernels  53.2 us (96%)
  between operations  1.29 us (2%)
    pallas_call x1, Pallas kernels, local(): pl.pallas_call(kernel, out_shape=(pltpu.VMEM((T, T, C), BF), pltpu.VMEM((...  52.1 us

profile of v7, /device:TPU:1, one launch (start us, length us, event | category | flops | bytes accessed | tf_op | source)
XLA Modules:
  0.0 54.4 jit_solution(11379244476960009176)
XLA Ops:
  1.3 52.1 %shard_map.93 = (bf16[32,32,256]{2,1,0:T(8,128)(2,1)S(1)}, bf16[32,32,256]{2,1,0:T(8,128)(2,1)S(1)}, bf16[2,9,2,16,128]{4,3,2,1,0:T(8,128)(2,1)S(1)}) custom-call(bf16[32,32,256]{2,1,0:T(8,128)(2,1)} %field_hbm.1, bf16[2304,256]{1,0:T(8,128)(2,1)} %w1_hbm.1, bf16[2304,256]{1,0:T(8,128)(2,1)} %w2_hbm.1, bf16[32,32,256]{2,1,0:T(8,128)(2,1)} %cot_hbm.1, ...), custom_call_target="tpu_custom_call" | custom-call | flops 7247757312 | bytes 6000000 | tf_op jit(solution)/shard_map/pallas_call | solution.py:811
  53.4 1.1 %shard_map.94 = (bf16[32,32,256]{2,1,0:T(8,128)(2,1)}, bf16[32,32,256]{2,1,0:T(8,128)(2,1)}, f32[144,256]{1,0:T(8,128)}, f32[144,256]{1,0:T(8,128)}) custom-call(bf16[32,32,256]{2,1,0:T(8,128)(2,1)S(1)} %get-tuple-element.7.made, bf16[32,32,256]{2,1,0:T(8,128)(2,1)S(1)} %get-tuple-element.8.back, bf16[2,9,2,16,128]{4,3,2,1,0:T(8,128)(2,1)S(1)} %get-tuple-element.9.sums), custom_call_target="tpu_custom_call" | custom-call | flops 73728 | bytes 3000000 | tf_op jit(solution)/shard_map/pallas_call | solution.py:879

commit v8 on v7

--- a/solution.py
+++ b/solution.py
@@ -21,8 +21,9 @@
 LAT = 16
 PLANES = 8
 SHARE = 3 * T // 2 * 3
-XT = 3
-PICK = MSG + T
+XT = (5, 4)
+NEAR = 4 * T + 16
+PICK = 5 * T
 
 
 def dot(a, b):
@@ -250,7 +251,7 @@
     @pl.when(rim_tile)
     def _():
         for d in range(1, 4):
-            remote(send_ns.at[side], near.at[low], pas_sem, par_sem, {"lon": quarter(d), "lat": v}).start()
+            remote(send_ns.at[side, pl.ds(0, NEAR)], near.at[low], pas_sem, par_sem, {"lon": quarter(d), "lat": v}).start()
 
     to_west = edge(send_ew.at[0], halo_ew.at[1], 0, west, v)
     to_east = edge(send_ew.at[1], halo_ew.at[0], 1, east, v)
@@ -344,7 +345,7 @@
     def _():
         drain(near.at[pl.ds(0, 3)], par_sem)
         drain(near.at[pl.ds(0, 3)], pas_sem)
-        near[low] = send_ns[side]
+        near[low] = send_ns[side, 0:NEAR, :]
         pivot = links[side, 0]
         n = lax.broadcasted_iota(jnp.int32, (8 * T, 4 * T), 0)
         at = lax.broadcasted_iota(jnp.int32, (8 * T, 4 * T), 1) + x * (4 * T)
@@ -352,20 +353,26 @@
         n = n & (2 * T - 1)
         q = n & 15
         in_east = n >= T + 16
-        ring_col = jnp.where(in_east, T, -1)
         outer_col = jnp.where(in_east, T, -2) + (q & 1)
-        col = jnp.where(n < T, n, jnp.where(q == 8, ring_col, outer_col))
+        col = jnp.where(n < T, n, outer_col)
         hit = ((pivot - to * T - col) & (LON * T - 1)) == at
-        line = jnp.where(q == 8, 4, jnp.where(q < 8, q // 2, 5))
+        line = jnp.where(q < 8, q // 2, 5)
         corners = jnp.zeros((4, T, C), F32)
-        for part in range(5):
-            target = part if part == 4 else part ^ 1
+        for part in range(4):
+            target = part ^ 1
             pick = jnp.where(hit & ((n < T) | (line == target)), 1.0, 0.0).astype(BF)
             lines = near[:, part * T : (part + 1) * T, :].reshape(4 * T, C)
             found = dot(pick, lines).reshape(4, 2 * T, C)
             picked[:, target * T : (target + 1) * T, :] = found[:, :T].astype(BF)
             corners = corners + found[:, T:]
-        picked[:, MSG:, :] = corners.astype(BF)
+        lane = lax.broadcasted_iota(jnp.int32, (T, C), 1)
+        lane_col = jnp.where(lane == T + 1, -1, lane)
+        for k in range(4):
+            tile = ((pivot - (4 * k + low) * T - lane_col) & (LON * T - 1)) // T
+            flags = jnp.zeros((T, C), F32)
+            for t in range(4):
+                flags = flags + jnp.where(tile == 4 * x + t, near[t, 4 * T : 4 * T + 1, :].astype(F32), 0.0)
+            picked[k, 4 * T :, :] = jnp.where(lane_row == 9, flags, corners[k]).astype(BF)
         for d in range(1, 4):
             to = lax.rem(x + d, 4)
             remote(picked.at[to], arrived.at[x], pbs_sem, pbr_sem, {"lon": lax.rem(u + 4 * d, LON), "lat": v}).start()
@@ -539,9 +546,18 @@
         total = arrived[0].astype(F32)
         for k in range(1, 4):
             total = total + arrived[k].astype(F32)
-        halo_ns[side] = total[:MSG].astype(BF)
-        halo_dg[2 * side] = total[MSG : MSG + 16].astype(BF)
-        halo_dg[2 * side + 1] = total[MSG + 16 :].astype(BF)
+        lane = lax.broadcasted_iota(jnp.int32, (T, C), 1)
+        flags = jnp.broadcast_to(total[4 * T + 9 : 4 * T + 10], (T, C))
+
+        def flag(hit):
+            return jnp.broadcast_to(jnp.sum(jnp.where(hit, flags, 0.0), axis=1, keepdims=True), (T, C))
+
+        halo_ns[side, 0 : 4 * T, :] = total[: 4 * T].astype(BF)
+        halo_ns[side, 4 * T :, :] = flag(lane == lane_row).astype(BF)
+        ends = jnp.where(lane_row < 16, flag(lane == T + 1), flag(lane == T))
+        ends = jnp.where((lane_row & 15) == 8, ends, total[4 * T :]).astype(BF)
+        halo_dg[2 * side] = ends[:16]
+        halo_dg[2 * side + 1] = ends[16:]
         place(side)
         for n, e in enumerate((e_out, e_ring, e_edge, e_in)):
             extend(n, sx, (zx.at[0], zx.at[1]), (zx.at[6], zx.at[7]), e)
@@ -580,39 +596,49 @@
         gsum[g, 3 * a : 3 * a + 3] = total.astype(BF).reshape(3, 4, 4, 16, C // 2)
 
     def first_axis(g):
+        n, m = XT[g], 9 - XT[g]
         for d in range(1, 4):
             to = lax.rem(x + d, 4)
-            remote(gsum.at[g, pl.ds(0, XT), to], px1.at[g, x], s2_sem.at[g, 0], r2_sem.at[g, 0], along_x(d)).start()
+            dst = px1.at[g, x, pl.ds(0, n)]
+            remote(gsum.at[g, pl.ds(0, n), to], dst, s2_sem.at[g, 0], r2_sem.at[g, 0], along_x(d)).start()
             to = lax.rem(y + d, 4)
-            remote(gsum.at[g, pl.ds(XT, 9 - XT), :, to], py1.at[g, y], s2_sem.at[g, 1], r2_sem.at[g, 1], along_y(d)).start()
-
-    def total_of(ref, g):
-        total = ref[g, 0].astype(F32)
+            dst = py1.at[g, y, pl.ds(0, m)]
+            remote(gsum.at[g, pl.ds(n, m), :, to], dst, s2_sem.at[g, 1], r2_sem.at[g, 1], along_y(d)).start()
+
+    def total_of(ref, g, n):
+        total = ref[g, 0, 0:n].astype(F32)
         for k in range(1, 4):
-            total = total + ref[g, k].astype(F32)
+            total = total + ref[g, k, 0:n].astype(F32)
         return total.astype(BF)
 
+    def three(ref, g, n):
+        return ref.at[g, pl.ds(0, 3), pl.ds(0, n)]
+
     def second_axis(g):
-        drain(px1.at[g, pl.ds(0, 3)], r2_sem.at[g, 0])
-        px1[g, x] = gsum[g, 0:XT, x]
-        sx1[g] = total_of(px1, g)
+        n, m = XT[g], 9 - XT[g]
+        drain(three(px1, g, n), r2_sem.at[g, 0])
+        px1[g, x, 0:n] = gsum[g, 0:n, x]
+        sx1[g, 0:n] = total_of(px1, g, n)
         for d in range(1, 4):
             to = lax.rem(y + d, 4)
-            remote(sx1.at[g, :, to], py2.at[g, y], s2_sem.at[g, 2], r2_sem.at[g, 2], along_y(d)).start()
-        drain(py1.at[g, pl.ds(0, 3)], r2_sem.at[g, 1])
-        py1[g, y] = gsum[g, XT:9, :, y]
-        sy1[g] = total_of(py1, g)
+            dst = py2.at[g, y, pl.ds(0, n)]
+            remote(sx1.at[g, pl.ds(0, n), to], dst, s2_sem.at[g, 2], r2_sem.at[g, 2], along_y(d)).start()
+        drain(three(py1, g, m), r2_sem.at[g, 1])
+        py1[g, y, 0:m] = gsum[g, n:9, :, y]
+        sy1[g, 0:m] = total_of(py1, g, m)
         for d in range(1, 4):
             to = lax.rem(x + d, 4)
-            remote(sy1.at[g, :, to], px2.at[g, x], s2_sem.at[g, 3], r2_sem.at[g, 3], along_x(d)).start()
+            dst = px2.at[g, x, pl.ds(0, m)]
+            remote(sy1.at[g, pl.ds(0, m), to], dst, s2_sem.at[g, 3], r2_sem.at[g, 3], along_x(d)).start()
 
     def plane_total(g):
-        drain(py2.at[g, pl.ds(0, 3)], r2_sem.at[g, 2])
-        py2[g, y] = sx1[g, :, y]
-        tiles[g, 0:XT] = total_of(py2, g)
-        drain(px2.at[g, pl.ds(0, 3)], r2_sem.at[g, 3])
-        px2[g, x] = sy1[g, :, x]
-        tiles[g, XT:9] = total_of(px2, g)
+        n, m = XT[g], 9 - XT[g]
+        drain(three(py2, g, n), r2_sem.at[g, 2])
+        py2[g, y, 0:n] = sx1[g, 0:n, y]
+        tiles[g, 0:n] = total_of(py2, g, n)
+        drain(three(px2, g, m), r2_sem.at[g, 3])
+        px2[g, x, 0:m] = sy1[g, 0:m, x]
+        tiles[g, n:9] = total_of(px2, g, m)
 
     def column(ref, t, first, mask):
         return jnp.where(mask, ref[t, first : first + T, :], 0.0).astype(BF)
@@ -674,6 +700,7 @@
         wt1[tap * C : (tap + 1) * C, :] = w1[tap * C : (tap + 1) * C, :].T
     forward(0)
     forward(size)
+    second_axis(0)
     put_columns(sg, zg)
 
     row = lax.broadcasted_iota(jnp.int32, (T * T, C), 0) // T
@@ -692,7 +719,6 @@
         kept = jnp.full((T, C), i, jnp.int32) < live
         fgrad[i] = jnp.where(kept, total, 0.0).astype(BF)
 
-    second_axis(0)
     second_axis(1)
     plane_total(0)
     plane_total(1)
@@ -787,8 +813,9 @@
             copy.wait_send()
 
     for g in range(2):
-        for k, ref in enumerate((px1, py1, py2, px2)):
-            drain(ref.at[g, pl.ds(0, 3)], s2_sem.at[g, k])
+        n, m = XT[g], 9 - XT[g]
+        for k, (ref, size) in enumerate(((px1, n), (py1, m), (py2, n), (px2, m))):
+            drain(three(ref, g, size), s2_sem.at[g, k])
     drain(parts3.at[pl.ds(0, PLANES - 1)], s3_sem)
 
 
@@ -833,19 +860,16 @@
             message,
             message,
             corners,
-            pltpu.VMEM((4, MSG, C), BF),
+            pltpu.VMEM((4, NEAR, C), BF),
             pltpu.VMEM((4, PICK, C), BF),
             pltpu.VMEM((4, PICK, C), BF),
             pltpu.VMEM((2, 3, 3, C, half), F32),
             grads,
             grads,
             pltpu.VMEM((2, 9, 4, 4, 16, half), BF),
-            pltpu.VMEM((2, 4, XT, 4, 16, half), BF),
-            pltpu.VMEM((2, 4, 9 - XT, 4, 16, half), BF),
-            pltpu.VMEM((2, XT, 4, 16, half), BF),
-            pltpu.VMEM((2, 9 - XT, 4, 16, half), BF),
-            pltpu.VMEM((2, 4, XT, 16, half), BF),
-            pltpu.VMEM((2, 4, 9 - XT, 16, half), BF),
+            *([pltpu.VMEM((2, 4, 5, 4, 16, half), BF)] * 2),
+            *([pltpu.VMEM((2, 5, 4, 16, half), BF)] * 2),
+            *([pltpu.VMEM((2, 4, 5, 16, half), BF)] * 2),
             pltpu.VMEM((2, 10, 16, half), BF),
             pltpu.VMEM((PLANES, 2, 2, 16, half), BF),
             pltpu.VMEM((2, 2, 16, half), BF),

time: 55.2 us -> 52.1 us (0.944); the launches traced: 54.4 us -> 51.9 us
  Pallas kernels: 53.2 us -> 50.6 us
    pallas_call x1, Pallas kernels: 52.1 us -> 49.5 us  [local(): pl.pallas_call(kernel, out_shape=(pltpu.VMEM((T, T, C), BF), pltpu.VMEM((...]
where the time goes in v8:
time: 52.1 us; the launch traced here: 51.9 us
  Pallas kernels  50.6 us (97%)
  between operations  1.29 us (2%)
    pallas_call x1, Pallas kernels, local(): pl.pallas_call(kernel, out_shape=(pltpu.VMEM((T, T, C), BF), pltpu.VMEM((...  49.5 us
    pallas_call x1, Pallas kernels, local(): pl.pallas_call(finish, out_shape=(tile, tile, share, share), in_specs=[vm...  1.09 us

profile of v8, /device:TPU:1, one launch (start us, length us, event | category | flops | bytes accessed | tf_op | source)
XLA Modules:
  0.0 51.9 jit_solution(17449156076696092570)
XLA Ops:
  1.3 49.5 %shard_map.93 = (bf16[32,32,256]{2,1,0:T(8,128)(2,1)S(1)}, bf16[32,32,256]{2,1,0:T(8,128)(2,1)S(1)}, bf16[2,9,2,16,128]{4,3,2,1,0:T(8,128)(2,1)S(1)}) custom-call(bf16[32,32,256]{2,1,0:T(8,128)(2,1)} %field_hbm.1, bf16[2304,256]{1,0:T(8,128)(2,1)} %w1_hbm.1, bf16[2304,256]{1,0:T(8,128)(2,1)} %w2_hbm.1, bf16[32,32,256]{2,1,0:T(8,128)(2,1)} %cot_hbm.1, ...), custom_call_target="tpu_custom_call" | custom-call | flops 7247757312 | bytes 6000000 | tf_op jit(solution)/shard_map/pallas_call | solution.py:838
  50.8 1.1 %shard_map.94 = (bf16[32,32,256]{2,1,0:T(8,128)(2,1)}, bf16[32,32,256]{2,1,0:T(8,128)(2,1)}, f32[144,256]{1,0:T(8,128)}, f32[144,256]{1,0:T(8,128)}) custom-call(bf16[32,32,256]{2,1,0:T(8,128)(2,1)S(1)} %get-tuple-element.7.made, bf16[32,32,256]{2,1,0:T(8,128)(2,1)S(1)} %get-tuple-element.8.back, bf16[2,9,2,16,128]{4,3,2,1,0:T(8,128)(2,1)S(1)} %get-tuple-element.9.sums), custom_call_target="tpu_custom_call" | custom-call | flops 73728 | bytes 3000000 | tf_op jit(solution)/shard_map/pallas_call | solution.py:903

commit v9 on v8

--- a/solution.py
+++ b/solution.py
@@ -344,7 +344,6 @@
     @pl.when(rim_tile)
     def _():
         drain(near.at[pl.ds(0, 3)], par_sem)
-        drain(near.at[pl.ds(0, 3)], pas_sem)
         near[low] = send_ns[side, 0:NEAR, :]
         pivot = links[side, 0]
         n = lax.broadcasted_iota(jnp.int32, (8 * T, 4 * T), 0)
@@ -371,7 +370,7 @@
             tile = ((pivot - (4 * k + low) * T - lane_col) & (LON * T - 1)) // T
             flags = jnp.zeros((T, C), F32)
             for t in range(4):
-                flags = flags + jnp.where(tile == 4 * x + t, near[t, 4 * T : 4 * T + 1, :].astype(F32), 0.0)
+                flags = flags + jnp.where(tile == 4 * x + t, near[t, 4 * T : 4 * T + 16, :].astype(F32)[0:1], 0.0)
             picked[k, 4 * T :, :] = jnp.where(lane_row == 9, flags, corners[k]).astype(BF)
         for d in range(1, 4):
             to = lax.rem(x + d, 4)
@@ -541,7 +540,6 @@
     @pl.when(rim_tile)
     def _():
         drain(arrived.at[pl.ds(0, 3)], pbr_sem)
-        drain(arrived.at[pl.ds(0, 3)], pbs_sem)
         arrived[x] = picked[x]
         total = arrived[0].astype(F32)
         for k in range(1, 4):
@@ -798,6 +796,11 @@
         @pl.when(core != h)
         def _(h=h):
             sums[h] = final[h]
+
+    @pl.when(rim_tile)
+    def _():
+        drain(near.at[pl.ds(0, 3)], pas_sem)
+        drain(arrived.at[pl.ds(0, 3)], pbs_sem)
 
     to_west.wait_send()
     to_east.wait_send()

time: 52.1 us -> 52 us (level)
  no operation moved by 1% of the time
where the time goes in v9:
time: 52 us; the launch traced here: 51.9 us
  Pallas kernels  50.6 us (97%)
  between operations  1.29 us (2%)
    pallas_call x1, Pallas kernels, local(): pl.pallas_call(kernel, out_shape=(pltpu.VMEM((T, T, C), BF), pltpu.VMEM((...  49.5 us
    pallas_call x1, Pallas kernels, local(): pl.pallas_call(finish, out_shape=(tile, tile, share, share), in_specs=[vm...  1.09 us

profile of v9, /device:TPU:1, one launch (start us, length us, event | category | flops | bytes accessed | tf_op | source)
XLA Modules:
  0.0 51.9 jit_solution(1669565441411839820)
XLA Ops:
  1.3 49.5 %shard_map.93 = (bf16[32,32,256]{2,1,0:T(8,128)(2,1)S(1)}, bf16[32,32,256]{2,1,0:T(8,128)(2,1)S(1)}, bf16[2,9,2,16,128]{4,3,2,1,0:T(8,128)(2,1)S(1)}) custom-call(bf16[32,32,256]{2,1,0:T(8,128)(2,1)} %field_hbm.1, bf16[2304,256]{1,0:T(8,128)(2,1)} %w1_hbm.1, bf16[2304,256]{1,0:T(8,128)(2,1)} %w2_hbm.1, bf16[32,32,256]{2,1,0:T(8,128)(2,1)} %cot_hbm.1, ...), custom_call_target="tpu_custom_call" | custom-call | flops 7247757312 | bytes 6000000 | tf_op jit(solution)/shard_map/pallas_call | solution.py:841
  50.8 1.1 %shard_map.94 = (bf16[32,32,256]{2,1,0:T(8,128)(2,1)}, bf16[32,32,256]{2,1,0:T(8,128)(2,1)}, f32[144,256]{1,0:T(8,128)}, f32[144,256]{1,0:T(8,128)}) custom-call(bf16[32,32,256]{2,1,0:T(8,128)(2,1)S(1)} %get-tuple-element.7.made, bf16[32,32,256]{2,1,0:T(8,128)(2,1)S(1)} %get-tuple-element.8.back, bf16[2,9,2,16,128]{4,3,2,1,0:T(8,128)(2,1)S(1)} %get-tuple-element.9.sums), custom_call_target="tpu_custom_call" | custom-call | flops 73728 | bytes 3000000 | tf_op jit(solution)/shard_map/pallas_call | solution.py:906
